TPU v7x, 32 devices: a whole 2x2x4 slice. The times are simulated.
32 devices in a mesh: rows: 4 (over y, x), seq: 8 (over z, core).
Axes of the slice: x: 2, y: 2, z: 4, core: 2. Of those that a mesh axis runs over, the one named last changes fastest.
Arguments:
- inputs: bfloat16 [4, 2048, 1024], P('rows', 'seq'), may hold values from -6 to 6
- memory: bfloat16 [4, 4704, 1024], P('rows', 'seq'), may hold values from -6 to 6
- out_grad: bfloat16 [4, 2048, 1024], P('rows', 'seq'), may hold values from -6 to 6
- segment_ids: int32 [4, 2048], P('rows'), may hold values from 0 to 7, never falling along the last dimension, each value on 1 to 1920 neighbouring positions
- page_order: int32 [4, 8], P('rows'), may hold values from 0 to 7, each once within a row
- norm1_gain: bfloat16 [1024], replicated, may hold values from 0.5 to 1.5
- norm1_bias: bfloat16 [1024], replicated, may hold values from -1 to 1
- qkv_weight: bfloat16 [1024, 3072], replicated, may hold values from -0.1875 to 0.1875
- qv_bias: bfloat16 [2048], replicated, may hold values from -1.5 to 1.5
- self_out_weight: bfloat16 [1024, 1024], replicated, may hold values from -0.75 to 0.75
- self_out_bias: bfloat16 [1024], replicated, may hold values from -1.5 to 1.5
- norm2_gain: bfloat16 [1024], replicated, may hold values from 0.5 to 1.5
- norm2_bias: bfloat16 [1024], replicated, may hold values from -1 to 1
- cross_q_weight: bfloat16 [1024, 1024], replicated, may hold values from -0.1875 to 0.1875
- cross_q_bias: bfloat16 [1024], replicated, may hold values from -1.5 to 1.5
- cross_kv_weight: bfloat16 [1024, 2048], replicated, may hold values from -0.1875 to 0.1875
- cross_v_bias: bfloat16 [1024], replicated, may hold values from -1.5 to 1.5
- cross_out_weight: bfloat16 [1024, 1024], replicated, may hold values from -0.75 to 0.75
- cross_out_bias: bfloat16 [1024], replicated, may hold values from -1.5 to 1.5
- norm3_gain: bfloat16 [1024], replicated, may hold values from 0.5 to 1.5
- norm3_bias: bfloat16 [1024], replicated, may hold values from -1 to 1
- fc1_weight: bfloat16 [1024, 4096], replicated, may hold values from -0.1875 to 0.1875
- fc1_bias: bfloat16 [4096], replicated, may hold values from -1.5 to 1.5
- fc2_weight: bfloat16 [4096, 1024], replicated, may hold values from -0.09375 to 0.09375
- fc2_bias: bfloat16 [1024], replicated, may hold values from -1.5 to 1.5
Outputs:
- layer_out: bfloat16 [4, 2048, 1024], P('rows', 'seq')
- input_grad: float32 [4, 2048, 1024], P('rows', 'seq')
- memory_grad: float32 [4, 4704, 1024], P('rows', 'seq')
- norm1_gain_grad: float32 [1024], P('seq')
- norm1_bias_grad: float32 [1024], P('seq')
- qkv_weight_grad: float32 [1024, 3072], P('seq')
- qv_bias_grad: float32 [2048], P('seq')
- self_out_weight_grad: float32 [1024, 1024], P('seq')
- self_out_bias_grad: float32 [1024], P('seq')
- norm2_gain_grad: float32 [1024], P('seq')
- norm2_bias_grad: float32 [1024], P('seq')
- cross_q_weight_grad: float32 [1024, 1024], P('seq')
- cross_q_bias_grad: float32 [1024], P('seq')
- cross_kv_weight_grad: float32 [1024, 2048], P('seq')
- cross_v_bias_grad: float32 [1024], P('seq')
- cross_out_weight_grad: float32 [1024, 1024], P('seq')
- cross_out_bias_grad: float32 [1024], P('seq')
- norm3_gain_grad: float32 [1024], P('seq')
- norm3_bias_grad: float32 [1024], P('seq')
- fc1_weight_grad: float32 [1024, 4096], P('seq')
- fc1_bias_grad: float32 [4096], P('seq')
- fc2_weight_grad: float32 [4096, 1024], P('seq')
- fc2_bias_grad: float32 [1024], P('seq')
Inputs may be any that keep to these rules, and one draw needn't show every extreme that they name: `segment_ids`: along each row the segment ids never fall, every page number appears, and one page holds exactly 1920 tokens. `page_order`: each row is a permutation of the page numbers.
All inputs are finite; a program needn't handle non-finite values.
Results may differ from a plain program's by a relative error of at most 0.024.
Values may be sent and summed in bfloat16 or wider, within the bound.
A program may use at most 256 MiB of HBM per device.

v0:
```python
import jax
import jax.numpy as jnp
from jax import lax
from jax.sharding import PartitionSpec as P

HEADS = 16
PAGES = 8
PAGE_TOK = 588


NEGATIVE = -1e30
SCALE = 0.125
EPSILON = 1e-05


def from_behind(block, axis, distance):
    devices = range(lax.axis_size(axis))
    route = [((i - distance) % len(devices), i) for i in devices]
    return lax.ppermute(block, axis, route)


def shifted(array, axis, by):
    size = lax.axis_size(axis)
    pairs = [(i, i + by) for i in range(size) if 0 <= i + by < size]
    return lax.ppermute(array, axis, pairs)


def norm_forward(values, gain, shift):
    center = values - jnp.mean(values, axis=-1, keepdims=True)
    spread = jnp.mean(center * center, axis=-1, keepdims=True)
    return center * lax.rsqrt(spread + EPSILON) * gain + shift


def gelu_exact(values):
    return jax.nn.gelu(values, approximate=False)


def norm_backward(values, gain, shift, grad_normed):
    _, pullback = jax.vjp(norm_forward, values, gain, shift)
    return pullback(grad_normed)


def dot_left(first, second):
    return lax.dot_general(
        first, second, (((0,), (0,)), ((), ())), preferred_element_type=jnp.float32
    )


def dot_right(first, second):
    return lax.dot_general(
        first, second, (((1,), (1,)), ((), ())), preferred_element_type=jnp.float32
    )


def split_heads(block_in, head_count):
    return block_in.reshape(block_in.shape[0], head_count, block_in.shape[1] // head_count)


def head_scores(query_heads, key_block, head_count):
    return (
        jnp.einsum(
            "thd,nhd->htn",
            query_heads,
            split_heads(key_block, head_count),
            preferred_element_type=jnp.float32,
        )
        * SCALE
    )


def stat_update(running, scores, allowed):
    row_top, row_total = running
    masked = jnp.where(allowed[None], scores, NEGATIVE)
    new_top = jnp.maximum(row_top, jnp.max(masked, axis=-1))
    kept_exp = jnp.where(allowed[None], jnp.exp(masked - new_top[..., None]), 0.0)
    return (new_top, row_total * jnp.exp(row_top - new_top) + jnp.sum(kept_exp, axis=-1))


def block_probs(scores, allowed, row_top, row_total):
    return (
        jnp.where(allowed[None], jnp.exp(scores - row_top[..., None]), 0.0) / row_total[..., None]
    )


def fold_keys(update, running, arrays):
    key_rows = arrays[0].shape[0]
    block_len = 512

    def scan_step(state_now, block_index):
        offset = block_index * block_len
        blocks = tuple(
            (lax.dynamic_slice_in_dim(array_in, offset, block_len, 0) for array_in in arrays)
        )
        return (update(state_now, blocks, offset), None)

    running, _ = lax.scan(scan_step, running, jnp.arange(key_rows // block_len, dtype=jnp.int32))
    return running


def grad_block(
    query_heads,
    grad_heads,
    key_block,
    value_block,
    allowed,
    row_top,
    row_total,
    delta_rows,
    head_count,
):
    key_heads = split_heads(key_block, head_count)
    scores = (
        jnp.einsum("thd,nhd->htn", query_heads, key_heads, preferred_element_type=jnp.float32)
        * SCALE
    )
    prob_block = block_probs(scores, allowed, row_top, row_total)
    grad_probs = jnp.einsum(
        "thd,nhd->htn",
        grad_heads,
        split_heads(value_block, head_count),
        preferred_element_type=jnp.float32,
    )
    grad_scores = (prob_block * (grad_probs - delta_rows[..., None])).astype(jnp.bfloat16)
    grad_query = jnp.einsum(
        "htn,nhd->thd", grad_scores, key_heads, preferred_element_type=jnp.float32
    )
    grad_key = jnp.einsum(
        "htn,thd->nhd", grad_scores, query_heads, preferred_element_type=jnp.float32
    )
    grad_value = jnp.einsum(
        "htn,thd->nhd",
        prob_block.astype(jnp.bfloat16),
        grad_heads,
        preferred_element_type=jnp.float32,
    )
    key_rows = key_block.shape[0]
    return (grad_query, grad_key.reshape(key_rows, -1), grad_value.reshape(key_rows, -1))


def body(
    inputs,
    memory,
    out_grad,
    segment_ids,
    page_order,
    norm1_gain,
    norm1_bias,
    qkv_weight,
    qv_bias,
    self_out_weight,
    self_out_bias,
    norm2_gain,
    norm2_bias,
    cross_q_weight,
    cross_q_bias,
    cross_kv_weight,
    cross_v_bias,
    cross_out_weight,
    cross_out_bias,
    norm3_gain,
    norm3_bias,
    fc1_weight,
    fc1_bias,
    fc2_weight,
    fc2_bias,
):
    head_count = HEADS
    tokens = inputs.shape[1]
    width = inputs.shape[2]
    head_depth = width // head_count
    seq_count = lax.axis_size("seq")
    my_start = lax.axis_index("seq") * tokens
    resid = inputs[0].astype(jnp.float32)
    row_segs = segment_ids[0]
    page_ids = page_order[0]
    query_segs = lax.dynamic_slice_in_dim(row_segs, my_start, tokens, 0)
    query_pos = my_start + jnp.arange(tokens, dtype=jnp.int32)
    gain_one = norm1_gain.astype(jnp.float32)
    shift_one = norm1_bias.astype(jnp.float32)
    gain_two = norm2_gain.astype(jnp.float32)
    shift_two = norm2_bias.astype(jnp.float32)
    gain_three = norm3_gain.astype(jnp.float32)
    shift_three = norm3_bias.astype(jnp.float32)
    qv_shift = qv_bias.astype(jnp.float32)

    def self_mask(key_start, key_rows):
        key_segs = lax.dynamic_slice_in_dim(row_segs, key_start, key_rows, 0)
        key_pos = key_start + jnp.arange(key_rows, dtype=jnp.int32)
        return (query_segs[:, None] == key_segs[None, :]) & (key_pos[None, :] <= query_pos[:, None])

    def page_mask(page_id):
        return jnp.broadcast_to((query_segs == page_id)[:, None], (tokens, PAGE_TOK))

    normed_one = norm_forward(resid, gain_one, shift_one).astype(jnp.bfloat16)
    qkv_out = jnp.dot(normed_one, qkv_weight, preferred_element_type=jnp.float32)
    queries = (qkv_out[:, :width] + qv_shift[:width]).astype(jnp.bfloat16)
    self_keys = qkv_out[:, width : 2 * width].astype(jnp.bfloat16)
    self_values = (qkv_out[:, 2 * width :] + qv_shift[width:]).astype(jnp.bfloat16)
    query_heads = queries.reshape(tokens, head_count, head_depth)
    start_stats = (
        jnp.full((head_count, tokens), NEGATIVE, jnp.float32),
        jnp.zeros((head_count, tokens), jnp.float32),
    )
    zero_heads = jnp.zeros((tokens, head_count, head_depth), jnp.float32)

    def stat_blocks(state_now, blocks, key_start):
        scores = head_scores(query_heads, blocks[0], head_count)
        return stat_update(state_now, scores, self_mask(key_start, blocks[0].shape[0]))

    row_top, row_total = fold_keys(
        stat_blocks, start_stats, (lax.all_gather(self_keys, "seq", axis=0, tiled=True),)
    )

    def value_blocks(summed_out, blocks, key_start):
        scores = head_scores(query_heads, blocks[0], head_count)
        prob_block = block_probs(
            scores, self_mask(key_start, blocks[0].shape[0]), row_top, row_total
        )
        return summed_out + jnp.einsum(
            "htn,nhd->thd",
            prob_block.astype(jnp.bfloat16),
            split_heads(blocks[1], head_count),
            preferred_element_type=jnp.float32,
        )

    attended = fold_keys(
        value_blocks,
        zero_heads,
        (
            lax.all_gather(self_keys, "seq", axis=0, tiled=True),
            lax.all_gather(self_values, "seq", axis=0, tiled=True),
        ),
    )
    attended_low = attended.reshape(tokens, width).astype(jnp.bfloat16)
    resid_one = (
        resid
        + jnp.dot(attended_low, self_out_weight, preferred_element_type=jnp.float32)
        + self_out_bias.astype(jnp.float32)
    )
    normed_two = norm_forward(resid_one, gain_two, shift_two).astype(jnp.bfloat16)
    cross_queries = (
        jnp.dot(normed_two, cross_q_weight, preferred_element_type=jnp.float32)
        + cross_q_bias.astype(jnp.float32)
    ).astype(jnp.bfloat16)
    value_shift = cross_v_bias.astype(jnp.float32)
    mem_rows = memory[0]
    projected = jnp.dot(
        lax.all_gather(mem_rows, "seq", axis=0, tiled=True),
        cross_kv_weight,
        preferred_element_type=jnp.float32,
    )
    joined = jnp.concatenate(
        (
            projected[:, :width].astype(jnp.bfloat16),
            (projected[:, width:] + value_shift).astype(jnp.bfloat16),
        ),
        axis=1,
    )
    mem_keys = joined[:, :width]
    mem_values = joined[:, width:]
    key_pages = mem_keys.reshape(PAGES, PAGE_TOK, width)
    value_pages = mem_values.reshape(PAGES, PAGE_TOK, width)
    cross_heads = cross_queries.reshape(tokens, head_count, head_depth)

    def cross_stat(state_now, page_items):
        key_block, page_id = page_items
        scores = head_scores(cross_heads, key_block, head_count)
        return (stat_update(state_now, scores, page_mask(page_id)), None)

    (cross_top, cross_total), _ = lax.scan(cross_stat, start_stats, (key_pages, page_ids))

    def cross_value(summed_out, page_items):
        key_block, value_block, page_id = page_items
        prob_block = block_probs(
            head_scores(cross_heads, key_block, head_count),
            page_mask(page_id),
            cross_top,
            cross_total,
        )
        return (
            summed_out
            + jnp.einsum(
                "htn,nhd->thd",
                prob_block.astype(jnp.bfloat16),
                split_heads(value_block, head_count),
                preferred_element_type=jnp.float32,
            ),
            None,
        )

    cross_out, _ = lax.scan(cross_value, zero_heads, (key_pages, value_pages, page_ids))
    cross_low = cross_out.reshape(tokens, width).astype(jnp.bfloat16)
    resid_two = (
        resid_one
        + jnp.dot(cross_low, cross_out_weight, preferred_element_type=jnp.float32)
        + cross_out_bias.astype(jnp.float32)
    )
    normed_three = norm_forward(resid_two, gain_three, shift_three).astype(jnp.bfloat16)
    pre_act = jnp.dot(
        normed_three, fc1_weight, preferred_element_type=jnp.float32
    ) + fc1_bias.astype(jnp.float32)
    hidden_act = gelu_exact(pre_act).astype(jnp.bfloat16)
    final_sum = (
        resid_two
        + jnp.dot(hidden_act, fc2_weight, preferred_element_type=jnp.float32)
        + fc2_bias.astype(jnp.float32)
    )
    layer_out = final_sum.astype(jnp.bfloat16)[None]
    grad_out = out_grad[0]
    grad_out_wide = grad_out.astype(jnp.float32)
    grad_act = dot_right(grad_out, fc2_weight)
    _, gelu_pull = jax.vjp(gelu_exact, pre_act)
    grad_pre = gelu_pull(grad_act)[0].astype(jnp.bfloat16)
    grad_fc2_w = dot_left(hidden_act, grad_out)
    grad_fc2_b = jnp.sum(grad_out_wide, axis=0)
    grad_fc1_w = dot_left(normed_three, grad_pre)
    grad_fc1_b = jnp.sum(grad_pre.astype(jnp.float32), axis=0)
    grad_normed_three = dot_right(grad_pre, fc1_weight)
    grad_two_norm, grad_gain_three, grad_shift_three = norm_backward(
        resid_two, gain_three, shift_three, grad_normed_three
    )
    grad_resid_two = grad_out_wide + grad_two_norm
    grad_branch_two = grad_resid_two.astype(jnp.bfloat16)
    grad_co_w = dot_left(cross_low, grad_branch_two)
    grad_co_b = jnp.sum(grad_branch_two.astype(jnp.float32), axis=0)
    grad_cross_low = dot_right(grad_branch_two, cross_out_weight).astype(jnp.bfloat16)
    grad_cross_heads = grad_cross_low.reshape(tokens, head_count, head_depth)
    delta_cross = jnp.einsum("thd,thd->ht", grad_cross_heads.astype(jnp.float32), cross_out)

    def cross_back(summed_query, page_items):
        key_block, value_block, page_id = page_items
        grad_q_part, grad_k_part, grad_v_part = grad_block(
            cross_heads,
            grad_cross_heads,
            key_block,
            value_block,
            page_mask(page_id),
            cross_top,
            cross_total,
            delta_cross,
            head_count,
        )
        return (summed_query + grad_q_part, (grad_k_part, grad_v_part))

    grad_cq_heads, (grad_mem_keys, grad_mem_values) = lax.scan(
        cross_back, zero_heads, (key_pages, value_pages, page_ids)
    )
    grad_cross_q = (grad_cq_heads.reshape(tokens, width) * SCALE).astype(jnp.bfloat16)
    shard_keys, shard_values = (
        lax.psum_scatter(
            (grad_mem_keys.reshape(-1, width) * SCALE).astype(jnp.bfloat16),
            "seq",
            scatter_dimension=0,
            tiled=True,
        ).astype(jnp.float32),
        lax.psum_scatter(
            grad_mem_values.reshape(-1, width).astype(jnp.bfloat16),
            "seq",
            scatter_dimension=0,
            tiled=True,
        ).astype(jnp.float32),
    )
    shard_keys = shard_keys.astype(jnp.bfloat16)
    shard_values = shard_values.astype(jnp.bfloat16)
    grad_ckv = jnp.concatenate((shard_keys, shard_values), axis=1)
    grad_ckv_w = dot_left(mem_rows, grad_ckv)
    grad_cv_b = jnp.sum(shard_values.astype(jnp.float32), axis=0)
    memory_grad = dot_right(grad_ckv, cross_kv_weight)[None]
    grad_cq_w = dot_left(normed_two, grad_cross_q)
    grad_cq_b = jnp.sum(grad_cross_q.astype(jnp.float32), axis=0)
    grad_normed_two = dot_right(grad_cross_q, cross_q_weight)
    grad_one_norm, grad_gain_two, grad_shift_two = norm_backward(
        resid_one, gain_two, shift_two, grad_normed_two
    )
    grad_resid_one = grad_resid_two + grad_one_norm
    grad_branch_one = grad_resid_one.astype(jnp.bfloat16)
    grad_o_w = dot_left(attended_low, grad_branch_one)
    grad_o_b = jnp.sum(grad_branch_one.astype(jnp.float32), axis=0)
    grad_attended = dot_right(grad_branch_one, self_out_weight).astype(jnp.bfloat16)
    grad_heads = grad_attended.reshape(tokens, head_count, head_depth)
    delta_self = jnp.einsum("thd,thd->ht", grad_heads.astype(jnp.float32), attended)

    def pass_grads(grad_keys, grad_values):
        return (
            from_behind(grad_keys.astype(jnp.bfloat16), "seq", 1).astype(grad_keys.dtype),
            from_behind(grad_values.astype(jnp.bfloat16), "seq", 1).astype(grad_values.dtype),
        )

    def accumulate(cycle_turn, cycle_state):
        held_keys, held_values, grad_keys, grad_values, grad_query = cycle_state
        owner_index = (lax.axis_index("seq") - cycle_turn) % seq_count
        grad_q_part, grad_k_part, grad_v_part = grad_block(
            query_heads,
            grad_heads,
            held_keys,
            held_values,
            self_mask(owner_index * tokens, tokens),
            row_top,
            row_total,
            delta_self,
            head_count,
        )
        return (
            held_keys,
            held_values,
            grad_keys + grad_k_part,
            grad_values + grad_v_part,
            grad_query + grad_q_part,
        )

    def cycle_step(cycle_turn, cycle_state):
        held_keys, held_values, grad_keys, grad_values, grad_query = accumulate(
            cycle_turn, cycle_state
        )
        held_keys, held_values = shifted((held_keys, held_values), "seq", 1)
        grad_keys, grad_values = pass_grads(grad_keys, grad_values)
        return (held_keys, held_values, grad_keys, grad_values, grad_query)

    zero_rows = jnp.zeros((tokens, width), jnp.float32)
    cycle_state = lax.fori_loop(
        0, seq_count - 1, cycle_step, (self_keys, self_values, zero_rows, zero_rows, zero_heads)
    )
    cycle_state = accumulate(seq_count - 1, cycle_state)
    home_keys, home_values = pass_grads(cycle_state[2], cycle_state[3])
    query_total = cycle_state[4]
    grad_queries = (query_total.reshape(tokens, width) * SCALE).astype(jnp.bfloat16)
    grad_keys_low = (home_keys * SCALE).astype(jnp.bfloat16)
    grad_values_low = home_values.astype(jnp.bfloat16)
    grad_qkv = jnp.concatenate((grad_queries, grad_keys_low, grad_values_low), axis=1)
    grad_qkv_w = dot_left(normed_one, grad_qkv)
    grad_qv_b = jnp.concatenate(
        (
            jnp.sum(grad_queries.astype(jnp.float32), axis=0),
            jnp.sum(grad_values_low.astype(jnp.float32), axis=0),
        )
    )
    grad_normed_one = dot_right(grad_qkv, qkv_weight)
    grad_in_norm, grad_gain_one, grad_shift_one = norm_backward(
        resid, gain_one, shift_one, grad_normed_one
    )
    input_grad = (grad_resid_one + grad_in_norm)[None]
    grad_terms = (
        grad_gain_one,
        grad_shift_one,
        grad_qkv_w,
        grad_qv_b,
        grad_o_w,
        grad_o_b,
        grad_gain_two,
        grad_shift_two,
        grad_cq_w,
        grad_cq_b,
        grad_ckv_w,
        grad_cv_b,
        grad_co_w,
        grad_co_b,
        grad_gain_three,
        grad_shift_three,
        grad_fc1_w,
        grad_fc1_b,
        grad_fc2_w,
        grad_fc2_b,
    )
    shares = (
        lax.psum_scatter(
            grad_terms[0].astype(jnp.bfloat16), "seq", scatter_dimension=0, tiled=True
        ).astype(jnp.float32),
        lax.psum_scatter(
            grad_terms[1].astype(jnp.bfloat16), "seq", scatter_dimension=0, tiled=True
        ).astype(jnp.float32),
        lax.psum_scatter(
            grad_terms[2].astype(jnp.bfloat16), "seq", scatter_dimension=0, tiled=True
        ).astype(jnp.float32),
        lax.psum_scatter(
            grad_terms[3].astype(jnp.bfloat16), "seq", scatter_dimension=0, tiled=True
        ).astype(jnp.float32),
        lax.psum_scatter(
            grad_terms[4].astype(jnp.bfloat16), "seq", scatter_dimension=0, tiled=True
        ).astype(jnp.float32),
        lax.psum_scatter(
            grad_terms[5].astype(jnp.bfloat16), "seq", scatter_dimension=0, tiled=True
        ).astype(jnp.float32),
        lax.psum_scatter(
            grad_terms[6].astype(jnp.bfloat16), "seq", scatter_dimension=0, tiled=True
        ).astype(jnp.float32),
        lax.psum_scatter(
            grad_terms[7].astype(jnp.bfloat16), "seq", scatter_dimension=0, tiled=True
        ).astype(jnp.float32),
        lax.psum_scatter(
            grad_terms[8].astype(jnp.bfloat16), "seq", scatter_dimension=0, tiled=True
        ).astype(jnp.float32),
        lax.psum_scatter(
            grad_terms[9].astype(jnp.bfloat16), "seq", scatter_dimension=0, tiled=True
        ).astype(jnp.float32),
        lax.psum_scatter(
            grad_terms[10].astype(jnp.bfloat16), "seq", scatter_dimension=0, tiled=True
        ).astype(jnp.float32),
        lax.psum_scatter(
            grad_terms[11].astype(jnp.bfloat16), "seq", scatter_dimension=0, tiled=True
        ).astype(jnp.float32),
        lax.psum_scatter(
            grad_terms[12].astype(jnp.bfloat16), "seq", scatter_dimension=0, tiled=True
        ).astype(jnp.float32),
        lax.psum_scatter(
            grad_terms[13].astype(jnp.bfloat16), "seq", scatter_dimension=0, tiled=True
        ).astype(jnp.float32),
        lax.psum_scatter(
            grad_terms[14].astype(jnp.bfloat16), "seq", scatter_dimension=0, tiled=True
        ).astype(jnp.float32),
        lax.psum_scatter(
            grad_terms[15].astype(jnp.bfloat16), "seq", scatter_dimension=0, tiled=True
        ).astype(jnp.float32),
        lax.psum_scatter(
            grad_terms[16].astype(jnp.bfloat16), "seq", scatter_dimension=0, tiled=True
        ).astype(jnp.float32),
        lax.psum_scatter(
            grad_terms[17].astype(jnp.bfloat16), "seq", scatter_dimension=0, tiled=True
        ).astype(jnp.float32),
        lax.psum_scatter(
            grad_terms[18].astype(jnp.bfloat16), "seq", scatter_dimension=0, tiled=True
        ).astype(jnp.float32),
        lax.psum_scatter(
            grad_terms[19].astype(jnp.bfloat16), "seq", scatter_dimension=0, tiled=True
        ).astype(jnp.float32),
    )
    summed = (
        lax.psum(shares[0].astype(jnp.bfloat16), "rows").astype(jnp.float32),
        lax.psum(shares[1].astype(jnp.bfloat16), "rows").astype(jnp.float32),
        lax.psum(shares[2].astype(jnp.bfloat16), "rows").astype(jnp.float32),
        lax.psum(shares[3].astype(jnp.bfloat16), "rows").astype(jnp.float32),
        lax.psum(shares[4].astype(jnp.bfloat16), "rows").astype(jnp.float32),
        lax.psum(shares[5].astype(jnp.bfloat16), "rows").astype(jnp.float32),
        lax.psum(shares[6].astype(jnp.bfloat16), "rows").astype(jnp.float32),
        lax.psum(shares[7].astype(jnp.bfloat16), "rows").astype(jnp.float32),
        lax.psum(shares[8].astype(jnp.bfloat16), "rows").astype(jnp.float32),
        lax.psum(shares[9].astype(jnp.bfloat16), "rows").astype(jnp.float32),
        lax.psum(shares[10].astype(jnp.bfloat16), "rows").astype(jnp.float32),
        lax.psum(shares[11].astype(jnp.bfloat16), "rows").astype(jnp.float32),
        lax.psum(shares[12].astype(jnp.bfloat16), "rows").astype(jnp.float32),
        lax.psum(shares[13].astype(jnp.bfloat16), "rows").astype(jnp.float32),
        lax.psum(shares[14].astype(jnp.bfloat16), "rows").astype(jnp.float32),
        lax.psum(shares[15].astype(jnp.bfloat16), "rows").astype(jnp.float32),
        lax.psum(shares[16].astype(jnp.bfloat16), "rows").astype(jnp.float32),
        lax.psum(shares[17].astype(jnp.bfloat16), "rows").astype(jnp.float32),
        lax.psum(shares[18].astype(jnp.bfloat16), "rows").astype(jnp.float32),
        lax.psum(shares[19].astype(jnp.bfloat16), "rows").astype(jnp.float32),
    )
    return (
        layer_out,
        input_grad,
        memory_grad,
        summed[0],
        summed[1],
        summed[2],
        summed[3],
        summed[4],
        summed[5],
        summed[6],
        summed[7],
        summed[8],
        summed[9],
        summed[10],
        summed[11],
        summed[12],
        summed[13],
        summed[14],
        summed[15],
        summed[16],
        summed[17],
        summed[18],
        summed[19],
    )


def solution(mesh):
    in_specs = (
        P("rows", "seq", None),
        P("rows", "seq", None),
        P("rows", "seq", None),
        P("rows", None),
        P("rows", None),
        P(),
        P(),
        P(),
        P(),
        P(),
        P(),
        P(),
        P(),
        P(),
        P(),
        P(),
        P(),
        P(),
        P(),
        P(),
        P(),
        P(),
        P(),
        P(),
        P(),
    )
    out_specs = (
        P("rows", "seq", None),
        P("rows", "seq", None),
        P("rows", "seq", None),
        P("seq"),
        P("seq"),
        P("seq", None),
        P("seq"),
        P("seq", None),
        P("seq"),
        P("seq"),
        P("seq"),
        P("seq", None),
        P("seq"),
        P("seq", None),
        P("seq"),
        P("seq", None),
        P("seq"),
        P("seq"),
        P("seq"),
        P("seq", None),
        P("seq"),
        P("seq", None),
        P("seq"),
    )
    return jax.shard_map(body, mesh=mesh, in_specs=in_specs, out_specs=out_specs, check_vma=False)
```

profile of v0, /device:TPU:0, one launch (start us, length us, event | category | flops | bytes accessed | tf_op | source)
XLA Modules:
  0.0 1868.8 jit_solution(2798184836429318269)
XLA Ops:
  31.4 37.4 %all-gather.7.cloned.1.call-done = bf16[2048,1024]{1,0:T(8,128)(2,1)} async-done(((bf16[256,1024]{1,0:T(8,128)(2,1)}), bf16[2048,1024]{1,0:T(8,128)(2,1)}) %all-gather.7.cloned.1.call-update) | async-done | bytes 4194320 | tf_op jit(solution)/shard_map/all_gather | solution.py:230
  75.3 52.7 %while.87 = (s32[]{:T(128)}, f32[16,256]{1,0:T(8,128)S(1)}, f32[16,256]{1,0:T(8,128)S(1)}, s32[256]{0:T(256)S(1)}, s32[4]{0:T(128)S(1)}, /*index=5*/s32[2048]{0:...) while((s32[]{:T(128)}, f32[16,256]{1,0:T(8,128)S(1)}, ...), condition=%wide.region_5.6_spmd.clone, body=%wide.region_2.5_spmd.clone.sunk | while | flops 285627136 | bytes 21066960 | solution.py:96
  128.1 52.3 %while.88 = (s32[]{:T(128)}, f32[256,16,64]{0,2,1:T(8,128)}, s32[4]{0:T(128)S(1)}, bf16[2048,1024]{1,0:T(8,128)(2,1)}, s32[256]{0:T(256)S(1)}, /*index=5*/s32[20...) while((s32[]{:T(128)}, f32[256,16,64]{0,2,1:T(8,128)}, ...), condition=%wide.region_7.8_spmd.clone, body=%wide.region_6.7_spmd.clone.sunk | while | flops 548274944 | bytes 15512861 | solution.py:96
  188.0 101.4 %all-gather.9.cloned.1.call-done = bf16[1,4704,1024]{2,0,1:T(2,128)(2,1)} async-done(((bf16[1,588,1024]{2,0,1:T(2,128)(2,1)}), bf16[1,4704,1024]{2,0,1:T(2,128)(2,1)}) %all-gather.9.cloned.1.call-update) | async-done | bytes 9633808 | tf_op jit(solution)/shard_map/all_gather | solution.py:248
  289.4 31.9 %fusion.44 = f32[4704,2048]{1,0:T(8,128)} fusion(bf16[1024,2048]{1,0:T(8,128)(2,1)} %param.52, bf16[1,4704,1024]{2,0,1:T(2,128)(2,1)} %all-gather.9.cloned.1.call-done), kind=kOutput, calls=%fused_computation.76 | convolution fusion | flops 19730006016 | bytes 52363264 | tf_op jit(solution)/shard_map/dot_general | solution.py:247
  321.3 11.7 slice.50
  333.0 8.4 reshape.543
  341.4 14.3 copy.117
  355.7 120.2 %while.89 = (s32[]{:T(128)}, f32[16,256]{1,0:T(8,128)S(1)}, f32[16,256]{1,0:T(8,128)S(1)}, s32[8]{0:T(128)S(1)}, s32[256]{0:T(256)S(1)}, /*index=5*/bf16[8,588,1...) while((s32[]{:T(128)}, f32[16,256]{1,0:T(8,128)S(1)}, ...), condition=%wide.region_13.14_spmd.clone, body=%wide.region_10.13_spmd.clone.sunk | while | flops 327569664 | bytes 23619452 | solution.py:270
  475.9 12.4 fusion.43
  488.3 8.3 reshape.542
  496.6 14.2 copy.116
  510.8 82.2 %while.90 = (s32[]{:T(128)}, f32[256,16,64]{0,2,1:T(8,128)}, bf16[8,588,1024]{1,2,0:T(8,128)(2,1)}, s32[8]{0:T(128)S(1)}, s32[256]{0:T(256)S(1)}, /*index=5*/bf1...) while((s32[]{:T(128)}, f32[256,16,64]{0,2,1:T(8,128)}, ...), condition=%wide.region_15.16_spmd.clone, body=%wide.region_14.15_spmd.clone.sunk | while | flops 629129472 | bytes 9881227 | solution.py:291
  597.5 15.4 multiply_convert_fusion.4
  613.0 12.0 fusion.117
  640.3 200.7 %while.91 = (s32[]{:T(128)}, f32[256,16,64]{0,2,1:T(8,128)}, f32[8,588,1024]{1,2,0:T(8,128)}, bf16[8,588,1024]{1,2,0:T(8,128)(2,1)}, bf16[8,588,1024]{1,2,0:T(8,...) while((s32[]{:T(128)}, f32[256,16,64]{0,2,1:T(8,128)}, ...), condition=%wide.region_21.22_spmd.clone, body=%wide.region_20.21_spmd.clone.sunk | while | flops 1561198848 | bytes 86559432 | solution.py:345
  841.0 12.6 multiply_convert_fusion.2
  853.6 14.7 copy.124
  868.3 8.3 convert_element_type.434
  876.6 14.7 copy.125
  891.3 8.3 convert_element_type.436
  899.6 190.6 %fusion.104 = (bf16[592,1024]{1,0:T(8,128)(2,1)S(1)}, bf16[592,1024]{1,0:T(8,128)(2,1)}) fusion(bf16[4704,1024]{1,0:T(8,128)(2,1)} %convert_element_type.436, bf16[4704,1024]{1,0:T(8,128)(2,1)} %convert_element_type.434), kind=kCustom, calls=%all-reduce-scatter.2 | all-reduce-scatter fusion | flops 9699329 | bytes 21692928
  1154.0 302.7 %while.92 = (s32[]{:T(128)}, bf16[256,1024]{0,1:T(8,128)(2,1)}, bf16[256,1024]{0,1:T(8,128)(2,1)}, f32[256,1024]{0,1:T(8,128)}, f32[256,1024]{0,1:T(8,128)}, /*i...) while((s32[]{:T(128)}, bf16[256,1024]{0,1:T(8,128)(2,1)}, ...), condition=%wide.region_25.26_spmd.clone, body=%wide.region_24.25_spmd.clone.sunk | while | flops 682295808 | bytes 62579328 | solution.py:420
  1202.2 18.7 %collective-permute-start.2 = (bf16[256,1024]{0,1:T(8,128)(2,1)}, bf16[256,1024]{0,1:T(8,128)(2,1)}, u32[]{:S(2)}, u32[]{:S(2)}) collective-permute-start(bf16[256,1024]{0,1:T(8,128)(2,1)} %fusion.270), channel_id=1, source_target_pairs={{7,0},{0,1},{1,2},{2,3},{3,4},{4,5},{5,6},{6,7},{15,8},{8,9},{9,10... | collective-permute-start | bytes 1572872 | tf_op jit(solution)/shard_map/while/body/eval_jaxpr/ppermute | solution.py:19
  1250.8 26.8 %collective-permute-start.2 = (bf16[256,1024]{0,1:T(8,128)(2,1)}, bf16[256,1024]{0,1:T(8,128)(2,1)}, u32[]{:S(2)}, u32[]{:S(2)}) collective-permute-start(bf16[256,1024]{0,1:T(8,128)(2,1)} %fusion.270), channel_id=1, source_target_pairs={{7,0},{0,1},{1,2},{2,3},{3,4},{4,5},{5,6},{6,7},{15,8},{8,9},{9,10... | collective-permute-start | bytes 1572872 | tf_op jit(solution)/shard_map/while/body/eval_jaxpr/ppermute | solution.py:19
  1313.6 13.9 collective-permute-start.2
  1505.1 56.4 %reduce-scatter.14.cloned.1.call-done = bf16[128,3072]{1,0:T(8,128)(2,1)} async-done(((bf16[1024,3072]{1,0:T(8,128)(2,1)}), bf16[128,3072]{1,0:T(8,128)(2,1)}) %reduce-scatter.14.cloned.1.call-update) | async-done | bytes 786448 | tf_op jit(solution)/shard_map/reduce_scatter | solution.py:471
  1561.5 90.3 %reduce-scatter.22.cloned.1.call-done = bf16[128,4096]{1,0:T(8,128)(2,1)} async-done(((bf16[1024,4096]{1,0:T(8,128)(2,1)}), bf16[128,4096]{1,0:T(8,128)(2,1)}) %reduce-scatter.22.cloned.1.call-update) | async-done | bytes 1048592 | tf_op jit(solution)/shard_map/reduce_scatter | solution.py:513
  1651.8 90.1 %reduce-scatter.24.cloned.1.call-done = bf16[512,1024]{1,0:T(8,128)(2,1)} async-done(((bf16[4096,1024]{1,0:T(8,128)(2,1)}), bf16[512,1024]{1,0:T(8,128)(2,1)}) %reduce-scatter.24.cloned.1.call-update) | async-done | bytes 1048592 | tf_op jit(solution)/shard_map/reduce_scatter | solution.py:519
  1766.0 26.3 %all-reduce.17 = (bf16[1024]{0:T(1024)(128)(2,1)S(1)}, bf16[1024]{0:T(1024)(128)(2,1)S(1)}, bf16[2048]{0:T(1024)(128)(2,1)S(1)}, bf16[1024]{0:T(1024)(128)(2,1)S...) all-reduce(bf16[1024]{0:T(1024)(128)(2,1)S(1)} %get-tuple-element.1, ...), channel_id=5, replica_groups=mesh['rows'=4,'seq'=8] {'seq'}, use_global_device_ids=true, to_apply=%region_31.32.clone | all-reduce | flops 17408 | bytes 69632
  1793.3 10.2 all-reduce.18
  1813.1 38.2 %all-reduce.23.cloned.1.call-done = (bf16[128,2048]{0,1:T(8,128)(2,1)}, bf16[128,3072]{1,0:T(8,128)(2,1)}, bf16[128,1024]{1,0:T(8,128)(2,1)}, bf16[128,1024]{1,0...) async-done(((bf16[128,2048]{0,1:T(8,128)(2,1)}, bf16[128,3072]{1,0:T(8,128)(2,1)}, bf16[128,1024]{1,0:T(8,128)(2,1)}, ...) | async-done | bytes 4194320 | tf_op jit(solution)/shard_map/psum | solution.py:537
  (862 shorter events, 955.4 us)
Async XLA Ops:
  7.2 61.6 %all-gather.7.cloned.1.call-start = ((), (), s32[]{:S(2)}) async-start(), calls=%async_computation.8 | async-start | bytes 4718592 | tf_op jit(solution)/shard_map/all_gather | solution.py:230
  18.8 109.3 %all-gather.5.cloned.1.call-start = ((), (), s32[]{:S(2)}) async-start(), calls=%async_computation.7 | async-start | bytes 4718592 | tf_op jit(solution)/shard_map/all_gather | solution.py:231
  21.6 267.8 %all-gather.9.cloned.1.call-start = ((), (), s32[]{:S(2)}) async-start(), calls=%async_computation.15 | async-start | bytes 21676032 | tf_op jit(solution)/shard_map/all_gather | solution.py:248
  26.2 1476.9 %reduce-scatter.26.cloned.1.call-start = ((), (), s32[]{:S(2)}) async-start(), calls=%async_computation.16 | async-start | bytes 4718592
  1130.0 375.2 %reduce-scatter.20.cloned.1.call-start = ((), (), s32[]{:S(2)}) async-start(), calls=%async_computation.12 | async-start | bytes 2359296 | tf_op jit(solution)/shard_map/reduce_scatter | solution.py:501
  1133.4 371.7 %reduce-scatter.18.cloned.1.call-start = ((), (), s32[]{:S(2)}) async-start(), calls=%async_computation.11 | async-start | bytes 2359296 | tf_op jit(solution)/shard_map/reduce_scatter | solution.py:489
  1138.0 367.1 %reduce-scatter.16.cloned.1.call-start = ((), (), s32[]{:S(2)}) async-start(), calls=%async_computation.10 | async-start | bytes 2359296 | tf_op jit(solution)/shard_map/reduce_scatter | solution.py:477
  1154.0 407.5 %reduce-scatter.14.cloned.1.call-start = ((), (), s32[]{:S(2)}) async-start(), calls=%async_computation.9 | async-start | bytes 7077888 | tf_op jit(solution)/shard_map/reduce_scatter | solution.py:471
  1165.8 17.5 collective-permute-start.2
  1167.4 21.4 %collective-permute-start.3 = (bf16[256,1024]{0,1:T(8,128)(2,1)}, bf16[256,1024]{0,1:T(8,128)(2,1)}, u32[]{:S(2)}, u32[]{:S(2)}) collective-permute-start(bf16[256,1024]{0,1:T(8,128)(2,1)} %fusion.272), channel_id=1, source_target_pairs={{7,0},{0,1},{1,2},{2,3},{3,4},{4,5},{5,6},{6,7},{15,8},{8,9},{9,10... | collective-permute-start | bytes 1572872 | tf_op jit(solution)/shard_map/while/body/eval_jaxpr/ppermute | solution.py:19
  1168.5 22.5 %collective-permute-start = (bf16[256,1024]{0,1:T(8,128)(2,1)}, bf16[256,1024]{0,1:T(8,128)(2,1)}, u32[]{:S(2)}, u32[]{:S(2)}) collective-permute-start(bf16[256,1024]{0,1:T(8,128)(2,1)} %copy.208), channel_id=1, source_target_pairs={{0,1},{1,2},{2,3},{3,4},{4,5},{5,6},{6,7},{8,9},{9,10},{10,11},{11... | collective-permute-start | bytes 1572872 | tf_op jit(solution)/shard_map/while/body/eval_jaxpr/ppermute | solution.py:25
  1171.3 19.6 %collective-permute-start.1 = (bf16[256,1024]{0,1:T(8,128)(2,1)}, bf16[256,1024]{0,1:T(8,128)(2,1)}, u32[]{:S(2)}, u32[]{:S(2)}) collective-permute-start(bf16[256,1024]{0,1:T(8,128)(2,1)} %copy.209), channel_id=1, source_target_pairs={{0,1},{1,2},{2,3},{3,4},{4,5},{5,6},{6,7},{8,9},{9,10},{10,11},{11... | collective-permute-start | bytes 1572872 | tf_op jit(solution)/shard_map/while/body/eval_jaxpr/ppermute | solution.py:25
  1202.2 33.2 %collective-permute-start.2 = (bf16[256,1024]{0,1:T(8,128)(2,1)}, bf16[256,1024]{0,1:T(8,128)(2,1)}, u32[]{:S(2)}, u32[]{:S(2)}) collective-permute-start(bf16[256,1024]{0,1:T(8,128)(2,1)} %fusion.270), channel_id=1, source_target_pairs={{7,0},{0,1},{1,2},{2,3},{3,4},{4,5},{5,6},{6,7},{15,8},{8,9},{9,10... | collective-permute-start | bytes 1572872 | tf_op jit(solution)/shard_map/while/body/eval_jaxpr/ppermute | solution.py:19
  1222.4 15.1 collective-permute-start.3
  1224.9 14.7 collective-permute-start
  1250.8 41.2 %collective-permute-start.2 = (bf16[256,1024]{0,1:T(8,128)(2,1)}, bf16[256,1024]{0,1:T(8,128)(2,1)}, u32[]{:S(2)}, u32[]{:S(2)}) collective-permute-start(bf16[256,1024]{0,1:T(8,128)(2,1)} %fusion.270), channel_id=1, source_target_pairs={{7,0},{0,1},{1,2},{2,3},{3,4},{4,5},{5,6},{6,7},{15,8},{8,9},{9,10... | collective-permute-start | bytes 1572872 | tf_op jit(solution)/shard_map/while/body/eval_jaxpr/ppermute | solution.py:19
  1279.0 21.3 %collective-permute-start.3 = (bf16[256,1024]{0,1:T(8,128)(2,1)}, bf16[256,1024]{0,1:T(8,128)(2,1)}, u32[]{:S(2)}, u32[]{:S(2)}) collective-permute-start(bf16[256,1024]{0,1:T(8,128)(2,1)} %fusion.272), channel_id=1, source_target_pairs={{7,0},{0,1},{1,2},{2,3},{3,4},{4,5},{5,6},{6,7},{15,8},{8,9},{9,10... | collective-permute-start | bytes 1572872 | tf_op jit(solution)/shard_map/while/body/eval_jaxpr/ppermute | solution.py:19
  1281.5 20.8 %collective-permute-start = (bf16[256,1024]{0,1:T(8,128)(2,1)}, bf16[256,1024]{0,1:T(8,128)(2,1)}, u32[]{:S(2)}, u32[]{:S(2)}) collective-permute-start(bf16[256,1024]{0,1:T(8,128)(2,1)} %copy.208), channel_id=1, source_target_pairs={{0,1},{1,2},{2,3},{3,4},{4,5},{5,6},{6,7},{8,9},{9,10},{10,11},{11... | collective-permute-start | bytes 1572872 | tf_op jit(solution)/shard_map/while/body/eval_jaxpr/ppermute | solution.py:25
  1284.4 18.0 collective-permute-start.1
  1313.6 28.1 %collective-permute-start.2 = (bf16[256,1024]{0,1:T(8,128)(2,1)}, bf16[256,1024]{0,1:T(8,128)(2,1)}, u32[]{:S(2)}, u32[]{:S(2)}) collective-permute-start(bf16[256,1024]{0,1:T(8,128)(2,1)} %fusion.270), channel_id=1, source_target_pairs={{7,0},{0,1},{1,2},{2,3},{3,4},{4,5},{5,6},{6,7},{15,8},{8,9},{9,10... | collective-permute-start | bytes 1572872 | tf_op jit(solution)/shard_map/while/body/eval_jaxpr/ppermute | solution.py:19
  1329.0 14.8 collective-permute-start.3
  1331.5 14.4 collective-permute-start
  1357.1 21.6 %collective-permute-start.2 = (bf16[256,1024]{0,1:T(8,128)(2,1)}, bf16[256,1024]{0,1:T(8,128)(2,1)}, u32[]{:S(2)}, u32[]{:S(2)}) collective-permute-start(bf16[256,1024]{0,1:T(8,128)(2,1)} %fusion.270), channel_id=1, source_target_pairs={{7,0},{0,1},{1,2},{2,3},{3,4},{4,5},{5,6},{6,7},{15,8},{8,9},{9,10... | collective-permute-start | bytes 1572872 | tf_op jit(solution)/shard_map/while/body/eval_jaxpr/ppermute | solution.py:19
  1366.0 14.8 collective-permute-start.3
  1368.4 14.4 collective-permute-start
  1394.1 21.6 %collective-permute-start.2 = (bf16[256,1024]{0,1:T(8,128)(2,1)}, bf16[256,1024]{0,1:T(8,128)(2,1)}, u32[]{:S(2)}, u32[]{:S(2)}) collective-permute-start(bf16[256,1024]{0,1:T(8,128)(2,1)} %fusion.270), channel_id=1, source_target_pairs={{7,0},{0,1},{1,2},{2,3},{3,4},{4,5},{5,6},{6,7},{15,8},{8,9},{9,10... | collective-permute-start | bytes 1572872 | tf_op jit(solution)/shard_map/while/body/eval_jaxpr/ppermute | solution.py:19
  1402.9 14.8 collective-permute-start.3
  1431.0 21.6 %collective-permute-start.2 = (bf16[256,1024]{0,1:T(8,128)(2,1)}, bf16[256,1024]{0,1:T(8,128)(2,1)}, u32[]{:S(2)}, u32[]{:S(2)}) collective-permute-start(bf16[256,1024]{0,1:T(8,128)(2,1)} %fusion.270), channel_id=1, source_target_pairs={{7,0},{0,1},{1,2},{2,3},{3,4},{4,5},{5,6},{6,7},{15,8},{8,9},{9,10... | collective-permute-start | bytes 1572872 | tf_op jit(solution)/shard_map/while/body/eval_jaxpr/ppermute | solution.py:19
  1439.9 14.8 collective-permute-start.3
  1486.8 165.0 %reduce-scatter.22.cloned.1.call-start = ((), (), s32[]{:S(2)}) async-start(), calls=%async_computation.13 | async-start | bytes 9437184 | tf_op jit(solution)/shard_map/reduce_scatter | solution.py:513
  1495.4 246.6 %reduce-scatter.24.cloned.1.call-start = ((), (), s32[]{:S(2)}) async-start(), calls=%async_computation.14 | async-start | bytes 9437184 | tf_op jit(solution)/shard_map/reduce_scatter | solution.py:519
  1502.8 348.5 %all-reduce.23.cloned.1.call-start = ((), (), s32[]{:S(2)}) async-start(), calls=%async_computation.17 | async-start | bytes 8388608 | tf_op jit(solution)/shard_map/psum | solution.py:537
  (147 other events, 2699.5 us)
Sparse Core Ops, SparseCore 0:
  18.9 49.8 all-gather.6
  71.0 45.8 all-gather.4
  119.1 170.2 all-gather.8
  1130.0 51.4 reduce-scatter.25
  1183.7 38.7 reduce-scatter.19
  1225.2 38.5 reduce-scatter.17
  1266.7 37.8 reduce-scatter.15
  1486.9 74.5 reduce-scatter.13
  1563.8 87.9 reduce-scatter.21
  1654.0 87.9 reduce-scatter.23
  1746.4 104.8 all-reduce.22
where the time goes:
time: 1880 us; the launch traced here: 1870 us
  matrix products  480 us (26%)
  waiting for transfers between devices  436 us (23%)
  local copies, waits for them, and re-layouts  349 us (19%)
  blocking collectives  227 us (12%)
  other arithmetic  194 us (10%)
  starting transfers between devices  157 us (8%)
    unnamed x2, blocking collectives  217 us
    ppermute x16, starting transfers between devices, from_behind(): return lax.ppermute(block, axis, route)  108 us
    all_gather x1, waiting for transfers between devices, body(): lax.all_gather(mem_rows, 'seq', axis=0, tiled=True)  101 us
    reduce_scatter x1, waiting for transfers between devices, body(): lax.psum_scatter(grad_terms[16].astype(jnp.bfloat16), 'seq', scatter_dime...  90.3 us
    reduce_scatter x1, waiting for transfers between devices, body(): lax.psum_scatter(grad_terms[18].astype(jnp.bfloat16), 'seq', scatter_dime...  90.1 us
    unnamed x227, local copies, waits for them, and re-layouts  87.5 us
    dot_general x12, matrix products, head_scores(): jnp.einsum('thd,nhd->htn', query_heads, split_heads(key_block, head_count...  69.6 us
    reduce_sum x12, other arithmetic, stat_update(): jnp.sum(kept_exp, axis=-1)  66.8 us
  transfers between devices with their start and end apart: 43, of which 10 were waited for; matrix products, arithmetic and copies ran while one was open for 19% of the time, Pallas kernels for 0%

commit v1 on v0

v1 whole, which is shorter than its diff:
```python
import functools

import jax
import jax.numpy as jnp
from jax import lax
from jax.experimental import pallas as pl
from jax.experimental.pallas import tpu as pltpu
from jax.sharding import PartitionSpec as P

HEADS = 16
DEPTH = 64
PAGES = 8
PAGE_TOK = 588
PAGE_PAD = 640
SLOTS = 128
BLOCK = 256


NEGATIVE = -1e30
SCALE = 0.125
EPSILON = 1e-05
MESH = pl.DeviceIdType.MESH
VMEM_LIMIT = 56 * 1024 * 1024


def norm_forward(values, gain, shift):
    center = values - jnp.mean(values, axis=-1, keepdims=True)
    spread = jnp.mean(center * center, axis=-1, keepdims=True)
    return center * lax.rsqrt(spread + EPSILON) * gain + shift


def gelu_exact(values):
    return jax.nn.gelu(values, approximate=False)


def norm_backward(values, gain, shift, grad_normed):
    _, pullback = jax.vjp(norm_forward, values, gain, shift)
    return pullback(grad_normed)


def dot_plain(first, second):
    return jnp.dot(first, second, preferred_element_type=jnp.float32)


def dot_left(first, second):
    return lax.dot_general(
        first, second, (((0,), (0,)), ((), ())), preferred_element_type=jnp.float32
    )


def dot_right(first, second):
    return lax.dot_general(
        first, second, (((1,), (1,)), ((), ())), preferred_element_type=jnp.float32
    )


def low(values):
    return values.astype(jnp.bfloat16)


def wide(values):
    return values.astype(jnp.float32)


def place(index):
    return (lax.axis_index("rows"), index)


def gather_kernel(count, block_ref, whole_ref, own_sem, send_sem, recv_sem):
    rows = block_ref.shape[0]
    me = lax.axis_index("seq")
    chip, core, chips = me // 2, me % 2, count // 2
    other = me + 1 - 2 * core
    barrier = pltpu.get_barrier_semaphore()

    def block(index):
        return whole_ref.at[pl.ds(index * rows, rows)]

    pl.semaphore_signal(barrier, inc=1, device_id=place(other), device_id_type=MESH)

    @pl.when(chip > 0)
    def _():
        pl.semaphore_signal(barrier, inc=1, device_id=place(me - 2), device_id_type=MESH)

    @pl.when(chip < chips - 1)
    def _():
        pl.semaphore_signal(barrier, inc=1, device_id=place(me + 2), device_id_type=MESH)

    peers = 1 + jnp.where(chip > 0, 1, 0) + jnp.where(chip < chips - 1, 1, 0)
    pl.semaphore_wait(barrier, peers)
    own = pltpu.make_async_copy(block_ref, block(me), own_sem)
    own.start()

    def copy(lane, source, target, from_own=False):
        there = block(2 * source + core)
        return pltpu.make_async_remote_copy(
            src_ref=block_ref if from_own else there,
            dst_ref=there,
            send_sem=send_sem.at[lane, source],
            recv_sem=recv_sem.at[lane, source],
            device_id=place(target),
            device_id_type=MESH,
        )

    def right(source, from_own=False):
        return copy(0, source, me + 2, from_own)

    def left(source, from_own=False):
        return copy(1, source, me - 2, from_own)

    def across(source, from_own=False):
        return copy(2, source, other, from_own)

    @pl.when(chip < chips - 1)
    def _():
        right(chip, True).start()

    @pl.when(chip > 0)
    def _():
        left(chip, True).start()

    across(chip, True).start()
    for step in range(1, chips):

        @pl.when(chip - step >= 0)
        def _():
            right(chip - step).wait_recv()

            @pl.when(chip < chips - 1)
            def _():
                right(chip - step).start()

            across(chip - step).start()

        @pl.when(chip + step < chips)
        def _():
            left(chip + step).wait_recv()

            @pl.when(chip > 0)
            def _():
                left(chip + step).start()

            across(chip + step).start()

    own.wait()
    for source in range(chips):
        there = block(2 * source + 1 - core)
        pltpu.make_async_remote_copy(
            src_ref=there,
            dst_ref=there,
            send_sem=send_sem.at[2, source],
            recv_sem=recv_sem.at[2, source],
            device_id=place(other),
            device_id_type=MESH,
        ).wait_recv()
        across(source).wait_send()

        @pl.when((source <= chip) & (chip < chips - 1))
        def _():
            right(source).wait_send()

        @pl.when((source >= chip) & (chip > 0))
        def _():
            left(source).wait_send()


def gather_rows(block_in, count, collective_id):
    rows, width = block_in.shape
    return pl.pallas_call(
        functools.partial(gather_kernel, count),
        out_shape=jax.ShapeDtypeStruct((count * rows, width), block_in.dtype),
        in_specs=[pl.BlockSpec(memory_space=pl.ANY)],
        out_specs=pl.BlockSpec(memory_space=pl.ANY),
        scratch_shapes=[
            pltpu.SemaphoreType.DMA,
            pltpu.SemaphoreType.DMA((3, count // 2)),
            pltpu.SemaphoreType.DMA((3, count // 2)),
        ],
        compiler_params=pltpu.CompilerParams(
            collective_id=collective_id, has_side_effects=True
        ),
    )(block_in)


def exchange_kernel(count, parts, *refs):
    ins, outs = refs[: len(parts)], refs[len(parts) : 2 * len(parts)]
    own_sem, send_sem, recv_sem = refs[2 * len(parts) :]
    me = lax.axis_index("seq")
    barrier = pltpu.get_barrier_semaphore()
    for step in range(1, count):
        pl.semaphore_signal(
            barrier, inc=1, device_id=place(lax.rem(me + step, count)), device_id_type=MESH
        )
    pl.semaphore_wait(barrier, count - 1)
    own = []
    for index, same in enumerate(parts):
        source = ins[index] if same else ins[index].at[me]
        own.append(pltpu.make_async_copy(source, outs[index].at[me], own_sem.at[index]))
        own[-1].start()
    copies = []
    order = sorted(range(1, count), key=lambda step: -min(step, count - step))
    for step in order:
        target = lax.rem(me + step, count)
        for index, same in enumerate(parts):
            copies.append(
                pltpu.make_async_remote_copy(
                    src_ref=ins[index] if same else ins[index].at[target],
                    dst_ref=outs[index].at[me],
                    send_sem=send_sem.at[index, step],
                    recv_sem=recv_sem.at[index, step],
                    device_id=place(target),
                    device_id_type=MESH,
                )
            )
            copies[-1].start()
    for copy in copies:
        copy.wait()
    for copy in own:
        copy.wait()


def exchange(arrays, parts, count, collective_id):
    shapes = [
        jax.ShapeDtypeStruct(
            (count,) + (array.shape if same else array.shape[1:]), array.dtype
        )
        for array, same in zip(arrays, parts)
    ]
    return pl.pallas_call(
        functools.partial(exchange_kernel, count, parts),
        out_shape=shapes,
        in_specs=[pl.BlockSpec(memory_space=pl.ANY)] * len(arrays),
        out_specs=[pl.BlockSpec(memory_space=pl.ANY)] * len(arrays),
        scratch_shapes=[
            pltpu.SemaphoreType.DMA((len(arrays),)),
            pltpu.SemaphoreType.DMA((len(arrays), count)),
            pltpu.SemaphoreType.DMA((len(arrays), count)),
        ],
        compiler_params=pltpu.CompilerParams(
            collective_id=collective_id, has_side_effects=True
        ),
    )(*arrays)


def head_lanes(width):
    return lax.broadcasted_iota(jnp.int32, (1, width), 1) // DEPTH


def pick_head(values, head, width):
    if width == DEPTH:
        return values
    return jnp.where(head_lanes(width) == head, values, jnp.zeros_like(values))


def self_forward_kernel(qkv_ref, start_ref, out_ref, stat_ref):
    length, width = out_ref.shape
    heads = width // DEPTH
    blocks = length // BLOCK
    for index in range(blocks):
        rows = pl.ds(index * BLOCK, BLOCK)
        keys_end = (index + 1) * BLOCK
        query = qkv_ref[rows, 0:width]
        begin = start_ref[rows, :]
        position = index * BLOCK + lax.broadcasted_iota(jnp.int32, (BLOCK, 1), 0)
        if index == blocks - 1 or index <= 1:
            cuts = [(0, keys_end)]
        else:
            cuts = [(0, BLOCK), (BLOCK, index * BLOCK), (index * BLOCK, keys_end)]
        outs, stats = [], []
        for head in range(heads):
            query_head = pick_head(query, head, width) * jnp.bfloat16(SCALE)
            scores = []
            for low_end, high_end in cuts:
                part = dot_right(query_head, qkv_ref[low_end:high_end, width : 2 * width])
                if low_end == 0 or high_end == keys_end:
                    column = low_end + lax.broadcasted_iota(jnp.int32, part.shape, 1)
                    allowed = column >= begin
                    if high_end == keys_end:
                        allowed = allowed & (column <= position)
                    part = jnp.where(allowed, part, NEGATIVE)
                scores.append(part)
            top = functools.reduce(
                jnp.maximum, [jnp.max(part, axis=-1, keepdims=True) for part in scores]
            )
            total, mixed = 0.0, 0.0
            for (low_end, high_end), part in zip(cuts, scores):
                weight = jnp.exp(part - top)
                total = total + jnp.sum(weight, axis=-1, keepdims=True)
                mixed = mixed + dot_plain(
                    low(weight), qkv_ref[low_end:high_end, 2 * width : 3 * width]
                )
            outs.append(mixed / total)
            stats.append(top + jnp.log(total))
        merged = outs[0]
        for head in range(1, heads):
            merged = jnp.where(head_lanes(width) == head, outs[head], merged)
        out_ref[rows, :] = low(merged)
        stat_ref[rows, :] = jnp.concatenate(stats, axis=1)


def self_forward(qkv, begins):
    length, width = qkv.shape[0], qkv.shape[1] // 3
    heads = width // DEPTH
    return pl.pallas_call(
        self_forward_kernel,
        out_shape=(
            jax.ShapeDtypeStruct((length, width), jnp.bfloat16),
            jax.ShapeDtypeStruct((length, heads), jnp.float32),
        ),
        in_specs=[pl.BlockSpec(memory_space=pltpu.VMEM)] * 2,
        out_specs=[pl.BlockSpec(memory_space=pltpu.VMEM)] * 2,
        compiler_params=pltpu.CompilerParams(vmem_limit_bytes=VMEM_LIMIT),
    )(qkv, begins[:, None])


def self_backward_kernel(qkv_ref, out_ref, grad_ref, start_ref, stat_ref, dqkv_ref, dk_ref, dv_ref):
    length, width = out_ref.shape
    heads = width // DEPTH
    blocks = length // BLOCK
    dk_ref[...] = jnp.zeros_like(dk_ref)
    dv_ref[...] = jnp.zeros_like(dv_ref)

    def query_block(index, carry):
        rows = pl.ds(pl.multiple_of(index * BLOCK, BLOCK), BLOCK)
        query = qkv_ref[rows, 0:width]
        grad = grad_ref[rows, :]
        product = (wide(grad) * wide(out_ref[rows, :])).T
        begin = start_ref[:, rows]
        position = index * BLOCK + lax.broadcasted_iota(jnp.int32, (1, BLOCK), 1)
        query_heads = [pick_head(query, head, width) * jnp.bfloat16(SCALE) for head in range(heads)]
        grad_heads = [pick_head(grad, head, width) for head in range(heads)]
        stats = [stat_ref[head : head + 1, rows] for head in range(heads)]
        deltas = [
            jnp.sum(product[head * DEPTH : (head + 1) * DEPTH, :], axis=0, keepdims=True)
            for head in range(heads)
        ]

        def key_block(key_index, sums):
            keys = pl.ds(pl.multiple_of(key_index * BLOCK, BLOCK), BLOCK)
            key = qkv_ref[keys, width : 2 * width]
            value = qkv_ref[keys, 2 * width : 3 * width]
            row = key_index * BLOCK + lax.broadcasted_iota(jnp.int32, (BLOCK, 1), 0)
            allowed = (row >= begin) & (row <= position)
            dk_part, dv_part, found = 0.0, 0.0, []
            for head in range(heads):
                scores = jnp.where(allowed, dot_right(key, query_heads[head]), NEGATIVE)
                prob = jnp.exp(scores - stats[head])
                dv_part = dv_part + dot_plain(low(prob), grad_heads[head])
                grad_prob = dot_right(value, grad_heads[head])
                grad_score = low(prob * (grad_prob - deltas[head]))
                dk_part = dk_part + dot_plain(grad_score, query_heads[head])
                found.append(sums[head] + dot_left(grad_score, key))
            dk_ref[keys, :] += dk_part
            dv_ref[keys, :] += dv_part
            return tuple(found)

        zero = tuple(jnp.zeros((BLOCK, width), jnp.float32) for _ in range(heads))
        sums = lax.fori_loop(0, index + 1, key_block, zero)
        merged = sums[0]
        for head in range(1, heads):
            merged = jnp.where(head_lanes(width) == head, sums[head], merged)
        dqkv_ref[rows, 0:width] = low(merged * SCALE)
        return carry

    lax.fori_loop(0, blocks, query_block, 0)
    dqkv_ref[:, width : 2 * width] = low(dk_ref[...])
    dqkv_ref[:, 2 * width : 3 * width] = low(dv_ref[...])


def self_backward(qkv, out, grad, begins, stats):
    length, width = out.shape
    return pl.pallas_call(
        self_backward_kernel,
        out_shape=jax.ShapeDtypeStruct((length, 3 * width), jnp.bfloat16),
        in_specs=[pl.BlockSpec(memory_space=pltpu.VMEM)] * 5,
        out_specs=pl.BlockSpec(memory_space=pltpu.VMEM),
        scratch_shapes=[pltpu.VMEM((length, width), jnp.float32)] * 2,
        compiler_params=pltpu.CompilerParams(vmem_limit_bytes=VMEM_LIMIT),
    )(qkv, out, grad, begins[None, :], stats.T)


def cross_forward_kernel(query_ref, key_ref, value_ref, own_key_ref, own_value_ref, out_ref, stat_ref):
    tokens = query_ref.shape[0] - SLOTS
    width = query_ref.shape[1]
    for begin, size, keys, values in (
        (0, tokens, key_ref, value_ref),
        (tokens, SLOTS, own_key_ref, own_value_ref),
    ):
        query = query_ref[begin : begin + size, :]
        outs = []
        for head in range(width // DEPTH):
            query_head = pick_head(query, head, width) * jnp.bfloat16(SCALE)
            scores = dot_right(query_head, keys[...])
            column = lax.broadcasted_iota(jnp.int32, scores.shape, 1)
            scores = jnp.where(column < PAGE_TOK, scores, NEGATIVE)
            top = jnp.max(scores, axis=-1, keepdims=True)
            weight = jnp.exp(scores - top)
            total = jnp.sum(weight, axis=-1, keepdims=True)
            outs.append(dot_plain(low(weight), values[...]) / total)
            stat_ref[0, begin : begin + size, head : head + 1] = top + jnp.log(total)
        merged = outs[0]
        for head in range(1, len(outs)):
            merged = jnp.where(head_lanes(width) == head, outs[head], merged)
        out_ref[begin : begin + size, :] = low(merged)


def cross_forward(query, kv_big, kv_own):
    rows, features = query.shape
    pair = 2 * DEPTH
    steps = features // pair
    tall = pl.BlockSpec((rows, pair), lambda i: (0, i))
    keys = pl.BlockSpec((PAGE_PAD, pair), lambda i: (0, i))
    values = pl.BlockSpec((PAGE_PAD, pair), lambda i: (0, i + steps))
    return pl.pallas_call(
        cross_forward_kernel,
        grid=(steps,),
        out_shape=(
            jax.ShapeDtypeStruct((rows, features), jnp.bfloat16),
            jax.ShapeDtypeStruct((steps, rows, 2), jnp.float32),
        ),
        in_specs=[tall, keys, values, keys, values],
        out_specs=[tall, pl.BlockSpec((1, rows, 2), lambda i: (i, 0, 0))],
        compiler_params=pltpu.CompilerParams(vmem_limit_bytes=VMEM_LIMIT),
    )(query, kv_big, kv_big, kv_own, kv_own)


def cross_backward_kernel(
    query_ref,
    key_ref,
    value_ref,
    own_key_ref,
    own_value_ref,
    out_ref,
    grad_ref,
    stat_ref,
    dq_ref,
    dk_ref,
    dv_ref,
    own_dk_ref,
    own_dv_ref,
):
    tokens = query_ref.shape[0] - SLOTS
    width = query_ref.shape[1]
    row = lax.broadcasted_iota(jnp.int32, (PAGE_PAD, 1), 0)
    for begin, size, keys, values, dk_out, dv_out in (
        (0, tokens, key_ref, value_ref, dk_ref, dv_ref),
        (tokens, SLOTS, own_key_ref, own_value_ref, own_dk_ref, own_dv_ref),
    ):
        rows = slice(begin, begin + size)
        query, grad = query_ref[rows, :], grad_ref[rows, :]
        product = (wide(grad) * wide(out_ref[rows, :])).T
        dk_sum, dv_sum, found = 0.0, 0.0, []
        for head in range(width // DEPTH):
            query_head = pick_head(query, head, width) * jnp.bfloat16(SCALE)
            grad_head = pick_head(grad, head, width)
            delta = jnp.sum(product[head * DEPTH : (head + 1) * DEPTH, :], axis=0, keepdims=True)
            scores = dot_right(keys[...], query_head)
            scores = jnp.where(row < PAGE_TOK, scores, NEGATIVE)
            prob = jnp.exp(scores - stat_ref[0, head : head + 1, rows])
            dv_sum = dv_sum + dot_plain(low(prob), grad_head)
            grad_prob = dot_right(values[...], grad_head)
            grad_score = low(prob * (grad_prob - delta))
            dk_sum = dk_sum + dot_plain(grad_score, query_head)
            found.append(dot_left(grad_score, keys[...]))
        merged = found[0]
        for head in range(1, len(found)):
            merged = jnp.where(head_lanes(width) == head, found[head], merged)
        dq_ref[rows, :] = low(merged * SCALE)
        dk_out[...] = low(dk_sum)
        dv_out[...] = low(dv_sum)


def cross_backward(query, kv_big, kv_own, out, grad, stats):
    rows, features = query.shape
    pair = 2 * DEPTH
    steps = features // pair
    tall = pl.BlockSpec((rows, pair), lambda i: (0, i))
    keys = pl.BlockSpec((PAGE_PAD, pair), lambda i: (0, i))
    values = pl.BlockSpec((PAGE_PAD, pair), lambda i: (0, i + steps))
    page = jax.ShapeDtypeStruct((PAGE_PAD, features), jnp.bfloat16)
    return pl.pallas_call(
        cross_backward_kernel,
        grid=(steps,),
        out_shape=(jax.ShapeDtypeStruct((rows, features), jnp.bfloat16), page, page, page, page),
        in_specs=[
            tall,
            keys,
            values,
            keys,
            values,
            tall,
            tall,
            pl.BlockSpec((1, 2, rows), lambda i: (i, 0, 0)),
        ],
        out_specs=[tall, keys, keys, keys, keys],
        compiler_params=pltpu.CompilerParams(vmem_limit_bytes=VMEM_LIMIT),
    )(query, kv_big, kv_big, kv_own, kv_own, out, grad, stats.transpose(0, 2, 1))


def body(
    inputs,
    memory,
    out_grad,
    segment_ids,
    page_order,
    norm1_gain,
    norm1_bias,
    qkv_weight,
    qv_bias,
    self_out_weight,
    self_out_bias,
    norm2_gain,
    norm2_bias,
    cross_q_weight,
    cross_q_bias,
    cross_kv_weight,
    cross_v_bias,
    cross_out_weight,
    cross_out_bias,
    norm3_gain,
    norm3_bias,
    fc1_weight,
    fc1_bias,
    fc2_weight,
    fc2_bias,
):
    tokens, features = inputs.shape[1:]
    count = lax.axis_size("seq")
    me = lax.axis_index("seq")
    length = tokens * count
    width = features // count
    mem_rows = memory.shape[1]
    sharers = PAGE_TOK // mem_rows
    row_segs = segment_ids[0]
    row_pages = page_order[0]
    gain_one, shift_one = wide(norm1_gain), wide(norm1_bias)
    gain_two, shift_two = wide(norm2_gain), wide(norm2_bias)
    gain_three, shift_three = wide(norm3_gain), wide(norm3_bias)

    page_sizes = jnp.sum(row_segs[None, :] == jnp.arange(PAGES)[:, None], axis=1)
    page_starts = jnp.cumsum(page_sizes) - page_sizes
    begins = sum(
        jnp.where(row_segs == page, page_starts[page], 0) for page in range(PAGES)
    ).astype(jnp.int32)
    big_page = row_segs[length // 2]
    big_start = jnp.sum(row_segs < big_page)
    own_page = lax.dynamic_index_in_dim(row_pages, me // sharers, 0, keepdims=False)
    slot = jnp.arange(SLOTS)
    in_front = (slot < big_start)[:, None]
    slot_segs = jnp.where(slot < big_start, row_segs[:SLOTS], row_segs[length - SLOTS :])
    slot_mine = (slot_segs == own_page) & (slot * sharers // SLOTS == me % sharers)
    home_segs = lax.dynamic_slice_in_dim(row_segs, me * tokens, tokens, 0)
    active = jnp.concatenate((home_segs == big_page, slot_mine))[:, None]
    is_first, is_last = me == 0, me == count - 1

    def slots_of(front, back):
        return jnp.where(in_front, front, back)

    mem_own = memory[0]
    mem_page = mem_own
    if sharers > 1:
        groups = [[g * sharers + s for s in range(sharers)] for g in range(count // sharers)]
        mem_page = lax.all_gather(mem_own, "seq", axis=0, tiled=True, axis_index_groups=groups)
    mem_page = jnp.pad(mem_page, ((0, PAGE_PAD - PAGE_TOK), (0, 0)))
    gives_big = (own_page == big_page) & (me % sharers == 0)
    ends_grad = jnp.where(
        is_first, out_grad[0, :SLOTS], jnp.zeros((SLOTS, features), jnp.bfloat16)
    ), jnp.where(is_last, out_grad[0, tokens - SLOTS :], jnp.zeros((SLOTS, features), jnp.bfloat16))
    mem_big, front_grad, back_grad = lax.psum(
        (jnp.where(gives_big, mem_page, jnp.zeros_like(mem_page)), *ends_grad), "seq"
    )

    x_own = inputs[0]
    x_all = gather_rows(x_own, count, 0)
    qkv_own_weight = jnp.concatenate(
        [
            lax.dynamic_slice_in_dim(qkv_weight, part * features + me * width, width, 1)
            for part in range(3)
        ],
        axis=1,
    )
    qkv_own_bias = jnp.concatenate(
        (
            lax.dynamic_slice_in_dim(qv_bias, me * width, width, 0),
            jnp.zeros((width,), jnp.bfloat16),
            lax.dynamic_slice_in_dim(qv_bias, features + me * width, width, 0),
        )
    )
    normed_all = low(norm_forward(wide(x_all), gain_one, shift_one))
    qkv = low(dot_plain(normed_all, qkv_own_weight) + wide(qkv_own_bias))
    mixed, mixed_stats = self_forward(qkv, begins)
    blocks_mixed, ends_mixed = exchange(
        (
            mixed.reshape(count, tokens, width),
            jnp.concatenate((mixed[:SLOTS], mixed[length - SLOTS :])),
        ),
        (False, True),
        count,
        1,
    )

    def beside(blocks):
        return blocks.transpose(1, 0, 2).reshape(blocks.shape[1], -1)

    attended = jnp.concatenate(
        (
            beside(blocks_mixed),
            slots_of(beside(ends_mixed[:, :SLOTS]), beside(ends_mixed[:, SLOTS:])),
        )
    )
    resid = wide(
        jnp.concatenate((x_own, slots_of(x_all[:SLOTS], x_all[length - SLOTS :])))
    )
    resid_one = resid + dot_plain(attended, self_out_weight) + wide(self_out_bias)
    normed_two = low(norm_forward(resid_one, gain_two, shift_two))
    cross_queries = low(dot_plain(normed_two, cross_q_weight) + wide(cross_q_bias))
    kv_shift = jnp.concatenate((jnp.zeros((features,), jnp.float32), wide(cross_v_bias)))
    kv_big = low(dot_plain(mem_big, cross_kv_weight) + kv_shift)
    kv_own = low(dot_plain(mem_page, cross_kv_weight) + kv_shift)
    cross_low, cross_stats = cross_forward(cross_queries, kv_big, kv_own)
    resid_two = resid_one + dot_plain(cross_low, cross_out_weight) + wide(cross_out_bias)
    normed_three = low(norm_forward(resid_two, gain_three, shift_three))
    pre_act = dot_plain(normed_three, fc1_weight) + wide(fc1_bias)
    hidden_act = low(gelu_exact(pre_act))
    final = low(resid_two + dot_plain(hidden_act, fc2_weight) + wide(fc2_bias))

    grad_out = jnp.concatenate((out_grad[0], slots_of(front_grad, back_grad)))
    grad_out = jnp.where(active, grad_out, jnp.zeros_like(grad_out))
    grad_act = dot_right(grad_out, fc2_weight)
    _, gelu_pull = jax.vjp(gelu_exact, pre_act)
    grad_pre = low(gelu_pull(grad_act)[0])
    grad_fc2_w = dot_left(hidden_act, grad_out)
    grad_fc2_b = jnp.sum(wide(grad_out), axis=0)
    grad_fc1_w = dot_left(normed_three, grad_pre)
    grad_fc1_b = jnp.sum(wide(grad_pre), axis=0)
    grad_two_norm, grad_gain_three, grad_shift_three = norm_backward(
        resid_two, gain_three, shift_three, dot_right(grad_pre, fc1_weight)
    )
    grad_resid_two = wide(grad_out) + grad_two_norm
    grad_branch_two = low(grad_resid_two)
    grad_co_w = dot_left(cross_low, grad_branch_two)
    grad_co_b = jnp.sum(wide(grad_branch_two), axis=0)
    grad_cross_low = low(dot_right(grad_branch_two, cross_out_weight))
    grad_cross_q, big_dk, big_dv, own_dk, own_dv = cross_backward(
        cross_queries, kv_big, kv_own, cross_low, grad_cross_low, cross_stats
    )
    big_dk, big_dv = lax.psum((big_dk, big_dv), "seq")
    grad_ckv = jnp.where(
        gives_big,
        jnp.concatenate((big_dk, big_dv), axis=1),
        jnp.concatenate((own_dk, own_dv), axis=1),
    )[:PAGE_TOK]
    if sharers > 1:
        grad_ckv = lax.psum_scatter(
            grad_ckv, "seq", scatter_dimension=0, tiled=True, axis_index_groups=groups
        )
    grad_ckv_w = dot_left(mem_own, grad_ckv)
    grad_cv_b = jnp.sum(wide(grad_ckv[:, features:]), axis=0)
    memory_grad = dot_right(grad_ckv, cross_kv_weight)[None]

    grad_cq_w = dot_left(normed_two, grad_cross_q)
    grad_cq_b = jnp.sum(wide(grad_cross_q), axis=0)
    grad_one_norm, grad_gain_two, grad_shift_two = norm_backward(
        resid_one, gain_two, shift_two, dot_right(grad_cross_q, cross_q_weight)
    )
    grad_resid_one = grad_resid_two + grad_one_norm
    grad_branch_one = low(grad_resid_one)
    grad_o_w = dot_left(attended, grad_branch_one)
    grad_o_b = jnp.sum(wide(grad_branch_one), axis=0)
    grad_attended = low(dot_right(grad_branch_one, self_out_weight))
    by_device = grad_attended.reshape(-1, count, width).transpose(1, 0, 2)
    blocks_grad, slots_grad = exchange(
        (by_device[:, :tokens], by_device[:, tokens:]), (False, False), count, 2
    )
    slots_grad = low(jnp.sum(wide(slots_grad), axis=0))
    grad_mixed = blocks_grad.reshape(length, width)
    no_slots = jnp.zeros_like(slots_grad)
    grad_mixed = jnp.concatenate(
        (
            grad_mixed[:SLOTS] + jnp.where(in_front, slots_grad, no_slots),
            grad_mixed[SLOTS : length - SLOTS],
            grad_mixed[length - SLOTS :] + jnp.where(in_front, no_slots, slots_grad),
        )
    )
    dqkv = self_backward(qkv, mixed, grad_mixed, begins, mixed_stats)

    slot_results = lax.psum(
        (
            jnp.where(active[tokens:], final[tokens:], jnp.zeros_like(final[tokens:])),
            low(grad_resid_one[tokens:]),
        ),
        "seq",
    )

    def at_home(own, returned, keep):
        front = is_first & in_front
        back = is_last & ~in_front
        head = jnp.where(front, returned.astype(own.dtype), own[:SLOTS])
        tail = jnp.where(back, returned.astype(own.dtype), own[tokens - SLOTS :])
        return jnp.concatenate((head, own[SLOTS : tokens - SLOTS], tail))

    layer_out = at_home(final[:tokens], slot_results[0], False)[None]
    grad_home = at_home(grad_resid_one[:tokens], slot_results[1], False)

    grad_qkv_w_own = low(dot_left(normed_all, dqkv))
    (blocks_dqkv,) = exchange((dqkv.reshape(count, tokens, 3 * width),), (False,), count, 3)
    grad_qkv = blocks_dqkv.reshape(count, tokens, 3, width).transpose(1, 2, 0, 3)
    grad_qkv = grad_qkv.reshape(tokens, 3 * features)
    grad_in_norm, grad_gain_one, grad_shift_one = norm_backward(
        wide(x_own), gain_one, shift_one, dot_right(grad_qkv, qkv_weight)
    )
    input_grad = (grad_home + grad_in_norm)[None]
    column_sums = jnp.sum(wide(grad_qkv), axis=0)
    grad_qv_b = jnp.concatenate((column_sums[:features], column_sums[2 * features :]))

    qkv_w_share = lax.all_to_all(grad_qkv_w_own, "seq", 0, 1, tiled=True)
    qkv_w_share = (
        qkv_w_share.reshape(-1, count, 3, width).transpose(0, 2, 1, 3).reshape(-1, 3 * features)
    )
    shares = [
        lax.psum_scatter(low(term), "seq", scatter_dimension=0, tiled=True)
        for term in (grad_o_w, grad_cq_w, grad_ckv_w, grad_co_w, grad_fc1_w, grad_fc2_w)
    ]
    shares = lax.psum((qkv_w_share, *shares), "rows")
    qkv_w, o_w, cq_w, ckv_w, co_w, fc1_w, fc2_w = [wide(share) for share in shares]
    vectors = (
        grad_gain_one,
        grad_shift_one,
        grad_qv_b,
        grad_o_b,
        grad_gain_two,
        grad_shift_two,
        grad_cq_b,
        grad_cv_b,
        grad_co_b,
        grad_gain_three,
        grad_shift_three,
        grad_fc1_b,
        grad_fc2_b,
    )
    joined = lax.psum(
        jnp.concatenate([vector.reshape(count, -1) for vector in vectors], axis=1),
        ("rows", "seq"),
    )
    joined = lax.dynamic_index_in_dim(joined, me, 0, keepdims=False)
    pieces, offset = [], 0
    for vector in vectors:
        size = vector.shape[0] // count
        pieces.append(joined[offset : offset + size])
        offset += size
    g1, s1, qvb, ob, g2, s2, cqb, cvb, cob, g3, s3, f1b, f2b = pieces
    return (
        layer_out,
        input_grad,
        memory_grad,
        g1,
        s1,
        qkv_w,
        qvb,
        o_w,
        ob,
        g2,
        s2,
        cq_w,
        cqb,
        ckv_w,
        cvb,
        co_w,
        cob,
        g3,
        s3,
        fc1_w,
        f1b,
        fc2_w,
        f2b,
    )


def solution(mesh):
    split = P("rows", "seq", None)
    in_specs = (split, split, split, P("rows", None), P("rows", None)) + (P(),) * 20
    vector, matrix = P("seq"), P("seq", None)
    out_specs = (split, split, split) + (
        vector,
        vector,
        matrix,
        vector,
        matrix,
        vector,
        vector,
        vector,
        matrix,
        vector,
        matrix,
        vector,
        matrix,
        vector,
        vector,
        vector,
        matrix,
        vector,
        matrix,
        vector,
    )
    return jax.shard_map(body, mesh=mesh, in_specs=in_specs, out_specs=out_specs, check_vma=False)
```

time: 1880 us -> 1000 us (0.53)
  matrix products: 480 us -> 132 us
  local copies, waits for them, and re-layouts: 349 us -> 60.1 us
  Pallas kernels: 0 us -> 239 us
  blocking collectives: 227 us -> 0 us
  other arithmetic: 194 us -> 53.8 us
  starting transfers between devices: 157 us -> 18 us
  waiting for transfers between devices: 436 us -> 476 us
    dot_general x111 -> x8, matrix products: 410 us -> 51.9 us  [dot_plain(): return jnp.dot(first, second, preferred_element_type=jnp.float32)]
    psum x1 -> x4, waiting for transfers between devices: 38.2 us -> 300 us  [the longest x1 110 us: body(): shares = lax.psum((qkv_w_share, *shares), 'rows')]
    pallas_call x0 -> x8, Pallas kernels: none -> 239 us  [the longest x3 87.1 us: exchange(): pl.pallas_call(functools.partial(exchange_kernel, count, parts), out_shap...]
    unnamed x2 -> x0, blocking collectives: 217 us -> none
    ppermute x30 -> x0, starting transfers between devices: 152 us -> none  [the longest x16 108 us: from_behind(): return lax.ppermute(block, axis, route)]
    all_gather x3 -> x0, waiting for transfers between devices: 139 us -> none  [the longest x1 101 us: body(): lax.all_gather(mem_rows, 'seq', axis=0, tiled=True)]
    dynamic_slice x88 -> x3, local copies, waits for them, and re-layouts: 104 us -> 3.87 us  [the longest x1 1.85 us: body(): lax.dynamic_slice_in_dim(qkv_weight, part * features + me * width, width, 1)]
    convert_element_type x67 -> x19, other arithmetic: 94.2 us -> 11.5 us  [the longest x18 8 us: wide(): return values.astype(jnp.float32)]
  transfers between devices with their start and end apart: 43 -> 11, of which waited for: 10 -> 6; matrix products, arithmetic and copies ran while one was open for 19% -> 13% of each run, Pallas kernels for 0% -> 21%
where the time goes in v1:
time: 1000 us; the launch traced here: 996 us
  waiting for transfers between devices  476 us (48%)
  Pallas kernels  239 us (24%)
  matrix products  132 us (13%)
  local copies, waits for them, and re-layouts  60.1 us (6%)
  other arithmetic  53.8 us (5%)
  starting transfers between devices  18 us (2%)
  between operations  16.6 us (2%)
    reduce_scatter x5, waiting for transfers between devices, body(): lax.psum_scatter(low(term), 'seq', scatter_dimension=0, tiled=True)  163 us
    psum x1, waiting for transfers between devices, body(): shares = lax.psum((qkv_w_share, *shares), 'rows')  110 us
    psum x1, waiting for transfers between devices, body(): lax.psum(jnp.concatenate([vector.reshape(count, -1) for vector in vectors...  110 us
    pallas_call x3, Pallas kernels, exchange(): pl.pallas_call(functools.partial(exchange_kernel, count, parts), out_shap...  87.1 us
    psum x1, waiting for transfers between devices, body(): big_dk, big_dv = lax.psum((big_dk, big_dv), 'seq')  80.8 us
    pallas_call x1, Pallas kernels, gather_rows(): pl.pallas_call(functools.partial(gather_kernel, count), out_shape=jax.Sha...  70.6 us
    dot_general x8, matrix products, dot_plain(): return jnp.dot(first, second, preferred_element_type=jnp.float32)  51.9 us
    dot_general x7, matrix products, dot_left(): lax.dot_general(first, second, (((0,), (0,)), ((), ())), preferred_elemen...  42.4 us
  transfers between devices with their start and end apart: 11, of which 6 were waited for; matrix products, arithmetic and copies ran while one was open for 13% of the time, Pallas kernels for 21%

profile of v1, /device:TPU:0, one launch (start us, length us, event | category | flops | bytes accessed | tf_op | source)
XLA Modules:
  0.0 995.7 jit_solution(10267439789395187753)
XLA Ops:
  20.0 5.2 fusion.93
  26.5 70.6 %shard_map.416 = bf16[2048,1024]{1,0:T(8,128)(2,1)} custom-call(bf16[256,1024]{1,0:T(8,128)(2,1)} %bitcast.158), custom_call_target="tpu_custom_call" | custom-call | tf_op jit(solution)/shard_map/pallas_call | solution.py:169
  111.7 12.7 %shard_map.417 = (bf16[2048,128]{1,0:T(8,128)(2,1)}, f32[2048,2]{1,0:T(8,128)}) custom-call(bf16[2048,384]{1,0:T(8,128)(2,1)} %add_convert_fusion.3.qkv_ref, s32[2048,1]{1,0:T(8,128)} %copy.85.start_ref), custom_call_target="tpu_custom_call" | custom-call | tf_op jit(solution)/shard_map/pallas_call | solution.py:304
  125.8 22.0 %shard_map.418 = (bf16[8,256,128]{2,1,0:T(8,128)(2,1)}, bf16[8,256,128]{2,1,0:T(8,128)(2,1)}) custom-call(bf16[8,256,128]{2,1,0:T(8,128)(2,1)} %bitcast.170, bf16[256,128]{1,0:T(8,128)(2,1)} %pad_maximum_fusion.4.refs_1_), custom_call_target="tpu_custom_call" | custom-call | tf_op jit(solution)/shard_map/pallas_call | solution.py:229
  153.1 7.0 add_convert_fusion.1.own_key_ref.own_value_ref
  160.1 7.1 add_convert_fusion.2.key_ref.value_ref
  177.2 14.6 %shard_map.419 = (bf16[384,1024]{1,0:T(8,128)(2,1)}, f32[8,384,2]{2,1,0:T(8,128)}) custom-call(bf16[384,1024]{1,0:T(8,128)(2,1)} %add_convert_fusion.6.query_ref, bf16[640,2048]{1,0:T(8,128)(2,1)} %add_convert_fusion.2.key_ref.value_ref, bf16[640,2048]{1,0:T(8,128)(2,1)} %add_convert_fusion.2.key_ref.value_ref, ...), custom_call_target="tpu_custom_call" | custom-call | tf_op jit(solution)/shard_map/pallas_call | solution.py:414
  198.1 22.4 %multiply_convert_fusion = (bf16[384,4096]{1,0:T(8,128)(2,1)S(1)}, f32[384,4096]{1,0:T(8,128)}, f32[384,4096]{1,0:T(8,128)}) fusion(f32[4096]{0:T(1024)S(1)} %convert_element_type.194, bf16[1024,4096]{1,0:T(8,128)(2,1)} %param.46, f32[384,1024]{1,0:T(8,128)S(1)} %get-tuple-element.224, f32[1024]{0:T(1024)S(1)} %convert_element_type.192, ...), kind=kOutput, calls=%fused_computation.14 | convolution fusion | flops 3327000576 | bytes 25717760 | tf_op jit(solution)/shard_map/dot_general | solution.py:42
  224.9 11.9 %convert_reduce_fusion.1 = (f32[4096]{0:T(1024)S(1)}, bf16[384,4096]{1,0:T(8,128)(2,1)}) fusion(f32[384,4096]{1,0:T(8,128)} %get-tuple-element.176, f32[384,4096]{1,0:T(8,128)} %get-tuple-element.225, bf16[4096,1024]{1,0:T(8,128)(2,1)S(1)} %bitcast.190, bf16[128,1024]{1,0:T(8,128)(2,1)S(1)} %get-tuple-element.210, bf16[256,1024]{1,0:T(8,128)(2,1)S(1)} %bitcast.161, ...), kind=kOutput, calls=%fused_computation.12 | convolution fusion | flops 3248353280 | bytes 24920448 | tf_op jit(solution)/shard_map/dot_general | solution.py:52
  236.8 7.4 multiply_reduce_fusion
  248.6 18.8 %shard_map.420 = (bf16[384,1024]{1,0:T(8,128)(2,1)}, bf16[640,1024]{1,0:T(8,128)(2,1)}, bf16[640,1024]{1,0:T(8,128)(2,1)}, bf16[640,1024]{1,0:T(8,128)(2,1)}, bf16[640,1024]{1,0:T(8,128)(2,1)}) custom-call(bf16[384,1024]{1,0:T(8,128)(2,1)} %add_convert_fusion.6.query_ref, bf16[640,2048]{1,0:T(8,128)(2,1)} %add_convert_fusion.2.key_ref.value_ref, ...), custom_call_target="tpu_custom_call" | custom-call | tf_op jit(solution)/shard_map/pallas_call | solution.py:481
  273.8 80.8 %all-reduce.12.cloned.1.call-done = (bf16[640,1024]{1,0:T(8,128)(2,1)}, bf16[640,1024]{1,0:T(8,128)(2,1)}, bf16[128,1024]{1,0:T(8,128)(2,1)}, bf16[128,1024]{1,0:T(8,128)(2,1)}) async-done(((bf16[640,1024]{1,0:T(8,128)(2,1)}, bf16[640,1024]{1,0:T(8,128)(2,1)}, bf16[128,1024]{1,0:T(8,128)(2,1)}, bf16[128,1024]{1,0:T(8,128)(2,1)}), (bf16[640,1024]{1,0:T(8,128)(2,1)}, bf16[640,1024]{1,0:T(8,128)(2,1)}, ...) | async-done | bytes 3145744 | tf_op jit(solution)/shard_map/psum | solution.py:647
  359.3 5.0 convert_bitcast_fusion
  364.2 6.5 copy.101
  370.8 4.0 convolution_convert_fusion.2
  375.1 4.4 convolution_convert_fusion.3
  379.5 3.9 convolution_convert_fusion.4
  383.5 10.3 %convolution_convert_fusion.1 = bf16[1024,4096]{1,0:T(8,128)(2,1)} fusion(bf16[384,4096]{1,0:T(8,128)(2,1)} %get-tuple-element.230, f32[384,1024]{1,0:T(8,128)} %copy-done.4, f32[1024]{0:T(1024)S(1)} %convert_element_type.192, f32[1024]{0:T(1024)S(1)} %convert_element_type.191, f32[384]{0:T(512)S(1)} %fusion.42, f32[384]{0:T(512)S(1)} %broadcast_multiply_fusion.1), kind=kOutput, calls=%fused_computation.10 | convolution fusion | flops 3227385856 | bytes 13118464 | tf_op jit(solution)/shard_map/dot_general | solution.py:46
  394.4 8.8 convolution_convert_fusion
  405.6 5.8 fusion.40.start_ref
  420.3 23.6 %shard_map.421 = (bf16[8,256,128]{2,1,0:T(8,128)(2,1)}, bf16[8,128,128]{2,1,0:T(8,128)(2,1)}) custom-call(bf16[8,256,128]{2,1,0:T(8,128)(2,1)} %slice.275.refs_0_, bf16[8,128,128]{2,1,0:T(8,128)(2,1)} %slice.276.refs_1_), custom_call_target="tpu_custom_call" | custom-call | tf_op jit(solution)/shard_map/pallas_call | solution.py:229
  447.7 35.5 %shard_map.422 = bf16[2048,384]{1,0:T(8,128)(2,1)} custom-call(bf16[2048,384]{1,0:T(8,128)(2,1)} %add_convert_fusion.3.qkv_ref, bf16[2048,128]{1,0:T(8,128)(2,1)} %get-tuple-element.36.out_ref, bf16[2048,128]{1,0:T(8,128)(2,1)} %pad_maximum_fusion.1.grad_ref, s32[1,2048]{1,0:T(1,128)} %fusion.40.start_ref, f32[2,2048]{1,0:T(2,128)} %bitcast.185), custom_call_target="tpu_custom_call" | custom-call | tf_op jit(solution)/shard_map/pallas_call | solution.py:372
  483.2 41.4 %shard_map.423 = bf16[8,256,384]{2,1,0:T(8,128)(2,1)} custom-call(bf16[8,256,384]{2,1,0:T(8,128)(2,1)} %bitcast.160), custom_call_target="tpu_custom_call" | custom-call | tf_op jit(solution)/shard_map/pallas_call | solution.py:229
  527.3 5.9 convolution_convert_fusion.5
  533.2 16.8 %all-to-all-start = ((bf16[8,128,384]{2,1,0:T(8,128)(2,1)}), bf16[8,128,384]{2,1,0:T(8,128)(2,1)S(1)}, u32[]{:S(2)}, u32[]{:S(2)}) async-start(bf16[8,128,384]{2,1,0:T(8,128)(2,1)} %bitcast.176), calls=%async_computation | async-start | bytes 1572864 | tf_op jit(solution)/shard_map/all_to_all | solution.py:716
  553.7 5.4 fusion.52
  563.1 12.2 %all-to-all-done = bf16[8,128,384]{2,1,0:T(8,128)(2,1)S(1)} async-done(((bf16[8,128,384]{2,1,0:T(8,128)(2,1)}), bf16[8,128,384]{2,1,0:T(8,128)(2,1)S(1)}, u32[]{:S(2)}, u32[]{:S(2)}) %all-to-all-start) | async-done | bytes 786464 | tf_op jit(solution)/shard_map/all_to_all | solution.py:716
  578.8 71.4 %reduce-scatter.15.cloned.1.call-done = bf16[128,4096]{1,0:T(8,128)(2,1)} async-done(((bf16[1024,4096]{1,0:T(8,128)(2,1)}), bf16[128,4096]{1,0:T(8,128)(2,1)}) %reduce-scatter.15.cloned.1.call-update) | async-done | bytes 1048592 | tf_op jit(solution)/shard_map/reduce_scatter | solution.py:721
  650.3 91.8 %reduce-scatter.17.cloned.1.call-done = bf16[512,1024]{1,0:T(8,128)(2,1)} async-done(((bf16[4096,1024]{1,0:T(8,128)(2,1)}), bf16[512,1024]{1,0:T(8,128)(2,1)}) %reduce-scatter.17.cloned.1.call-update) | async-done | bytes 1048592 | tf_op jit(solution)/shard_map/reduce_scatter | solution.py:721
  742.7 5.3 fusion.15
  754.7 109.7 %all-reduce.10.cloned.1.call-done = f32[8,2176]{1,0:T(8,128)} async-done(((f32[8,2176]{1,0:T(8,128)}), f32[8,2176]{1,0:T(8,128)}) %all-reduce.10.cloned.1.call-update) | async-done | bytes 69648 | tf_op jit(solution)/shard_map/psum | solution.py:741
  868.5 109.9 %all-reduce.16.cloned.1.call-done = (bf16[128,2048]{0,1:T(8,128)(2,1)}, bf16[128,3072]{1,0:T(8,128)(2,1)}, bf16[128,1024]{1,0:T(8,128)(2,1)}, bf16[128,1024]{1,0...) async-done(((bf16[128,2048]{0,1:T(8,128)(2,1)}, bf16[128,3072]{1,0:T(8,128)(2,1)}, bf16[128,1024]{1,0:T(8,128)(2,1)}, ...) | async-done | bytes 4194320 | tf_op jit(solution)/shard_map/psum | solution.py:724
  (256 shorter events, 121.0 us)
Async XLA Ops:
  7.2 168.0 %copy-start = (bf16[1024,1024]{1,0:T(8,128)(2,1)S(1)}, bf16[1024,1024]{1,0:T(8,128)(2,1)}, u32[]{:S(2)}) copy-start(bf16[1024,1024]{1,0:T(8,128)(2,1)} %param.38) | copy-start | bytes 6291460
  7.2 152.9 %all-reduce.14.cloned.1.call-start = ((), (), s32[]{:S(2)}) async-start(), calls=%async_computation.15 | async-start | bytes 3670016 | tf_op jit(solution)/shard_map/psum | solution.py:569
  11.2 8.6 copy-start.37
  11.2 8.6 copy-start.38
  11.2 8.6 copy-start.39
  11.2 8.6 copy-start.40
  11.2 8.6 copy-start.41
  11.2 8.6 copy-start.42
  11.2 8.6 copy-start.43
  11.3 8.6 copy-start.44
  11.3 8.6 copy-start.45
  11.3 8.6 copy-start.46
  11.3 8.6 copy-start.36
  14.8 339.8 %all-reduce.12.cloned.1.call-start = ((), (), s32[]{:S(2)}) async-start(), calls=%async_computation.14 | async-start | bytes 6291456 | tf_op jit(solution)/shard_map/psum | solution.py:647
  19.7 83.0 %copy-start.34 = (f32[1024]{0:T(1024)}, f32[1024]{0:T(1024)S(1)}, u32[]{:S(2)}) copy-start(f32[1024]{0:T(1024)S(1)} %convert_element_type.176) | copy-start | bytes 12292
  125.8 27.3 %copy-start.47 = (bf16[1024]{0:T(1024)(128)(2,1)S(1)}, bf16[1024]{0:T(1024)(128)(2,1)}, u32[]{:S(2)}) copy-start(bf16[1024]{0:T(1024)(128)(2,1)} %param.41) | copy-start | bytes 6148
  160.1 7.1 copy-start.27
  194.3 26.2 %slice-start = ((s8[8388608]{0:T(1024)(128)(4,1)}), s8[4194304]{0:T(1024)(128)(4,1)S(1)}, s32[]{:S(2)}) async-start(s8[8388608]{0:T(1024)(128)(4,1)} %bitcast.189), calls=%async_computation.17 | async-start | bytes 8388608
  197.8 46.5 %copy-start.4 = (f32[384,1024]{1,0:T(8,128)}, f32[384,1024]{1,0:T(8,128)S(1)}, u32[]{:S(2)}) copy-start(f32[384,1024]{1,0:T(8,128)S(1)} %get-tuple-element.224) | copy-start | bytes 4718596
  198.1 22.4 %slice-start.1 = ((s8[8388608]{0:T(1024)(128)(4,1)}), s8[4194304]{0:T(1024)(128)(4,1)S(1)}, s32[]{:S(2)}) async-start(s8[8388608]{0:T(1024)(128)(4,1)} %bitcast.189), calls=%async_computation.18 | async-start | bytes 8388608
  224.0 12.8 %copy-start.20 = (bf16[384,1024]{1,0:T(8,128)(2,1)}, bf16[384,1024]{1,0:T(8,128)(2,1)S(1)}, u32[]{:S(2)}) copy-start(bf16[384,1024]{1,0:T(8,128)(2,1)S(1)} %add_convert_fusion.4) | copy-start | bytes 2359300
  248.6 18.8 %copy-start.6 = (f32[384,1024]{1,0:T(8,128)S(1)}, f32[384,1024]{1,0:T(8,128)}, u32[]{:S(2)}) copy-start(f32[384,1024]{1,0:T(8,128)} %copy-done.5) | copy-start | bytes 4718596
  273.7 303.0 %reduce-scatter.19.cloned.1.call-start = ((), (), s32[]{:S(2)}) async-start(), calls=%async_computation.13 | async-start | bytes 4718592
  370.8 208.1 %reduce-scatter.13.cloned.1.call-start = ((), (), s32[]{:S(2)}) async-start(), calls=%async_computation.10 | async-start | bytes 2359296 | tf_op jit(solution)/shard_map/reduce_scatter | solution.py:721
  374.8 204.0 %reduce-scatter.11.cloned.1.call-start = ((), (), s32[]{:S(2)}) async-start(), calls=%async_computation.9 | async-start | bytes 2359296 | tf_op jit(solution)/shard_map/reduce_scatter | solution.py:721
  379.5 199.4 %reduce-scatter.9.cloned.1.call-start = ((), (), s32[]{:S(2)}) async-start(), calls=%async_computation.8 | async-start | bytes 2359296 | tf_op jit(solution)/shard_map/reduce_scatter | solution.py:721
  383.5 266.8 %reduce-scatter.15.cloned.1.call-start = ((), (), s32[]{:S(2)}) async-start(), calls=%async_computation.11 | async-start | bytes 9437184 | tf_op jit(solution)/shard_map/reduce_scatter | solution.py:721
  393.9 348.1 %reduce-scatter.17.cloned.1.call-start = ((), (), s32[]{:S(2)}) async-start(), calls=%async_computation.12 | async-start | bytes 9437184 | tf_op jit(solution)/shard_map/reduce_scatter | solution.py:721
  403.2 8.3 copy-start.14
  533.2 42.1 %all-to-all-start = ((bf16[8,128,384]{2,1,0:T(8,128)(2,1)}), bf16[8,128,384]{2,1,0:T(8,128)(2,1)S(1)}, u32[]{:S(2)}, u32[]{:S(2)}) async-start(bf16[8,128,384]{2,1,0:T(8,128)(2,1)} %bitcast.176), calls=%async_computation | async-start | bytes 1572864 | tf_op jit(solution)/shard_map/all_to_all | solution.py:716
  550.0 314.4 %all-reduce.10.cloned.1.call-start = ((), (), s32[]{:S(2)}) async-start(), calls=%async_computation.7 | async-start | bytes 139264 | tf_op jit(solution)/shard_map/psum | solution.py:741
  563.1 415.3 %all-reduce.16.cloned.1.call-start = ((), (), s32[]{:S(2)}) async-start(), calls=%async_computation.16 | async-start | bytes 8388608 | tf_op jit(solution)/shard_map/psum | solution.py:724
  (31 other events, 117.7 us)
Sparse Core Ops, SparseCore 0:
  14.9 82.2 all-reduce.13
  273.9 80.6 all-reduce.11
  370.9 50.0 reduce-scatter.18
  423.7 39.0 reduce-scatter.12
  465.5 40.1 reduce-scatter.10
  508.4 45.4 reduce-scatter.8
  556.2 94.0 reduce-scatter.14
  652.6 89.4 reduce-scatter.16
  748.2 116.1 all-reduce.9
  869.9 108.4 all-reduce.15

commit v2 on v1

--- a/solution.py
+++ b/solution.py
@@ -182,59 +182,142 @@
     )(block_in)
 
 
-def exchange_kernel(count, parts, *refs):
-    ins, outs = refs[: len(parts)], refs[len(parts) : 2 * len(parts)]
-    own_sem, send_sem, recv_sem = refs[2 * len(parts) :]
-    me = lax.axis_index("seq")
+AXES = {"seq": 1, "chip": 1, "rows": 0}
+
+
+def peer(axis, step, counts):
+    row, me = lax.axis_index("rows"), lax.axis_index("seq")
+    if axis == "rows":
+        there = lax.rem(row + step, counts["rows"])
+        return (there, me), there
+    if axis == "seq":
+        there = lax.rem(me + step, counts["seq"])
+        return (row, there), there
+    there = lax.rem(me // 2 + step, counts["chip"])
+    return (row, there * 2 + me % 2), there
+
+
+def own_place(axis):
+    if axis == "rows":
+        return lax.axis_index("rows")
+    return lax.axis_index("seq") if axis == "seq" else lax.axis_index("seq") // 2
+
+
+def whole(ref, index):
+    return ref
+
+
+def lead(ref, index):
+    return ref.at[index]
+
+
+def second_dim(ref, index):
+    return ref.at[:, index]
+
+
+def rows_of(size, first=0, lanes=None):
+    def find(ref, index):
+        rows = pl.ds(pl.multiple_of(index * size, size), size)
+        return ref.at[rows] if lanes is None else ref.at[rows, first : first + lanes]
+
+    return find
+
+
+def columns_of(size, first=0):
+    def find(ref, index):
+        return ref.at[:, pl.ds(pl.multiple_of(first + index * size, size), size)]
+
+    return find
+
+
+def greet(axes, counts):
     barrier = pltpu.get_barrier_semaphore()
-    for step in range(1, count):
-        pl.semaphore_signal(
-            barrier, inc=1, device_id=place(lax.rem(me + step, count)), device_id_type=MESH
-        )
-    pl.semaphore_wait(barrier, count - 1)
-    own = []
-    for index, same in enumerate(parts):
-        source = ins[index] if same else ins[index].at[me]
-        own.append(pltpu.make_async_copy(source, outs[index].at[me], own_sem.at[index]))
-        own[-1].start()
-    copies = []
-    order = sorted(range(1, count), key=lambda step: -min(step, count - step))
-    for step in order:
-        target = lax.rem(me + step, count)
-        for index, same in enumerate(parts):
-            copies.append(
+    total = 0
+    for axis in axes:
+        for step in range(1, counts[axis]):
+            pl.semaphore_signal(
+                barrier, inc=1, device_id=peer(axis, step, counts)[0], device_id_type=MESH
+            )
+            total += 1
+    pl.semaphore_wait(barrier, total)
+
+
+def steps_of(total):
+    return sorted(range(1, total), key=lambda step: -min(step, total - step))
+
+
+class Transfers:
+    def __init__(self, part, counts, own_sem, send_sem, recv_sem):
+        from_ref, to_ref, axis, source, target = part
+        here = own_place(axis)
+        self.own = pltpu.make_async_copy(source(from_ref, here), target(to_ref, here), own_sem)
+        self.remote = []
+        for step in steps_of(counts[axis]):
+            device, there = peer(axis, step, counts)
+            self.remote.append(
                 pltpu.make_async_remote_copy(
-                    src_ref=ins[index] if same else ins[index].at[target],
-                    dst_ref=outs[index].at[me],
-                    send_sem=send_sem.at[index, step],
-                    recv_sem=recv_sem.at[index, step],
-                    device_id=place(target),
+                    src_ref=source(from_ref, there),
+                    dst_ref=target(to_ref, here),
+                    send_sem=send_sem.at[step],
+                    recv_sem=recv_sem.at[step],
+                    device_id=device,
                     device_id_type=MESH,
                 )
             )
-            copies[-1].start()
-    for copy in copies:
-        copy.wait()
-    for copy in own:
-        copy.wait()
-
-
-def exchange(arrays, parts, count, collective_id):
-    shapes = [
-        jax.ShapeDtypeStruct(
-            (count,) + (array.shape if same else array.shape[1:]), array.dtype
+
+    def start(self):
+        for copy in self.remote:
+            copy.start()
+        self.own.start()
+
+    def arrived(self):
+        self.own.wait()
+        for copy in self.remote:
+            copy.wait_recv()
+
+    def sent(self):
+        for copy in self.remote:
+            copy.wait_send()
+
+
+def axes_of(axes):
+    return tuple(axis for axis in ("seq", "rows") if axis in axes)
+
+
+def exchange_kernel(counts, ins_count, parts, *refs):
+    outs_count = len({part[1] for part in parts})
+    ins, outs = refs[:ins_count], refs[ins_count : ins_count + outs_count]
+    own_sem, send_sem, recv_sem = refs[ins_count + outs_count :]
+    greet(axes_of([part[2] for part in parts]), counts)
+    moves = [
+        Transfers(
+            (ins[part[0]], outs[part[1]]) + part[2:],
+            counts,
+            own_sem.at[index],
+            send_sem.at[index],
+            recv_sem.at[index],
         )
-        for array, same in zip(arrays, parts)
+        for index, part in enumerate(parts)
     ]
+    for move in moves:
+        move.start()
+    for move in moves:
+        move.arrived()
+    for move in moves:
+        move.sent()
+
+
+def exchange(arrays, shapes, parts, counts, collective_id):
+    longest = max(counts[part[2]] for part in parts)
     return pl.pallas_call(
-        functools.partial(exchange_kernel, count, parts),
+        functools.partial(exchange_kernel, counts, len(arrays), parts),
         out_shape=shapes,
         in_specs=[pl.BlockSpec(memory_space=pl.ANY)] * len(arrays),
-        out_specs=[pl.BlockSpec(memory_space=pl.ANY)] * len(arrays),
+        out_specs=[pl.BlockSpec(memory_space=pl.ANY)] * len(shapes),
         scratch_shapes=[
-            pltpu.SemaphoreType.DMA((len(arrays),)),
-            pltpu.SemaphoreType.DMA((len(arrays), count)),
-            pltpu.SemaphoreType.DMA((len(arrays), count)),
+            pltpu.SemaphoreType.DMA((len(parts),)),
+            pltpu.SemaphoreType.DMA((len(parts), longest)),
+            pltpu.SemaphoreType.DMA((len(parts), longest)),
         ],
         compiler_params=pltpu.CompilerParams(
             collective_id=collective_id, has_side_effects=True
@@ -242,6 +325,232 @@
     )(*arrays)
 
 
+def add_slots(ref):
+    return low(functools.reduce(jnp.add, [wide(ref[i]) for i in range(ref.shape[0])]))
+
+
+def finish_kernel(counts, shapes, *refs):
+    rows_done, rows_open, lanes_ok = shapes
+    done, opened = len(rows_done), len(rows_open)
+    refs = list(refs)
+
+    def take(number):
+        found = refs[:number]
+        del refs[:number]
+        return found
+
+    dqkv_ref, own_ref = take(2)
+    done_in, open_in = take(done), take(opened)
+    tokens_ref, own_out = take(2)
+    done_out, open_out = take(done), take(opened)
+    own_slots, own_sum, own_block = take(3)
+    open_slots, open_sum = take(opened), take(opened)
+    chip_slots, chip_sum = take(done + opened), take(done + opened)
+    sems = take(3)
+    greet(("seq", "rows"), counts)
+    number = 0
+
+    def move(*part):
+        nonlocal number
+        found = Transfers(part, counts, *(sem.at[number] for sem in sems))
+        number += 1
+        return found
+
+    count = counts["seq"]
+    width = dqkv_ref.shape[1] // 3
+    tokens = dqkv_ref.shape[0] // count
+    if lanes_ok:
+        home = [
+            move(
+                dqkv_ref,
+                tokens_ref,
+                "seq",
+                rows_of(tokens, part * width, width),
+                columns_of(width, part * width * count),
+            )
+            for part in range(3)
+        ]
+    else:
+        home = [move(dqkv_ref, tokens_ref, "seq", rows_of(tokens), lead)]
+    over_rows = [
+        move(ref, slots, "rows", columns_of(slots.shape[2]), lead)
+        for ref, slots in zip(open_in, open_slots)
+    ]
+    own_rows = move(own_ref, own_slots, "rows", second_dim, lead)
+    done_chips = [
+        move(ref, slots, "chip", rows_of(slots.shape[1]), lead)
+        for ref, slots in zip(done_in, chip_slots[:done])
+    ]
+    for item in home + over_rows + [own_rows] + done_chips:
+        item.start()
+    open_chips = []
+    for item, slots, total, place_ref in zip(over_rows, open_slots, open_sum, chip_slots[done:]):
+        item.arrived()
+        total[...] = add_slots(slots)
+        open_chips.append(move(total, place_ref, "chip", rows_of(place_ref.shape[1]), lead))
+        open_chips[-1].start()
+    own_rows.arrived()
+    own_sum[...] = add_slots(own_slots)
+    if lanes_ok:
+        own_chips = [
+            move(
+                own_sum.at[:, :, part * width : (part + 1) * width],
+                own_block,
+                "seq",
+                lead,
+                columns_of(width, part * width * count),
+            )
+            for part in range(3)
+        ]
+    else:
+        own_chips = [move(own_sum, own_block, "seq", lead, lead)]
+    for item in own_chips:
+        item.start()
+    last = []
+    for item, slots, total, out in zip(
+        done_chips + open_chips, chip_slots, chip_sum, done_out + open_out
+    ):
+        item.arrived()
+        total[...] = add_slots(slots)
+        last.append(move(total, out, "rows", whole, columns_of(total.shape[1])))
+        last[-1].start()
+    for item in own_chips:
+        item.arrived()
+    if lanes_ok:
+        last.append(move(own_block, own_out, "rows", whole, rows_of(own_block.shape[0])))
+    else:
+        last.append(move(own_block, own_out, "rows", whole, lead))
+    last[-1].start()
+    for item in home + last:
+        item.arrived()
+    for item in home + over_rows + [own_rows] + done_chips + open_chips + own_chips + last:
+        item.sent()
+
+
+def finish(dqkv, own_grad, rows_done, rows_open, counts, collective_id):
+    count, chips, rows = counts["seq"], counts["chip"], counts["rows"]
+    length, all_width = dqkv.shape
+    width = all_width // 3
+    lanes_ok = width % 128 == 0
+    tokens, short = length // count, own_grad.shape[2]
+    bf = jnp.bfloat16
+    if lanes_ok:
+        tokens_shape = (tokens, all_width * count)
+        own_block, own_out = (short, all_width * count), (rows * short, all_width * count)
+    else:
+        tokens_shape = (count, tokens, all_width)
+        own_block, own_out = (count, short, all_width), (rows, count, short, all_width)
+    shares = [term.shape for term in rows_done]
+    shares += [(term.shape[0], term.shape[1] // rows) for term in rows_open]
+    blocks = [(shape[0] // chips, shape[1]) for shape in shares]
+    outs = [tokens_shape, own_out] + [(shape[0], shape[1] * rows) for shape in blocks]
+    open_shares = shares[len(rows_done) :]
+    scratch = [(rows,) + own_grad.shape[:1] + own_grad.shape[2:]]
+    scratch += [own_grad.shape[:1] + own_grad.shape[2:], own_block]
+    scratch += [(rows,) + shape for shape in open_shares] + open_shares
+    scratch += [(chips,) + shape for shape in blocks] + blocks
+    moves = 3 + 3 + 2 + len(rows_open) + 2 * len(shares)
+    longest = max(count, rows)
+    arrays = [dqkv, own_grad, *rows_done, *rows_open]
+    return pl.pallas_call(
+        functools.partial(
+            finish_kernel,
+            counts,
+            (
+                tuple(term.shape for term in rows_done),
+                tuple(term.shape for term in rows_open),
+                lanes_ok,
+            ),
+        ),
+        out_shape=[jax.ShapeDtypeStruct(shape, bf) for shape in outs],
+        in_specs=[pl.BlockSpec(memory_space=pl.ANY)] * len(arrays),
+        out_specs=[pl.BlockSpec(memory_space=pl.ANY)] * len(outs),
+        scratch_shapes=[pltpu.VMEM(shape, bf) for shape in scratch]
+        + [
+            pltpu.SemaphoreType.DMA((moves,)),
+            pltpu.SemaphoreType.DMA((moves, longest)),
+            pltpu.SemaphoreType.DMA((moves, longest)),
+        ],
+        compiler_params=pltpu.CompilerParams(
+            collective_id=collective_id, has_side_effects=True, vmem_limit_bytes=VMEM_LIMIT
+        ),
+    )(*arrays)
+
+
+def vectors_kernel(counts, given_ref, out_ref, slots, total, own_sem, send_sem, recv_sem):
+    greet(("seq", "rows"), counts)
+    over_seq = Transfers(
+        (given_ref, slots, "seq", lead, lead), counts, own_sem.at[0], send_sem.at[0], recv_sem.at[0]
+    )
+    over_seq.start()
+    over_seq.arrived()
+    total[...] = functools.reduce(jnp.add, [slots[i] for i in range(slots.shape[0])])
+    over_rows = Transfers(
+        (total, out_ref, "rows", whole, lead), counts, own_sem.at[1], send_sem.at[1], recv_sem.at[1]
+    )
+    over_rows.start()
+    over_rows.arrived()
+    over_seq.sent()
+    over_rows.sent()
+
+
+def sum_vectors(given, counts, collective_id):
+    longest = max(counts["seq"], counts["rows"])
+    block = given.shape[1:]
+    return pl.pallas_call(
+        functools.partial(vectors_kernel, counts),
+        out_shape=jax.ShapeDtypeStruct((counts["rows"],) + block, jnp.float32),
+        in_specs=[pl.BlockSpec(memory_space=pl.ANY)],
+        out_specs=pl.BlockSpec(memory_space=pl.ANY),
+        scratch_shapes=[
+            pltpu.VMEM((counts["seq"],) + block, jnp.float32),
+            pltpu.VMEM(block, jnp.float32),
+            pltpu.SemaphoreType.DMA((2,)),
+            pltpu.SemaphoreType.DMA((2, longest)),
+            pltpu.SemaphoreType.DMA((2, longest)),
+        ],
+        compiler_params=pltpu.CompilerParams(collective_id=collective_id, has_side_effects=True),
+    )(given)
+
+
+def weight_grad_kernel(which_ref, first_ref, second_ref, *refs):
+    grad = dot_left(first_ref[...], second_ref[...])
+    if len(refs) == 2:
+        grad = grad + wide(refs[0][...])
+    refs[-1][...] = low(grad)
+
+
+def weight_grad(first, second, which, chips, given=None):
+    tokens, depth = first.shape
+    block, columns = depth // (2 * chips), second.shape[1]
+    tile = min(columns, 1024)
+    out = pl.BlockSpec((block, tile), lambda n, z, which: (z, n))
+    specs = [
+        pl.BlockSpec((tokens, block), lambda n, z, which: (0, 2 * z + which[0])),
+        pl.BlockSpec((tokens, tile), lambda n, z, which: (0, n)),
+    ]
+    arrays = [first, second]
+    if given is not None:
+        specs.append(out)
+        arrays.append(given)
+    return pl.pallas_call(
+        weight_grad_kernel,
+        grid_spec=pltpu.PrefetchScalarGridSpec(
+            num_scalar_prefetch=1,
+            grid=(columns // tile, chips),
+            in_specs=specs,
+            out_specs=out,
+        ),
+        out_shape=jax.ShapeDtypeStruct((chips * block, columns), jnp.bfloat16),
+        compiler_params=pltpu.CompilerParams(vmem_limit_bytes=VMEM_LIMIT),
+        cost_estimate=pl.CostEstimate(
+            flops=tokens * depth * columns,
+            bytes_accessed=2 * (tokens * (depth + columns) + depth * columns),
+            transcendentals=0,
+        ),
+    )(which, *arrays)
+
+
 def head_lanes(width):
     return lax.broadcasted_iota(jnp.int32, (1, width), 1) // DEPTH
 
@@ -250,6 +559,10 @@
     if width == DEPTH:
         return values
     return jnp.where(head_lanes(width) == head, values, jnp.zeros_like(values))
+
+
+def as_row(column):
+    return jnp.broadcast_to(column, (column.shape[0], 8)).T[:1]
 
 
 def self_forward_kernel(qkv_ref, start_ref, out_ref, stat_ref):
@@ -260,7 +573,7 @@
         rows = pl.ds(index * BLOCK, BLOCK)
         keys_end = (index + 1) * BLOCK
         query = qkv_ref[rows, 0:width]
-        begin = start_ref[rows, :]
+        begin = jnp.broadcast_to(start_ref[:, rows], (8, BLOCK)).T[:, :1]
         position = index * BLOCK + lax.broadcasted_iota(jnp.int32, (BLOCK, 1), 0)
         if index == blocks - 1 or index <= 1:
             cuts = [(0, keys_end)]
@@ -295,7 +608,8 @@
         for head in range(1, heads):
             merged = jnp.where(head_lanes(width) == head, outs[head], merged)
         out_ref[rows, :] = low(merged)
-        stat_ref[rows, :] = jnp.concatenate(stats, axis=1)
+        for head in range(heads):
+            stat_ref[head : head + 1, rows] = as_row(stats[head])
 
 
 def self_forward(qkv, begins):
@@ -305,12 +619,12 @@
         self_forward_kernel,
         out_shape=(
             jax.ShapeDtypeStruct((length, width), jnp.bfloat16),
-            jax.ShapeDtypeStruct((length, heads), jnp.float32),
+            jax.ShapeDtypeStruct((heads, length), jnp.float32),
         ),
         in_specs=[pl.BlockSpec(memory_space=pltpu.VMEM)] * 2,
         out_specs=[pl.BlockSpec(memory_space=pltpu.VMEM)] * 2,
         compiler_params=pltpu.CompilerParams(vmem_limit_bytes=VMEM_LIMIT),
-    )(qkv, begins[:, None])
+    )(qkv, begins[None, :])
 
 
 def self_backward_kernel(qkv_ref, out_ref, grad_ref, start_ref, stat_ref, dqkv_ref, dk_ref, dv_ref):
@@ -376,7 +690,7 @@
         out_specs=pl.BlockSpec(memory_space=pltpu.VMEM),
         scratch_shapes=[pltpu.VMEM((length, width), jnp.float32)] * 2,
         compiler_params=pltpu.CompilerParams(vmem_limit_bytes=VMEM_LIMIT),
-    )(qkv, out, grad, begins[None, :], stats.T)
+    )(qkv, out, grad, begins[None, :], stats)
 
 
 def cross_forward_kernel(query_ref, key_ref, value_ref, own_key_ref, own_value_ref, out_ref, stat_ref):
@@ -397,7 +711,7 @@
             weight = jnp.exp(scores - top)
             total = jnp.sum(weight, axis=-1, keepdims=True)
             outs.append(dot_plain(low(weight), values[...]) / total)
-            stat_ref[0, begin : begin + size, head : head + 1] = top + jnp.log(total)
+            stat_ref[0, head : head + 1, begin : begin + size] = as_row(top + jnp.log(total))
         merged = outs[0]
         for head in range(1, len(outs)):
             merged = jnp.where(head_lanes(width) == head, outs[head], merged)
@@ -416,10 +730,10 @@
         grid=(steps,),
         out_shape=(
             jax.ShapeDtypeStruct((rows, features), jnp.bfloat16),
-            jax.ShapeDtypeStruct((steps, rows, 2), jnp.float32),
+            jax.ShapeDtypeStruct((steps, 2, rows), jnp.float32),
         ),
         in_specs=[tall, keys, values, keys, values],
-        out_specs=[tall, pl.BlockSpec((1, rows, 2), lambda i: (i, 0, 0))],
+        out_specs=[tall, pl.BlockSpec((1, 2, rows), lambda i: (i, 0, 0))],
         compiler_params=pltpu.CompilerParams(vmem_limit_bytes=VMEM_LIMIT),
     )(query, kv_big, kv_big, kv_own, kv_own)
 
@@ -494,7 +808,7 @@
         ],
         out_specs=[tall, keys, keys, keys, keys],
         compiler_params=pltpu.CompilerParams(vmem_limit_bytes=VMEM_LIMIT),
-    )(query, kv_big, kv_big, kv_own, kv_own, out, grad, stats.transpose(0, 2, 1))
+    )(query, kv_big, kv_big, kv_own, kv_own, out, grad, stats)
 
 
 def body(
@@ -529,6 +843,34 @@
     me = lax.axis_index("seq")
     length = tokens * count
     width = features // count
+    rows_count = lax.axis_size("rows")
+    counts = {"seq": count, "chip": count // 2, "rows": rows_count}
+    core = me % 2
+
+    def pair_sum(first, second):
+        this = core.astype(jnp.int32)[None]
+        if first.shape[1] // count % 128:
+            wider = jnp.pad(
+                first.reshape(-1, count, first.shape[1] // count),
+                ((0, 0), (0, 0), (0, 128 - first.shape[1] // count)),
+            ).reshape(first.shape[0], -1)
+            theirs, mine = (weight_grad(wider, second, w, count // 2) for w in (1 - this, this))
+            theirs, mine = (
+                term.reshape(count // 2, 128, -1)[:, : first.shape[1] // count].reshape(
+                    first.shape[1] // 2, -1
+                )
+                for term in (theirs, mine)
+            )
+            return low(wide(mine) + wide(swap(theirs)))
+        theirs = weight_grad(first, second, 1 - this, count // 2)
+        return weight_grad(first, second, this, count // 2, swap(theirs))
+
+    def swap(value):
+        return lax.ppermute(value, "seq", [(i, i ^ 1) for i in range(count)])
+
+    def after(value, other):
+        return lax.optimization_barrier((value, other))[0]
+
     mem_rows = memory.shape[1]
     sharers = PAGE_TOK // mem_rows
     row_segs = segment_ids[0]
@@ -563,15 +905,23 @@
         mem_page = lax.all_gather(mem_own, "seq", axis=0, tiled=True, axis_index_groups=groups)
     mem_page = jnp.pad(mem_page, ((0, PAGE_PAD - PAGE_TOK), (0, 0)))
     gives_big = (own_page == big_page) & (me % sharers == 0)
-    ends_grad = jnp.where(
-        is_first, out_grad[0, :SLOTS], jnp.zeros((SLOTS, features), jnp.bfloat16)
-    ), jnp.where(is_last, out_grad[0, tokens - SLOTS :], jnp.zeros((SLOTS, features), jnp.bfloat16))
-    mem_big, front_grad, back_grad = lax.psum(
-        (jnp.where(gives_big, mem_page, jnp.zeros_like(mem_page)), *ends_grad), "seq"
-    )
 
     x_own = inputs[0]
     x_all = gather_rows(x_own, count, 0)
+
+    half = PAGE_PAD // 2
+    masked_page = jnp.where(gives_big, mem_page, jnp.zeros_like(mem_page)).reshape(2, half, -1)
+    pair_page = masked_page[core] + swap(masked_page[1 - core])
+    at_end = jnp.where(core == 0, is_first, is_last)
+    end_grad = jnp.where(core == 0, out_grad[0, :SLOTS], out_grad[0, tokens - SLOTS :])
+    sent = jnp.concatenate((pair_page, jnp.where(at_end, end_grad, jnp.zeros_like(end_grad))))
+    same_core = [[2 * chip + which for chip in range(count // 2)] for which in range(2)]
+    mine = lax.psum(after(sent, x_all), "seq", axis_index_groups=same_core)
+    theirs = swap(mine)
+    zeroth, first = jnp.where(core == 0, mine, theirs), jnp.where(core == 0, theirs, mine)
+    mem_big = jnp.concatenate((zeroth[:half], first[:half]))
+    front_grad, back_grad = zeroth[half:], first[half:]
+
     qkv_own_weight = jnp.concatenate(
         [
             lax.dynamic_slice_in_dim(qkv_weight, part * features + me * width, width, 1)
@@ -589,24 +939,40 @@
     normed_all = low(norm_forward(wide(x_all), gain_one, shift_one))
     qkv = low(dot_plain(normed_all, qkv_own_weight) + wide(qkv_own_bias))
     mixed, mixed_stats = self_forward(qkv, begins)
-    blocks_mixed, ends_mixed = exchange(
-        (
-            mixed.reshape(count, tokens, width),
-            jnp.concatenate((mixed[:SLOTS], mixed[length - SLOTS :])),
-        ),
-        (False, True),
-        count,
-        1,
-    )
-
-    def beside(blocks):
-        return blocks.transpose(1, 0, 2).reshape(blocks.shape[1], -1)
-
+    bf = jnp.bfloat16
+    lanes_ok = width % 128 == 0
+    ends = jnp.concatenate((mixed[:SLOTS], mixed[length - SLOTS :]))
+    if lanes_ok:
+        blocks_mixed, ends_mixed = exchange(
+            (mixed, ends),
+            (
+                jax.ShapeDtypeStruct((tokens, features), bf),
+                jax.ShapeDtypeStruct((2 * SLOTS, features), bf),
+            ),
+            (
+                (1, 1, "seq", whole, columns_of(width)),
+                (0, 0, "seq", rows_of(tokens), columns_of(width)),
+            ),
+            counts,
+            1,
+        )
+    else:
+        blocks_mixed, ends_mixed = exchange(
+            (mixed, ends),
+            (
+                jax.ShapeDtypeStruct((count, tokens, width), bf),
+                jax.ShapeDtypeStruct((count, 2 * SLOTS, width), bf),
+            ),
+            ((1, 1, "seq", whole, lead), (0, 0, "seq", rows_of(tokens), lead)),
+            counts,
+            1,
+        )
+        blocks_mixed, ends_mixed = (
+            blocks.transpose(1, 0, 2).reshape(blocks.shape[1], -1)
+            for blocks in (blocks_mixed, ends_mixed)
+        )
     attended = jnp.concatenate(
-        (
-            beside(blocks_mixed),
-            slots_of(beside(ends_mixed[:, :SLOTS]), beside(ends_mixed[:, SLOTS:])),
-        )
+        (blocks_mixed, slots_of(ends_mixed[:SLOTS], ends_mixed[SLOTS:]))
     )
     resid = wide(
         jnp.concatenate((x_own, slots_of(x_all[:SLOTS], x_all[length - SLOTS :])))
@@ -629,51 +995,63 @@
     grad_act = dot_right(grad_out, fc2_weight)
     _, gelu_pull = jax.vjp(gelu_exact, pre_act)
     grad_pre = low(gelu_pull(grad_act)[0])
-    grad_fc2_w = dot_left(hidden_act, grad_out)
+    grad_fc2_w = pair_sum(hidden_act, grad_out)
+    fc2_share = lax.psum_scatter(grad_fc2_w, "rows", scatter_dimension=1, tiled=True)
     grad_fc2_b = jnp.sum(wide(grad_out), axis=0)
-    grad_fc1_w = dot_left(normed_three, grad_pre)
+    grad_fc1_w = pair_sum(normed_three, grad_pre)
+    fc1_share = lax.psum_scatter(grad_fc1_w, "rows", scatter_dimension=1, tiled=True)
     grad_fc1_b = jnp.sum(wide(grad_pre), axis=0)
     grad_two_norm, grad_gain_three, grad_shift_three = norm_backward(
         resid_two, gain_three, shift_three, dot_right(grad_pre, fc1_weight)
     )
     grad_resid_two = wide(grad_out) + grad_two_norm
     grad_branch_two = low(grad_resid_two)
-    grad_co_w = dot_left(cross_low, grad_branch_two)
+    grad_co_w = pair_sum(cross_low, grad_branch_two)
     grad_co_b = jnp.sum(wide(grad_branch_two), axis=0)
     grad_cross_low = low(dot_right(grad_branch_two, cross_out_weight))
     grad_cross_q, big_dk, big_dv, own_dk, own_dv = cross_backward(
         cross_queries, kv_big, kv_own, cross_low, grad_cross_low, cross_stats
     )
-    big_dk, big_dv = lax.psum((big_dk, big_dv), "seq")
-    grad_ckv = jnp.where(
-        gives_big,
-        jnp.concatenate((big_dk, big_dv), axis=1),
-        jnp.concatenate((own_dk, own_dv), axis=1),
-    )[:PAGE_TOK]
-    if sharers > 1:
-        grad_ckv = lax.psum_scatter(
-            grad_ckv, "seq", scatter_dimension=0, tiled=True, axis_index_groups=groups
-        )
-    grad_ckv_w = dot_left(mem_own, grad_ckv)
-    grad_cv_b = jnp.sum(wide(grad_ckv[:, features:]), axis=0)
-    memory_grad = dot_right(grad_ckv, cross_kv_weight)[None]
-
-    grad_cq_w = dot_left(normed_two, grad_cross_q)
+    grad_cq_w = pair_sum(normed_two, grad_cross_q)
     grad_cq_b = jnp.sum(wide(grad_cross_q), axis=0)
     grad_one_norm, grad_gain_two, grad_shift_two = norm_backward(
         resid_one, gain_two, shift_two, dot_right(grad_cross_q, cross_q_weight)
     )
     grad_resid_one = grad_resid_two + grad_one_norm
     grad_branch_one = low(grad_resid_one)
-    grad_o_w = dot_left(attended, grad_branch_one)
+    grad_o_w = pair_sum(attended, grad_branch_one)
     grad_o_b = jnp.sum(wide(grad_branch_one), axis=0)
     grad_attended = low(dot_right(grad_branch_one, self_out_weight))
-    by_device = grad_attended.reshape(-1, count, width).transpose(1, 0, 2)
-    blocks_grad, slots_grad = exchange(
-        (by_device[:, :tokens], by_device[:, tokens:]), (False, False), count, 2
+    if lanes_ok:
+        given, home_part, slot_part = (grad_attended,), (0, 0), (0, 1)
+
+        def piece(first, size):
+            def find(ref, index):
+                return ref.at[
+                    first : first + size, pl.ds(pl.multiple_of(index * width, width), width)
+                ]
+
+            return find
+
+        pieces = piece(0, tokens), piece(tokens, SLOTS)
+    else:
+        by_device = grad_attended.reshape(-1, count, width).transpose(1, 0, 2)
+        given, home_part, slot_part = (by_device[:, :tokens], by_device[:, tokens:]), (0, 0), (1, 1)
+        pieces = lead, lead
+    grad_mixed, slots_grad = exchange(
+        given,
+        (
+            jax.ShapeDtypeStruct((length, width), bf),
+            jax.ShapeDtypeStruct((count, SLOTS, width), bf),
+        ),
+        (
+            home_part + ("seq", pieces[0], rows_of(tokens)),
+            slot_part + ("seq", pieces[1], lead),
+        ),
+        counts,
+        2,
     )
     slots_grad = low(jnp.sum(wide(slots_grad), axis=0))
-    grad_mixed = blocks_grad.reshape(length, width)
     no_slots = jnp.zeros_like(slots_grad)
     grad_mixed = jnp.concatenate(
         (
@@ -684,45 +1062,77 @@
     )
     dqkv = self_backward(qkv, mixed, grad_mixed, begins, mixed_stats)
 
-    slot_results = lax.psum(
-        (
-            jnp.where(active[tokens:], final[tokens:], jnp.zeros_like(final[tokens:])),
-            low(grad_resid_one[tokens:]),
-        ),
-        "seq",
-    )
-
-    def at_home(own, returned, keep):
+    slot_final = jnp.where(active[tokens:], final[tokens:], jnp.zeros_like(final[tokens:]))
+    own_half = jnp.where(core == 0, big_dk, big_dv)
+    own_half = own_half + swap(jnp.where(core == 0, big_dv, big_dk))
+    slot_half = jnp.where(core == 0, slot_final, low(grad_resid_one[tokens:]))
+    slot_half = slot_half + swap(jnp.where(core == 0, low(grad_resid_one[tokens:]), slot_final))
+    mine = lax.psum(
+        jnp.concatenate((own_half[:PAGE_TOK], slot_half)), "seq", axis_index_groups=same_core
+    )
+    mine = after(mine, dqkv)
+    theirs = swap(mine)
+    zeroth, first = jnp.where(core == 0, mine, theirs), jnp.where(core == 0, theirs, mine)
+    big_dk, big_dv = zeroth[:PAGE_TOK], first[:PAGE_TOK]
+    slot_final, slot_grad = zeroth[PAGE_TOK:], first[PAGE_TOK:]
+    grad_ckv = jnp.where(
+        gives_big,
+        jnp.concatenate((big_dk, big_dv), axis=1),
+        jnp.concatenate((own_dk[:PAGE_TOK], own_dv[:PAGE_TOK]), axis=1),
+    )
+    if sharers > 1:
+        grad_ckv = lax.psum_scatter(
+            grad_ckv, "seq", scatter_dimension=0, tiled=True, axis_index_groups=groups
+        )
+    grad_ckv_w = pair_sum(mem_own, grad_ckv)
+    grad_cv_b = jnp.sum(wide(grad_ckv[:, features:]), axis=0)
+    memory_grad = dot_right(grad_ckv, cross_kv_weight)[None]
+
+    def at_home(own, returned):
         front = is_first & in_front
         back = is_last & ~in_front
         head = jnp.where(front, returned.astype(own.dtype), own[:SLOTS])
         tail = jnp.where(back, returned.astype(own.dtype), own[tokens - SLOTS :])
         return jnp.concatenate((head, own[SLOTS : tokens - SLOTS], tail))
 
-    layer_out = at_home(final[:tokens], slot_results[0], False)[None]
-    grad_home = at_home(grad_resid_one[:tokens], slot_results[1], False)
-
-    grad_qkv_w_own = low(dot_left(normed_all, dqkv))
-    (blocks_dqkv,) = exchange((dqkv.reshape(count, tokens, 3 * width),), (False,), count, 3)
-    grad_qkv = blocks_dqkv.reshape(count, tokens, 3, width).transpose(1, 2, 0, 3)
-    grad_qkv = grad_qkv.reshape(tokens, 3 * features)
+    layer_out = at_home(final[:tokens], slot_final)[None]
+    grad_home = at_home(grad_resid_one[:tokens], slot_grad)
+
+    grad_qkv_w = low(dot_left(normed_all, dqkv))
+    grad_qkv_w = grad_qkv_w.reshape(count, rows_count, -1, 3 * width)
+    column_sums = jnp.sum(wide(dqkv), axis=0)
+
+    def in_features(part):
+        return lax.dynamic_update_slice_in_dim(
+            jnp.zeros((features,), jnp.float32),
+            column_sums[part * width : (part + 1) * width],
+            me * width,
+            0,
+        )
+
+    grad_qv_b = jnp.concatenate((in_features(0), in_features(2)))
+
+    grad_qkv, qkv_w, fc1_w, fc2_w, o_w, cq_w, co_w, ckv_w = finish(
+        dqkv,
+        grad_qkv_w,
+        (fc1_share, fc2_share),
+        (grad_o_w, grad_cq_w, grad_co_w, grad_ckv_w),
+        counts,
+        3,
+    )
+    if not lanes_ok:
+        grad_qkv = grad_qkv.reshape(count, tokens, 3, width).transpose(1, 2, 0, 3)
+        grad_qkv = grad_qkv.reshape(tokens, 3 * features)
+        qkv_w = qkv_w.reshape(rows_count, count, -1, 3, width).transpose(0, 2, 3, 1, 4)
+        qkv_w = qkv_w.reshape(-1, 3 * features)
+    qkv_w, fc1_w, fc2_w, o_w, cq_w, co_w, ckv_w = [
+        wide(term) for term in (qkv_w, fc1_w, fc2_w, o_w, cq_w, co_w, ckv_w)
+    ]
     grad_in_norm, grad_gain_one, grad_shift_one = norm_backward(
         wide(x_own), gain_one, shift_one, dot_right(grad_qkv, qkv_weight)
     )
     input_grad = (grad_home + grad_in_norm)[None]
-    column_sums = jnp.sum(wide(grad_qkv), axis=0)
-    grad_qv_b = jnp.concatenate((column_sums[:features], column_sums[2 * features :]))
-
-    qkv_w_share = lax.all_to_all(grad_qkv_w_own, "seq", 0, 1, tiled=True)
-    qkv_w_share = (
-        qkv_w_share.reshape(-1, count, 3, width).transpose(0, 2, 1, 3).reshape(-1, 3 * features)
-    )
-    shares = [
-        lax.psum_scatter(low(term), "seq", scatter_dimension=0, tiled=True)
-        for term in (grad_o_w, grad_cq_w, grad_ckv_w, grad_co_w, grad_fc1_w, grad_fc2_w)
-    ]
-    shares = lax.psum((qkv_w_share, *shares), "rows")
-    qkv_w, o_w, cq_w, ckv_w, co_w, fc1_w, fc2_w = [wide(share) for share in shares]
+
     vectors = (
         grad_gain_one,
         grad_shift_one,
@@ -738,11 +1148,9 @@
         grad_fc1_b,
         grad_fc2_b,
     )
-    joined = lax.psum(
-        jnp.concatenate([vector.reshape(count, -1) for vector in vectors], axis=1),
-        ("rows", "seq"),
-    )
-    joined = lax.dynamic_index_in_dim(joined, me, 0, keepdims=False)
+    joined = jnp.concatenate([vector.reshape(count, -1) for vector in vectors], axis=1)
+    joined = jnp.pad(joined, ((0, 0), (0, -joined.shape[1] % 1024))).reshape(count, 8, -1)
+    joined = jnp.sum(sum_vectors(joined, counts, 4), axis=0).reshape(-1)
     pieces, offset = [], 0
     for vector in vectors:
         size = vector.shape[0] // count

time: 1000 us -> 659 us (0.66)
  waiting for transfers between devices: 476 us -> 16.4 us
  Pallas kernels: 239 us -> 432 us
  matrix products: 132 us -> 87.3 us
  local copies, waits for them, and re-layouts: 60.1 us -> 27 us
  starting transfers between devices: 18 us -> 3.36 us
  other arithmetic: 53.8 us -> 68.3 us
    psum x4 -> x2, waiting for transfers between devices: 300 us -> 1.98 us  [the longest x1 1.98 us: body(): mine = lax.psum(after(sent, x_all), 'seq', axis_index_groups=same_core)]
    pallas_call x3 -> x16, Pallas kernels: 87.1 us -> 306 us  [the longest x1 134 us: finish(): pl.pallas_call(functools.partial(finish_kernel, counts, (tuple((term.shap...]
    reduce_scatter x5 -> x2, waiting for transfers between devices: 163 us -> 5.66 us  [the longest x1 5.65 us: body(): lax.psum_scatter(grad_fc2_w, 'rows', scatter_dimension=1, tiled=True)]
    dot_general x7 -> x1, matrix products: 42.4 us -> 5.44 us  [dot_left(): lax.dot_general(first, second, (((0,), (0,)), ((), ())), preferred_elemen...]
    pallas_call x1, Pallas kernels: 70.6 us -> 44.6 us  [gather_rows(): pl.pallas_call(functools.partial(gather_kernel, count), out_shape=jax.Sha...]
    all_to_all x1 -> x0, starting transfers between devices: 16.8 us -> none  [body(): qkv_w_share = lax.all_to_all(grad_qkv_w_own, 'seq', 0, 1, tiled=True)]
    dot_general x8, matrix products: 51.9 us -> 35.9 us  [dot_plain(): return jnp.dot(first, second, preferred_element_type=jnp.float32)]
    all_to_all x1 -> x0, waiting for transfers between devices: 12.2 us -> none  [body(): qkv_w_share = lax.all_to_all(grad_qkv_w_own, 'seq', 0, 1, tiled=True)]
  transfers between devices with their start and end apart: 11 -> 15, of which waited for: 6 -> 4; matrix products, arithmetic and copies ran while one was open for 13% -> 13% of each run, Pallas kernels for 21% -> 38%
where the time goes in v2:
time: 659 us; the launch traced here: 651 us
  Pallas kernels  432 us (66%)
  matrix products  87.3 us (13%)
  other arithmetic  68.3 us (10%)
  local copies, waits for them, and re-layouts  27 us (4%)
  between operations  16.8 us (3%)
  waiting for transfers between devices  16.4 us (2%)
    pallas_call x1, Pallas kernels, finish(): pl.pallas_call(functools.partial(finish_kernel, counts, (tuple((term.shap...  134 us
    pallas_call x12, Pallas kernels, weight_grad(): pl.pallas_call(weight_grad_kernel, grid_spec=pltpu.PrefetchScalarGridSpec...  81.7 us
    pallas_call x2, Pallas kernels, exchange(): pl.pallas_call(functools.partial(exchange_kernel, counts, len(arrays), pa...  75.2 us
    dot_general x7, matrix products, dot_right(): lax.dot_general(first, second, (((1,), (1,)), ((), ())), preferred_elemen...  46 us
    pallas_call x1, Pallas kernels, gather_rows(): pl.pallas_call(functools.partial(gather_kernel, count), out_shape=jax.Sha...  44.6 us
    dot_general x8, matrix products, dot_plain(): return jnp.dot(first, second, preferred_element_type=jnp.float32)  35.9 us
    pallas_call x1, Pallas kernels, self_backward(): pl.pallas_call(self_backward_kernel, out_shape=jax.ShapeDtypeStruct((leng...  35.6 us
    pallas_call x1, Pallas kernels, cross_backward(): pl.pallas_call(cross_backward_kernel, grid=(steps,), out_shape=(jax.Shape...  18.7 us
  transfers between devices with their start and end apart: 15, of which 4 were waited for; matrix products, arithmetic and copies ran while one was open for 13% of the time, Pallas kernels for 38%

profile of v2, /device:TPU:0, one launch (start us, length us, event | category | flops | bytes accessed | tf_op | source)
XLA Modules:
  0.0 651.1 jit_solution(17810233834047253307)
XLA Ops:
  14.0 44.6 %shard_map.416 = bf16[2048,1024]{1,0:T(8,128)(2,1)} custom-call(bf16[256,1024]{1,0:T(8,128)(2,1)} %bitcast.105), custom_call_target="tpu_custom_call" | custom-call | tf_op jit(solution)/shard_map/pallas_call | solution.py:169
  66.2 4.6 fusion.5
  72.8 5.7 add_convert_fusion.3.qkv_ref
  81.1 6.0 fusion.37.start_ref
  87.1 11.8 %shard_map.417 = (bf16[2048,128]{1,0:T(8,128)(2,1)}, f32[2,2048]{1,0:T(2,128)}) custom-call(bf16[2048,384]{1,0:T(8,128)(2,1)} %add_convert_fusion.3.qkv_ref, s32[1,2048]{1,0:T(1,128)} %fusion.37.start_ref), custom_call_target="tpu_custom_call" | custom-call | tf_op jit(solution)/shard_map/pallas_call | solution.py:618
  100.3 35.0 %shard_map.418 = (bf16[256,1024]{1,0:T(8,128)(2,1)}, bf16[256,1024]{1,0:T(8,128)(2,1)}) custom-call(bf16[2048,128]{1,0:T(8,128)(2,1)} %get-tuple-element.46.refs_0_.out_ref, bf16[256,128]{1,0:T(8,128)(2,1)} %pad_maximum_fusion.4.refs_1_), custom_call_target="tpu_custom_call" | custom-call | tf_op jit(solution)/shard_map/pallas_call | solution.py:312
  141.9 6.8 %add_convert_fusion.1.own_key_ref.own_value_ref = bf16[640,2048]{1,0:T(8,128)(2,1)} fusion(bf16[1024,2048]{1,0:T(8,128)(2,1)} %param.40, f32[2048]{0:T(1024)S(1)} %pad_convert_fusion, bf16[588,1024]{1,0:T(8,128)(2,1)S(1)} %bitcast.104), kind=kOutput, calls=%fused_computation.27 | convolution fusion | flops 2686976000 | bytes 8028160 | tf_op jit(solution)/shard_map/dot_general | solution.py:42
  153.4 4.7 add_convert_fusion.2.key_ref.value_ref
  160.4 15.2 %shard_map.419 = (bf16[384,1024]{1,0:T(8,128)(2,1)}, f32[8,2,384]{2,1,0:T(2,128)}) custom-call(bf16[384,1024]{1,0:T(8,128)(2,1)} %add_convert_fusion.6.query_ref, bf16[640,2048]{1,0:T(8,128)(2,1)} %add_convert_fusion.2.key_ref.value_ref, bf16[640,2048]{1,0:T(8,128)(2,1)} %add_convert_fusion.2.key_ref.value_ref, ...), custom_call_target="tpu_custom_call" | custom-call | tf_op jit(solution)/shard_map/pallas_call | solution.py:728
  178.5 6.6 %convolution_add_fusion = f32[384,4096]{1,0:T(8,128)S(1)} fusion(bf16[384,1024]{1,0:T(8,128)(2,1)S(1)} %add_convert_fusion.5.first_ref, bf16[1024,4096]{1,0:T(8,128)(2,1)} %param.46, f32[4096]{0:T(1024)S(1)} %convert_element_type.176), kind=kOutput, calls=%fused_computation.26 | convolution fusion | flops 3222798336 | bytes 15482880 | tf_op jit(solution)/shard_map/dot_general | solution.py:42
  185.5 19.3 %convert_reduce_fusion.1 = (f32[4096]{0:T(1024)S(1)}, bf16[384,4096]{1,0:T(8,128)(2,1)S(1)}, f32[384,4096]{1,0:T(8,128)}) fusion(f32[384,4096]{1,0:T(8,128)S(1)} %convolution_add_fusion, bf16[384,1024]{1,0:T(8,128)(2,1)S(1)} %get-tuple-element.127.second_ref, bf16[4096,1024]{1,0:T(8,128)(2,1)S(1)} %bitcast.117), kind=kOutput, calls=%fused_computation.10 | convolution fusion | flops 3337613312 | bytes 24920064 | tf_op jit(solution)/shard_map/dot_general | solution.py:52
  204.8 5.3 multiply_convert_fusion.first_ref
  210.1 7.8 %multiply_reduce_fusion = (f32[1024]{0:T(1024)S(1)}, f32[384]{0:T(512)S(1)}, f32[1024]{0:T(1024)S(1)}, f32[384,1024]{1,0:T(8,128)S(1)}) fusion(f32[384,1024]{1,0:T(8,128)S(1)} %get-tuple-element.184, f32[384]{0:T(512)S(1)} %fusion.39, f32[384]{0:T(512)S(1)} %broadcast_multiply_fusion.1, f32[1024]{0:T(1024)S(1)} %convert_element_type.173, ...), kind=kOutput, calls=%fused_computation.38 | convolution fusion | flops 3224368640 | bytes 14696960 | tf_op jit(solution)/shard_map/dot_general | solution.py:52
  222.8 18.7 %shard_map.420 = (bf16[384,1024]{1,0:T(8,128)(2,1)}, bf16[640,1024]{1,0:T(8,128)(2,1)}, bf16[640,1024]{1,0:T(8,128)(2,1)}, bf16[640,1024]{1,0:T(8,128)(2,1)}, bf16[640,1024]{1,0:T(8,128)(2,1)}) custom-call(bf16[384,1024]{1,0:T(8,128)(2,1)} %add_convert_fusion.6.query_ref, bf16[640,2048]{1,0:T(8,128)(2,1)} %add_convert_fusion.2.key_ref.value_ref, ...), custom_call_target="tpu_custom_call" | custom-call | tf_op jit(solution)/shard_map/pallas_call | solution.py:795
  246.5 13.3 %shard_map.423 = bf16[512,4096]{1,0:T(8,128)(2,1)} custom-call(s32[1]{0:T(128)S(6)} %sub.71.which_ref, bf16[384,1024]{1,0:T(8,128)(2,1)} %copy-done.16, bf16[384,4096]{1,0:T(8,128)(2,1)} %copy-done.11), custom_call_target="tpu_custom_call" | custom-call | flops 1610612736 | bytes 12320768 | tf_op jit(solution)/shard_map/pallas_call | solution.py:536
  262.5 6.9 %add_convert_fusion.4 = bf16[384,1024]{1,0:T(8,128)(2,1)S(1)} fusion(f32[384,1024]{1,0:T(8,128)S(1)} %copy-done.8, bf16[384,4096]{1,0:T(8,128)(2,1)S(1)} %multiply_convert_fusion.first_ref, bf16[4096,1024]{1,0:T(8,128)(2,1)} %param.48, f32[1024]{0:T(1024)S(1)} %convert_element_type.181), kind=kOutput, calls=%fused_computation.46 | convolution fusion | flops 3222405120 | bytes 13897728 | tf_op jit(solution)/shard_map/dot_general | solution.py:42
  275.7 13.8 %shard_map.424 = bf16[512,4096]{1,0:T(8,128)(2,1)} custom-call(s32[1]{0:T(128)} %bitcast.24.which_ref, bf16[384,1024]{1,0:T(8,128)(2,1)} %copy-done.16, bf16[384,4096]{1,0:T(8,128)(2,1)} %copy-done.11, bf16[512,4096]{1,0:T(8,128)(2,1)} %collective-permute-done.5.refs_0_), custom_call_target="tpu_custom_call" | custom-call | flops 1610612736 | bytes 12320768 | tf_op jit(solution)/shard_map/pallas_call | solution.py:536
  289.6 5.9 shard_map.425
  295.7 7.2 %collective-permute-done.6.refs_0_ = bf16[2048,1024]{1,0:T(8,128)(2,1)S(1)} collective-permute-done((bf16[2048,1024]{1,0:T(8,128)(2,1)}, bf16[2048,1024]{1,0:T(8,128)(2,1)S(1)}, u32[]{:S(2)}, u32[]{:S(2)}) %collective-permute-start.6) | collective-permute-done | bytes 4194336 | tf_op jit(solution)/shard_map/ppermute | solution.py:869
  304.9 6.7 %shard_map.426 = bf16[2048,1024]{1,0:T(8,128)(2,1)} custom-call(s32[1]{0:T(128)} %bitcast.24.which_ref, bf16[384,4096]{1,0:T(8,128)(2,1)} %copy-done.3, bf16[384,1024]{1,0:T(8,128)(2,1)} %copy-done.4, bf16[2048,1024]{1,0:T(8,128)(2,1)} %copy-done.29), custom_call_target="tpu_custom_call" | custom-call | flops 1610612736 | bytes 12320768 | tf_op jit(solution)/shard_map/pallas_call | solution.py:536
  316.2 40.2 %shard_map.421 = (bf16[2048,128]{1,0:T(8,128)(2,1)}, bf16[8,128,128]{2,1,0:T(8,128)(2,1)}) custom-call(bf16[384,1024]{1,0:T(8,128)(2,1)} %convolution_convert_fusion.1.refs_0_), custom_call_target="tpu_custom_call" | custom-call | tf_op jit(solution)/shard_map/pallas_call | solution.py:312
  360.2 35.6 %shard_map.422.refs_0_ = bf16[2048,384]{1,0:T(8,128)(2,1)} custom-call(bf16[2048,384]{1,0:T(8,128)(2,1)} %add_convert_fusion.3.qkv_ref, bf16[2048,128]{1,0:T(8,128)(2,1)} %get-tuple-element.46.refs_0_.out_ref, bf16[2048,128]{1,0:T(8,128)(2,1)} %pad_maximum_fusion.3.grad_ref, s32[1,2048]{1,0:T(1,128)} %fusion.37.start_ref, f32[2,2048]{1,0:T(2,128)} %get-tuple-element.57.stat_ref), custom_call_target="tpu_custom_call" | custom-call | tf_op jit(solution)/shard_map/pallas_call | solution.py:686
  420.2 7.9 %shard_map.433 = bf16[512,2048]{1,0:T(8,128)(2,1)} custom-call(s32[1]{0:T(128)S(6)} %sub.71.which_ref, bf16[588,1024]{1,0:T(8,128)(2,1)} %bitcast.102, bf16[588,2048]{1,0:T(8,128)(2,1)} %maximum_select_fusion.second_ref), custom_call_target="tpu_custom_call" | custom-call | flops 1233125376 | bytes 7806976 | tf_op jit(solution)/shard_map/pallas_call | solution.py:536
  428.3 5.4 convolution_convert_fusion
  438.1 4.4 shard_map.430.refs_5_
  442.5 4.6 shard_map.432.refs_6_
  447.1 4.5 convolution_bitcast_fusion
  458.2 8.1 %shard_map.434.refs_7_ = bf16[512,2048]{1,0:T(8,128)(2,1)} custom-call(s32[1]{0:T(128)} %bitcast.24.which_ref, bf16[588,1024]{1,0:T(8,128)(2,1)} %bitcast.103, bf16[588,2048]{1,0:T(8,128)(2,1)} %maximum_select_fusion.second_ref, bf16[512,2048]{1,0:T(8,128)(2,1)} %collective-permute-done.10.refs_0_), custom_call_target="tpu_custom_call" | custom-call | flops 1233125376 | bytes 7806976 | tf_op jit(solution)/shard_map/pallas_call | solution.py:536
  466.2 5.7 reduce-scatter.5.cloned.1.call-done.refs_3_
  471.9 134.4 %shard_map.435 = (bf16[256,3072]{1,0:T(8,128)(2,1)}, bf16[128,3072]{1,0:T(8,128)(2,1)}, bf16[128,4096]{1,0:T(8,128)(2,1)}, bf16[512,1024]{1,0:T(8,128)(2,1)}, bf...) custom-call(bf16[2048,384]{1,0:T(8,128)(2,1)} %shard_map.422.refs_0_, ...), custom_call_target="tpu_custom_call" | custom-call | tf_op jit(solution)/shard_map/pallas_call | solution.py:455
  606.3 5.3 fusion.45
  613.9 14.8 %shard_map.436 = f32[4,8,384]{2,1,0:T(8,128)} custom-call(f32[8,8,384]{2,1,0:T(8,128)} %bitcast.111), custom_call_target="tpu_custom_call" | custom-call | tf_op jit(solution)/shard_map/pallas_call | solution.py:500
  (303 shorter events, 117.6 us)
Async XLA Ops:
  7.2 151.3 %copy-start = (bf16[1024,1024]{1,0:T(8,128)(2,1)S(1)}, bf16[1024,1024]{1,0:T(8,128)(2,1)}, u32[]{:S(2)}) copy-start(bf16[1024,1024]{1,0:T(8,128)(2,1)} %param.38) | copy-start | bytes 6291460
  7.2 134.1 %all-reduce.6.cloned.1.call-start = ((), (), s32[]{:S(2)}) async-start(), calls=%async_computation.2 | async-start | bytes 1835008 | tf_op jit(solution)/shard_map/psum | solution.py:919
  13.6 65.0 %collective-permute-start = (bf16[320,1024]{1,0:T(8,128)(2,1)}, bf16[320,1024]{1,0:T(8,128)(2,1)}, u32[]{:S(2)}, u32[]{:S(2)}) collective-permute-start(bf16[320,1024]{1,0:T(8,128)(2,1)} %dynamic-slice_bitcast_fusion), channel_id=1, source_target_pairs={{0,1},{1,0},{2,3},{3,2},{4,5},{5,4},{6,7},{7,6},{8,9},{9,8},{10,11... | collective-permute-start | bytes 1966088 | tf_op jit(solution)/shard_map/ppermute | solution.py:869
  14.0 44.6 %copy-start.51 = (bf16[1024]{0:T(1024)(128)(2,1)S(1)}, bf16[1024]{0:T(1024)(128)(2,1)}, u32[]{:S(2)}) copy-start(bf16[1024]{0:T(1024)(128)(2,1)} %param.31) | copy-start | bytes 6148
  14.0 44.6 %copy-start.52 = (bf16[1024]{0:T(1024)(128)(2,1)S(1)}, bf16[1024]{0:T(1024)(128)(2,1)}, u32[]{:S(2)}) copy-start(bf16[1024]{0:T(1024)(128)(2,1)} %param.30) | copy-start | bytes 6148
  80.7 54.6 %copy-start.55 = (bf16[1024]{0:T(1024)(128)(2,1)S(1)}, bf16[1024]{0:T(1024)(128)(2,1)}, u32[]{:S(2)}) copy-start(bf16[1024]{0:T(1024)(128)(2,1)} %param.37) | copy-start | bytes 6148
  80.7 54.6 %copy-start.56 = (bf16[1024]{0:T(1024)(128)(2,1)S(1)}, bf16[1024]{0:T(1024)(128)(2,1)}, u32[]{:S(2)}) copy-start(bf16[1024]{0:T(1024)(128)(2,1)} %param.36) | copy-start | bytes 6148
  80.7 54.6 %copy-start.57 = (bf16[1024]{0:T(1024)(128)(2,1)S(1)}, bf16[1024]{0:T(1024)(128)(2,1)}, u32[]{:S(2)}) copy-start(bf16[1024]{0:T(1024)(128)(2,1)} %param.39) | copy-start | bytes 6148
  80.7 54.6 %copy-start.58 = (bf16[1024]{0:T(1024)(128)(2,1)S(1)}, bf16[1024]{0:T(1024)(128)(2,1)}, u32[]{:S(2)}) copy-start(bf16[1024]{0:T(1024)(128)(2,1)} %param.45) | copy-start | bytes 6148
  80.7 54.6 %copy-start.59 = (bf16[1024]{0:T(1024)(128)(2,1)S(1)}, bf16[1024]{0:T(1024)(128)(2,1)}, u32[]{:S(2)}) copy-start(bf16[1024]{0:T(1024)(128)(2,1)} %param.44) | copy-start | bytes 6148
  80.8 54.6 %copy-start.50 = (bf16[4096]{0:T(1024)(128)(2,1)S(1)}, bf16[4096]{0:T(1024)(128)(2,1)}, u32[]{:S(2)}) copy-start(bf16[4096]{0:T(1024)(128)(2,1)} %param.47) | copy-start | bytes 24580
  80.8 54.7 %copy-start.60 = (bf16[1024]{0:T(1024)(128)(2,1)S(1)}, bf16[1024]{0:T(1024)(128)(2,1)}, u32[]{:S(2)}) copy-start(bf16[1024]{0:T(1024)(128)(2,1)} %param.49) | copy-start | bytes 6148
  80.8 61.1 %copy-start.61 = (bf16[1024]{0:T(1024)(128)(2,1)S(1)}, bf16[1024]{0:T(1024)(128)(2,1)}, u32[]{:S(2)}) copy-start(bf16[1024]{0:T(1024)(128)(2,1)} %param.41) | copy-start | bytes 6148
  80.8 61.1 %copy-start.12 = (bf16[1,588,1024]{2,1,0:T(8,128)(2,1)S(1)}, bf16[1,588,1024]{2,1,0:T(8,128)(2,1)}, u32[]{:S(2)}) copy-start(bf16[1,588,1024]{2,1,0:T(8,128)(2,1)} %param.26) | copy-start | bytes 3612676
  80.8 314.9 %all-reduce.8.cloned.1.call-start = ((), (), s32[]{:S(2)}) async-start(), calls=%async_computation.3 | async-start | bytes 2949120 | tf_op jit(solution)/shard_map/psum | solution.py:1070
  141.3 7.4 %collective-permute-start.1 = (bf16[448,1024]{1,0:T(8,128)(2,1)}, bf16[448,1024]{1,0:T(8,128)(2,1)S(1)}, u32[]{:S(2)}, u32[]{:S(2)}) collective-permute-start(bf16[448,1024]{1,0:T(8,128)(2,1)} %all-reduce.6.cloned.1.call-done), channel_id=1, source_target_pairs={{0,1},{1,0},{2,3},{3,2},{4,5},{5,4},{6,7},{7,6},{8,9},{9,8},{10,11... | collective-permute-start | bytes 2752520 | tf_op jit(solution)/shard_map/ppermute | solution.py:869
  177.8 40.1 %copy-start.7 = (f32[384,1024]{1,0:T(8,128)}, f32[384,1024]{1,0:T(8,128)S(1)}, u32[]{:S(2)}) copy-start(f32[384,1024]{1,0:T(8,128)S(1)} %get-tuple-element.184) | copy-start | bytes 4718596
  185.4 84.0 %copy-start.4 = (bf16[384,1024]{1,0:T(8,128)(2,1)}, bf16[384,1024]{1,0:T(8,128)(2,1)S(1)}, u32[]{:S(2)}) copy-start(bf16[384,1024]{1,0:T(8,128)(2,1)S(1)} %get-tuple-element.127.second_ref) | copy-start | bytes 2359300
  210.1 52.4 %copy-start.3 = (bf16[384,4096]{1,0:T(8,128)(2,1)}, bf16[384,4096]{1,0:T(8,128)(2,1)S(1)}, u32[]{:S(2)}) copy-start(bf16[384,4096]{1,0:T(8,128)(2,1)S(1)} %multiply_convert_fusion.first_ref) | copy-start | bytes 9437188
  246.5 26.4 %collective-permute-start.2 = (bf16[640,1024]{1,0:T(8,128)(2,1)}, bf16[640,1024]{1,0:T(8,128)(2,1)}, u32[]{:S(2)}, u32[]{:S(2)}) collective-permute-start(bf16[640,1024]{1,0:T(8,128)(2,1)} %broadcast_select_fusion.3), channel_id=1, source_target_pairs={{0,1},{1,0},{2,3},{3,2},{4,5},{5,4},{6,7},{7,6},{8,9},{9,8},{10,11... | collective-permute-start | bytes 3932168 | tf_op jit(solution)/shard_map/ppermute | solution.py:869
  259.8 15.9 %collective-permute-start.5 = (bf16[512,4096]{1,0:T(8,128)(2,1)}, bf16[512,4096]{1,0:T(8,128)(2,1)}, u32[]{:S(2)}, u32[]{:S(2)}) collective-permute-start(bf16[512,4096]{1,0:T(8,128)(2,1)} %shard_map.423), channel_id=1, source_target_pairs={{0,1},{1,0},{2,3},{3,2},{4,5},{5,4},{6,7},{7,6},{8,9},{9,8},{10,11... | collective-permute-start | bytes 12582920 | tf_op jit(solution)/shard_map/ppermute | solution.py:869
  271.1 1.6 collective-permute-start.3
  275.7 190.6 %reduce-scatter.3.cloned.1.call-start = ((), (), s32[]{:S(2)}) async-start(), calls=%async_computation.4 | async-start | bytes 5242880 | tf_op jit(solution)/shard_map/reduce_scatter | solution.py:1002
  289.6 182.3 %reduce-scatter.5.cloned.1.call-start = ((), (), s32[]{:S(2)}) async-start(), calls=%async_computation.5 | async-start | bytes 5242880 | tf_op jit(solution)/shard_map/reduce_scatter | solution.py:999
  295.5 7.4 %collective-permute-start.6 = (bf16[2048,1024]{1,0:T(8,128)(2,1)}, bf16[2048,1024]{1,0:T(8,128)(2,1)S(1)}, u32[]{:S(2)}, u32[]{:S(2)}) collective-permute-start(bf16[2048,1024]{1,0:T(8,128)(2,1)} %shard_map.425), channel_id=1, source_target_pairs={{0,1},{1,0},{2,3},{3,2},{4,5},{5,4},{6,7},{7,6},{8,9},{9,8},{10,11... | collective-permute-start | bytes 12582920 | tf_op jit(solution)/shard_map/ppermute | solution.py:869
  360.2 36.5 %copy-start.43 = (bf16[256,1024]{1,0:T(8,128)(2,1)S(1)}, bf16[256,1024]{1,0:T(8,128)(2,1)}, u32[]{:S(2)}) copy-start(bf16[256,1024]{1,0:T(8,128)(2,1)} %get-tuple-element.47) | copy-start | bytes 1572868
  395.8 18.3 %collective-permute-start.4 = (bf16[716,1024]{1,0:T(8,128)(2,1)}, bf16[716,1024]{1,0:T(8,128)(2,1)}, u32[]{:S(2)}, u32[]{:S(2)}) collective-permute-start(bf16[716,1024]{1,0:T(8,128)(2,1)} %all-reduce.8.cloned.1.call-done), channel_id=1, source_target_pairs={{0,1},{1,0},{2,3},{3,2},{4,5},{5,4},{6,7},{7,6},{8,9},{9,8},{10,11... | collective-permute-start | bytes 4399112 | tf_op jit(solution)/shard_map/ppermute | solution.py:869
  401.8 31.9 %collective-permute-start.7 = (bf16[512,1024]{1,0:T(8,128)(2,1)}, bf16[512,1024]{1,0:T(8,128)(2,1)}, u32[]{:S(2)}, u32[]{:S(2)}) collective-permute-start(bf16[512,1024]{1,0:T(8,128)(2,1)} %shard_map.427), channel_id=1, source_target_pairs={{0,1},{1,0},{2,3},{3,2},{4,5},{5,4},{6,7},{7,6},{8,9},{9,8},{10,11... | collective-permute-start | bytes 3145736 | tf_op jit(solution)/shard_map/ppermute | solution.py:869
  406.4 31.7 %collective-permute-start.8 = (bf16[512,1024]{1,0:T(8,128)(2,1)}, bf16[512,1024]{1,0:T(8,128)(2,1)}, u32[]{:S(2)}, u32[]{:S(2)}) collective-permute-start(bf16[512,1024]{1,0:T(8,128)(2,1)} %shard_map.429), channel_id=1, source_target_pairs={{0,1},{1,0},{2,3},{3,2},{4,5},{5,4},{6,7},{7,6},{8,9},{9,8},{10,11... | collective-permute-start | bytes 3145736 | tf_op jit(solution)/shard_map/ppermute | solution.py:869
  410.8 31.7 %collective-permute-start.9 = (bf16[512,1024]{1,0:T(8,128)(2,1)}, bf16[512,1024]{1,0:T(8,128)(2,1)}, u32[]{:S(2)}, u32[]{:S(2)}) collective-permute-start(bf16[512,1024]{1,0:T(8,128)(2,1)} %shard_map.431), channel_id=1, source_target_pairs={{0,1},{1,0},{2,3},{3,2},{4,5},{5,4},{6,7},{7,6},{8,9},{9,8},{10,11... | collective-permute-start | bytes 3145736 | tf_op jit(solution)/shard_map/ppermute | solution.py:869
  428.1 30.1 %collective-permute-start.10 = (bf16[512,2048]{1,0:T(8,128)(2,1)}, bf16[512,2048]{1,0:T(8,128)(2,1)}, u32[]{:S(2)}, u32[]{:S(2)}) collective-permute-start(bf16[512,2048]{1,0:T(8,128)(2,1)} %shard_map.433), channel_id=1, source_target_pairs={{0,1},{1,0},{2,3},{3,2},{4,5},{5,4},{6,7},{7,6},{8,9},{9,8},{10,11... | collective-permute-start | bytes 6291464 | tf_op jit(solution)/shard_map/ppermute | solution.py:869
  471.9 134.4 %copy-start.49 = (f32[1024]{0:T(1024)S(1)}, f32[1024]{0:T(1024)}, u32[]{:S(2)}) copy-start(f32[1024]{0:T(1024)} %copy-done.48) | copy-start | bytes 12292
  (51 other events, 243.0 us)
Sparse Core Ops, SparseCore 0:
  80.9 60.3 all-reduce.5
  275.8 85.6 all-reduce.7
  364.7 51.6 reduce-scatter.2
  419.2 52.6 reduce-scatter.4

commit v3 on v2

--- a/solution.py
+++ b/solution.py
@@ -329,9 +329,10 @@
     return low(functools.reduce(jnp.add, [wide(ref[i]) for i in range(ref.shape[0])]))
 
 
-def finish_kernel(counts, shapes, *refs):
-    rows_done, rows_open, lanes_ok = shapes
-    done, opened = len(rows_done), len(rows_open)
+def finish_kernel(counts, sizes, lanes_ok, *refs):
+    ready, opened = sizes
+    over_chips, over_rows = ready
+    done = over_chips + over_rows
     refs = list(refs)
 
     def take(number):
@@ -342,11 +343,11 @@
     dqkv_ref, own_ref = take(2)
     done_in, open_in = take(done), take(opened)
     tokens_ref, own_out = take(2)
-    done_out, open_out = take(done), take(opened)
+    outs = take(done + opened)
     own_slots, own_sum, own_block = take(3)
-    open_slots, open_sum = take(opened), take(opened)
+    row_slots, row_sum = take(over_rows + opened), take(over_rows + opened)
     chip_slots, chip_sum = take(done + opened), take(done + opened)
-    sems = take(3)
+    load_sem, *sems = take(4)
     greet(("seq", "rows"), counts)
     number = 0
 
@@ -372,23 +373,41 @@
         ]
     else:
         home = [move(dqkv_ref, tokens_ref, "seq", rows_of(tokens), lead)]
-    over_rows = [
+    open_rows = [
         move(ref, slots, "rows", columns_of(slots.shape[2]), lead)
-        for ref, slots in zip(open_in, open_slots)
+        for ref, slots in zip(open_in, row_slots[over_rows:])
     ]
     own_rows = move(own_ref, own_slots, "rows", second_dim, lead)
-    done_chips = [
-        move(ref, slots, "chip", rows_of(slots.shape[1]), lead)
-        for ref, slots in zip(done_in, chip_slots[:done])
+    for item in home + open_rows + [own_rows]:
+        item.start()
+    loads = [
+        pltpu.make_async_copy(ref, slots, load_sem.at[index])
+        for index, (ref, slots) in enumerate(
+            zip(done_in, chip_slots[:over_chips] + row_slots[:over_rows])
+        )
     ]
-    for item in home + over_rows + [own_rows] + done_chips:
-        item.start()
-    open_chips = []
-    for item, slots, total, place_ref in zip(over_rows, open_slots, open_sum, chip_slots[done:]):
-        item.arrived()
-        total[...] = add_slots(slots)
-        open_chips.append(move(total, place_ref, "chip", rows_of(place_ref.shape[1]), lead))
-        open_chips[-1].start()
+    for load in loads:
+        load.start()
+    chip_moves, last = [], []
+
+    def to_chips(index):
+        total, slots = row_sum[index], chip_slots[over_chips + index]
+        total[...] = add_slots(row_slots[index])
+        chip_moves.append(move(total, slots, "chip", rows_of(slots.shape[1]), lead))
+        chip_moves[-1].start()
+
+    def to_rows(index):
+        total = chip_sum[index]
+        total[...] = add_slots(chip_slots[index])
+        last.append(move(total, outs[index], "rows", whole, columns_of(total.shape[1])))
+        last[-1].start()
+
+    for index in range(over_rows):
+        loads[over_chips + index].wait()
+        to_chips(index)
+    for index in range(over_chips):
+        loads[index].wait()
+        to_rows(index)
     own_rows.arrived()
     own_sum[...] = add_slots(own_slots)
     if lanes_ok:
@@ -406,14 +425,12 @@
         own_chips = [move(own_sum, own_block, "seq", lead, lead)]
     for item in own_chips:
         item.start()
-    last = []
-    for item, slots, total, out in zip(
-        done_chips + open_chips, chip_slots, chip_sum, done_out + open_out
-    ):
+    for index, item in enumerate(open_rows):
         item.arrived()
-        total[...] = add_slots(slots)
-        last.append(move(total, out, "rows", whole, columns_of(total.shape[1])))
-        last[-1].start()
+        to_chips(over_rows + index)
+    for index, item in enumerate(chip_moves):
+        item.arrived()
+        to_rows(over_chips + index)
     for item in own_chips:
         item.arrived()
     if lanes_ok:
@@ -423,11 +440,11 @@
     last[-1].start()
     for item in home + last:
         item.arrived()
-    for item in home + over_rows + [own_rows] + done_chips + open_chips + own_chips + last:
+    for item in home + open_rows + [own_rows] + chip_moves + own_chips + last:
         item.sent()
 
 
-def finish(dqkv, own_grad, rows_done, rows_open, counts, collective_id):
+def finish(dqkv, own_grad, over_chips, over_rows, rows_open, counts, collective_id):
     count, chips, rows = counts["seq"], counts["chip"], counts["rows"]
     length, all_width = dqkv.shape
     width = all_width // 3
@@ -440,33 +457,31 @@
     else:
         tokens_shape = (count, tokens, all_width)
         own_block, own_out = (count, short, all_width), (rows, count, short, all_width)
-    shares = [term.shape for term in rows_done]
+    shares = [term.shape[1:] for term in over_rows]
     shares += [(term.shape[0], term.shape[1] // rows) for term in rows_open]
-    blocks = [(shape[0] // chips, shape[1]) for shape in shares]
+    blocks = [term.shape[1:] for term in over_chips]
+    blocks += [(shape[0] // chips, shape[1]) for shape in shares]
     outs = [tokens_shape, own_out] + [(shape[0], shape[1] * rows) for shape in blocks]
-    open_shares = shares[len(rows_done) :]
-    scratch = [(rows,) + own_grad.shape[:1] + own_grad.shape[2:]]
-    scratch += [own_grad.shape[:1] + own_grad.shape[2:], own_block]
-    scratch += [(rows,) + shape for shape in open_shares] + open_shares
+    own_share = own_grad.shape[:1] + own_grad.shape[2:]
+    scratch = [(rows,) + own_share, own_share, own_block]
+    scratch += [(rows,) + shape for shape in shares] + shares
     scratch += [(chips,) + shape for shape in blocks] + blocks
-    moves = 3 + 3 + 2 + len(rows_open) + 2 * len(shares)
+    moves = 3 + 3 + 2 + len(rows_open) + len(shares) + len(blocks)
     longest = max(count, rows)
-    arrays = [dqkv, own_grad, *rows_done, *rows_open]
+    arrays = [dqkv, own_grad, *over_chips, *over_rows, *rows_open]
     return pl.pallas_call(
         functools.partial(
             finish_kernel,
             counts,
-            (
-                tuple(term.shape for term in rows_done),
-                tuple(term.shape for term in rows_open),
-                lanes_ok,
-            ),
+            ((len(over_chips), len(over_rows)), len(rows_open)),
+            lanes_ok,
         ),
         out_shape=[jax.ShapeDtypeStruct(shape, bf) for shape in outs],
         in_specs=[pl.BlockSpec(memory_space=pl.ANY)] * len(arrays),
         out_specs=[pl.BlockSpec(memory_space=pl.ANY)] * len(outs),
         scratch_shapes=[pltpu.VMEM(shape, bf) for shape in scratch]
         + [
+            pltpu.SemaphoreType.DMA((len(over_chips) + len(over_rows),)),
             pltpu.SemaphoreType.DMA((moves,)),
             pltpu.SemaphoreType.DMA((moves, longest)),
             pltpu.SemaphoreType.DMA((moves, longest)),
@@ -513,44 +528,6 @@
     )(given)
 
 
-def weight_grad_kernel(which_ref, first_ref, second_ref, *refs):
-    grad = dot_left(first_ref[...], second_ref[...])
-    if len(refs) == 2:
-        grad = grad + wide(refs[0][...])
-    refs[-1][...] = low(grad)
-
-
-def weight_grad(first, second, which, chips, given=None):
-    tokens, depth = first.shape
-    block, columns = depth // (2 * chips), second.shape[1]
-    tile = min(columns, 1024)
-    out = pl.BlockSpec((block, tile), lambda n, z, which: (z, n))
-    specs = [
-        pl.BlockSpec((tokens, block), lambda n, z, which: (0, 2 * z + which[0])),
-        pl.BlockSpec((tokens, tile), lambda n, z, which: (0, n)),
-    ]
-    arrays = [first, second]
-    if given is not None:
-        specs.append(out)
-        arrays.append(given)
-    return pl.pallas_call(
-        weight_grad_kernel,
-        grid_spec=pltpu.PrefetchScalarGridSpec(
-            num_scalar_prefetch=1,
-            grid=(columns // tile, chips),
-            in_specs=specs,
-            out_specs=out,
-        ),
-        out_shape=jax.ShapeDtypeStruct((chips * block, columns), jnp.bfloat16),
-        compiler_params=pltpu.CompilerParams(vmem_limit_bytes=VMEM_LIMIT),
-        cost_estimate=pl.CostEstimate(
-            flops=tokens * depth * columns,
-            bytes_accessed=2 * (tokens * (depth + columns) + depth * columns),
-            transcendentals=0,
-        ),
-    )(which, *arrays)
-
-
 def head_lanes(width):
     return lax.broadcasted_iota(jnp.int32, (1, width), 1) // DEPTH
 
@@ -559,6 +536,13 @@
     if width == DEPTH:
         return values
     return jnp.where(head_lanes(width) == head, values, jnp.zeros_like(values))
+
+
+def begin_of(start_ref, position):
+    begin = jnp.zeros_like(position)
+    for page in range(1, PAGES):
+        begin = jnp.where(position >= start_ref[page], start_ref[page], begin)
+    return begin
 
 
 def as_row(column):
@@ -573,8 +557,8 @@
         rows = pl.ds(index * BLOCK, BLOCK)
         keys_end = (index + 1) * BLOCK
         query = qkv_ref[rows, 0:width]
-        begin = jnp.broadcast_to(start_ref[:, rows], (8, BLOCK)).T[:, :1]
         position = index * BLOCK + lax.broadcasted_iota(jnp.int32, (BLOCK, 1), 0)
+        begin = begin_of(start_ref, position)
         if index == blocks - 1 or index <= 1:
             cuts = [(0, keys_end)]
         else:
@@ -612,7 +596,7 @@
             stat_ref[head : head + 1, rows] = as_row(stats[head])
 
 
-def self_forward(qkv, begins):
+def self_forward(qkv, starts):
     length, width = qkv.shape[0], qkv.shape[1] // 3
     heads = width // DEPTH
     return pl.pallas_call(
@@ -621,16 +605,32 @@
             jax.ShapeDtypeStruct((length, width), jnp.bfloat16),
             jax.ShapeDtypeStruct((heads, length), jnp.float32),
         ),
-        in_specs=[pl.BlockSpec(memory_space=pltpu.VMEM)] * 2,
+        in_specs=[
+            pl.BlockSpec(memory_space=pltpu.VMEM),
+            pl.BlockSpec(memory_space=pltpu.SMEM),
+        ],
         out_specs=[pl.BlockSpec(memory_space=pltpu.VMEM)] * 2,
         compiler_params=pltpu.CompilerParams(vmem_limit_bytes=VMEM_LIMIT),
-    )(qkv, begins[None, :])
-
-
-def self_backward_kernel(qkv_ref, out_ref, grad_ref, start_ref, stat_ref, dqkv_ref, dk_ref, dv_ref):
+    )(qkv, starts)
+
+
+def self_backward_kernel(counts, hosted, *refs):
+    size = len(hosted)
+    qkv_ref, out_ref, grad_ref, start_ref, stat_ref = refs[:5]
+    sent, dqkv_ref, stacks = refs[5 : 5 + size], refs[5 + size], refs[6 + size : 6 + 2 * size]
+    dk_ref, dv_ref, own_sem, send_sem, recv_sem = refs[6 + 2 * size :]
     length, width = out_ref.shape
     heads = width // DEPTH
     blocks = length // BLOCK
+    greet(("seq", "rows"), counts)
+    moves = []
+    for index, ((axis, how), ref, stack) in enumerate(zip(hosted, sent, stacks)):
+        source = rows_of(stack.shape[1]) if how == "rows" else columns_of(stack.shape[2])
+        part = (ref, stack, axis, source, lead)
+        moves.append(
+            Transfers(part, counts, own_sem.at[index], send_sem.at[index], recv_sem.at[index])
+        )
+        moves[-1].start()
     dk_ref[...] = jnp.zeros_like(dk_ref)
     dv_ref[...] = jnp.zeros_like(dv_ref)
 
@@ -639,8 +639,8 @@
         query = qkv_ref[rows, 0:width]
         grad = grad_ref[rows, :]
         product = (wide(grad) * wide(out_ref[rows, :])).T
-        begin = start_ref[:, rows]
         position = index * BLOCK + lax.broadcasted_iota(jnp.int32, (1, BLOCK), 1)
+        begin = begin_of(start_ref, position)
         query_heads = [pick_head(query, head, width) * jnp.bfloat16(SCALE) for head in range(heads)]
         grad_heads = [pick_head(grad, head, width) for head in range(heads)]
         stats = [stat_ref[head : head + 1, rows] for head in range(heads)]
@@ -679,18 +679,38 @@
     lax.fori_loop(0, blocks, query_block, 0)
     dqkv_ref[:, width : 2 * width] = low(dk_ref[...])
     dqkv_ref[:, 2 * width : 3 * width] = low(dv_ref[...])
-
-
-def self_backward(qkv, out, grad, begins, stats):
+    for item in moves:
+        item.arrived()
+    for item in moves:
+        item.sent()
+
+
+def self_backward(qkv, out, grad, starts, stats, sent, hosted, counts, collective_id):
     length, width = out.shape
+    stacks = []
+    for array, (axis, how) in zip(sent, hosted):
+        rows, columns = array.shape
+        total = counts[axis]
+        block = (rows // total, columns) if how == "rows" else (rows, columns // total)
+        stacks.append(jax.ShapeDtypeStruct((total,) + block, array.dtype))
+    longest = max(counts["seq"], counts["rows"])
+    vmem, anywhere = pl.BlockSpec(memory_space=pltpu.VMEM), pl.BlockSpec(memory_space=pl.ANY)
     return pl.pallas_call(
-        self_backward_kernel,
-        out_shape=jax.ShapeDtypeStruct((length, 3 * width), jnp.bfloat16),
-        in_specs=[pl.BlockSpec(memory_space=pltpu.VMEM)] * 5,
-        out_specs=pl.BlockSpec(memory_space=pltpu.VMEM),
-        scratch_shapes=[pltpu.VMEM((length, width), jnp.float32)] * 2,
-        compiler_params=pltpu.CompilerParams(vmem_limit_bytes=VMEM_LIMIT),
-    )(qkv, out, grad, begins[None, :], stats)
+        functools.partial(self_backward_kernel, counts, hosted),
+        out_shape=[jax.ShapeDtypeStruct((length, 3 * width), jnp.bfloat16), *stacks],
+        in_specs=[vmem, vmem, vmem, pl.BlockSpec(memory_space=pltpu.SMEM), vmem]
+        + [anywhere] * len(sent),
+        out_specs=[vmem] + [anywhere] * len(sent),
+        scratch_shapes=[pltpu.VMEM((length, width), jnp.float32)] * 2
+        + [
+            pltpu.SemaphoreType.DMA((len(sent),)),
+            pltpu.SemaphoreType.DMA((len(sent), longest)),
+            pltpu.SemaphoreType.DMA((len(sent), longest)),
+        ],
+        compiler_params=pltpu.CompilerParams(
+            collective_id=collective_id, has_side_effects=True, vmem_limit_bytes=VMEM_LIMIT
+        ),
+    )(qkv, out, grad, starts, stats, *sent)
 
 
 def cross_forward_kernel(query_ref, key_ref, value_ref, own_key_ref, own_value_ref, out_ref, stat_ref):
@@ -848,22 +868,19 @@
     core = me % 2
 
     def pair_sum(first, second):
-        this = core.astype(jnp.int32)[None]
-        if first.shape[1] // count % 128:
-            wider = jnp.pad(
-                first.reshape(-1, count, first.shape[1] // count),
-                ((0, 0), (0, 0), (0, 128 - first.shape[1] // count)),
-            ).reshape(first.shape[0], -1)
-            theirs, mine = (weight_grad(wider, second, w, count // 2) for w in (1 - this, this))
-            theirs, mine = (
-                term.reshape(count // 2, 128, -1)[:, : first.shape[1] // count].reshape(
-                    first.shape[1] // 2, -1
-                )
-                for term in (theirs, mine)
+        size = first.shape[1] // count
+
+        def blocks_of(which):
+            return jnp.concatenate(
+                [
+                    lax.dynamic_slice_in_dim(first, (2 * chip + which) * size, size, 1)
+                    for chip in range(count // 2)
+                ],
+                axis=1,
             )
-            return low(wide(mine) + wide(swap(theirs)))
-        theirs = weight_grad(first, second, 1 - this, count // 2)
-        return weight_grad(first, second, this, count // 2, swap(theirs))
+
+        given = swap(low(dot_left(blocks_of(1 - core), second)))
+        return low(dot_left(blocks_of(core), second) + wide(given))
 
     def swap(value):
         return lax.ppermute(value, "seq", [(i, i ^ 1) for i in range(count)])
@@ -879,11 +896,7 @@
     gain_two, shift_two = wide(norm2_gain), wide(norm2_bias)
     gain_three, shift_three = wide(norm3_gain), wide(norm3_bias)
 
-    page_sizes = jnp.sum(row_segs[None, :] == jnp.arange(PAGES)[:, None], axis=1)
-    page_starts = jnp.cumsum(page_sizes) - page_sizes
-    begins = sum(
-        jnp.where(row_segs == page, page_starts[page], 0) for page in range(PAGES)
-    ).astype(jnp.int32)
+    starts = jnp.sum(row_segs[None, :] < jnp.arange(PAGES)[:, None], axis=1, dtype=jnp.int32)
     big_page = row_segs[length // 2]
     big_start = jnp.sum(row_segs < big_page)
     own_page = lax.dynamic_index_in_dim(row_pages, me // sharers, 0, keepdims=False)
@@ -938,16 +951,16 @@
     )
     normed_all = low(norm_forward(wide(x_all), gain_one, shift_one))
     qkv = low(dot_plain(normed_all, qkv_own_weight) + wide(qkv_own_bias))
-    mixed, mixed_stats = self_forward(qkv, begins)
+    mixed, mixed_stats = self_forward(qkv, starts)
     bf = jnp.bfloat16
     lanes_ok = width % 128 == 0
-    ends = jnp.concatenate((mixed[:SLOTS], mixed[length - SLOTS :]))
+    chosen = slots_of(mixed[:SLOTS], mixed[length - SLOTS :])
     if lanes_ok:
-        blocks_mixed, ends_mixed = exchange(
-            (mixed, ends),
+        blocks_mixed, slots_mixed = exchange(
+            (mixed, chosen),
             (
                 jax.ShapeDtypeStruct((tokens, features), bf),
-                jax.ShapeDtypeStruct((2 * SLOTS, features), bf),
+                jax.ShapeDtypeStruct((SLOTS, features), bf),
             ),
             (
                 (1, 1, "seq", whole, columns_of(width)),
@@ -957,23 +970,21 @@
             1,
         )
     else:
-        blocks_mixed, ends_mixed = exchange(
-            (mixed, ends),
+        blocks_mixed, slots_mixed = exchange(
+            (mixed, chosen),
             (
                 jax.ShapeDtypeStruct((count, tokens, width), bf),
-                jax.ShapeDtypeStruct((count, 2 * SLOTS, width), bf),
+                jax.ShapeDtypeStruct((count, SLOTS, width), bf),
             ),
             ((1, 1, "seq", whole, lead), (0, 0, "seq", rows_of(tokens), lead)),
             counts,
             1,
         )
-        blocks_mixed, ends_mixed = (
+        blocks_mixed, slots_mixed = (
             blocks.transpose(1, 0, 2).reshape(blocks.shape[1], -1)
-            for blocks in (blocks_mixed, ends_mixed)
+            for blocks in (blocks_mixed, slots_mixed)
         )
-    attended = jnp.concatenate(
-        (blocks_mixed, slots_of(ends_mixed[:SLOTS], ends_mixed[SLOTS:]))
-    )
+    attended = jnp.concatenate((blocks_mixed, slots_mixed))
     resid = wide(
         jnp.concatenate((x_own, slots_of(x_all[:SLOTS], x_all[length - SLOTS :])))
     )
@@ -1009,6 +1020,7 @@
     grad_co_w = pair_sum(cross_low, grad_branch_two)
     grad_co_b = jnp.sum(wide(grad_branch_two), axis=0)
     grad_cross_low = low(dot_right(grad_branch_two, cross_out_weight))
+    grad_cross_low = after(grad_cross_low, (grad_fc1_w, grad_fc2_w))
     grad_cross_q, big_dk, big_dv, own_dk, own_dv = cross_backward(
         cross_queries, kv_big, kv_own, cross_low, grad_cross_low, cross_stats
     )
@@ -1060,7 +1072,17 @@
             grad_mixed[length - SLOTS :] + jnp.where(in_front, no_slots, slots_grad),
         )
     )
-    dqkv = self_backward(qkv, mixed, grad_mixed, begins, mixed_stats)
+    dqkv, *stacks = self_backward(
+        qkv,
+        mixed,
+        grad_mixed,
+        starts,
+        mixed_stats,
+        (fc2_share, fc1_share, grad_co_w, grad_cq_w, grad_o_w),
+        (("chip", "rows"), ("chip", "rows")) + (("rows", "columns"),) * 3,
+        counts,
+        3,
+    )
 
     slot_final = jnp.where(active[tokens:], final[tokens:], jnp.zeros_like(final[tokens:]))
     own_half = jnp.where(core == 0, big_dk, big_dv)
@@ -1112,13 +1134,8 @@
 
     grad_qv_b = jnp.concatenate((in_features(0), in_features(2)))
 
-    grad_qkv, qkv_w, fc1_w, fc2_w, o_w, cq_w, co_w, ckv_w = finish(
-        dqkv,
-        grad_qkv_w,
-        (fc1_share, fc2_share),
-        (grad_o_w, grad_cq_w, grad_co_w, grad_ckv_w),
-        counts,
-        3,
+    grad_qkv, qkv_w, fc2_w, fc1_w, co_w, cq_w, o_w, ckv_w = finish(
+        dqkv, grad_qkv_w, stacks[:2], stacks[2:], (grad_ckv_w,), counts, 4
     )
     if not lanes_ok:
         grad_qkv = grad_qkv.reshape(count, tokens, 3, width).transpose(1, 2, 0, 3)
@@ -1150,7 +1167,7 @@
     )
     joined = jnp.concatenate([vector.reshape(count, -1) for vector in vectors], axis=1)
     joined = jnp.pad(joined, ((0, 0), (0, -joined.shape[1] % 1024))).reshape(count, 8, -1)
-    joined = jnp.sum(sum_vectors(joined, counts, 4), axis=0).reshape(-1)
+    joined = jnp.sum(sum_vectors(joined, counts, 5), axis=0).reshape(-1)
     pieces, offset = [], 0
     for vector in vectors:
         size = vector.shape[0] // count

time: 659 us -> 584 us (0.89)
  Pallas kernels: 432 us -> 299 us
  matrix products: 87.3 us -> 122 us
  waiting for transfers between devices: 16.4 us -> 50 us
  other arithmetic: 68.3 us -> 50.9 us
  local copies, waits for them, and re-layouts: 27 us -> 35.6 us
    pallas_call x14 -> x2, Pallas kernels: 252 us -> 151 us  [the longest x1 86.7 us: finish(): pl.pallas_call(functools.partial(finish_kernel, counts, ((len(over_chips)...]
    pallas_call x2, Pallas kernels: 75.2 us -> 45.8 us  [exchange(): pl.pallas_call(functools.partial(exchange_kernel, counts, len(arrays), pa...]
    dot_general x1 -> x13, matrix products: 5.44 us -> 34.9 us  [dot_left(): lax.dot_general(first, second, (((0,), (0,)), ((), ())), preferred_elemen...]
    psum x1, waiting for transfers between devices: 0.01 us -> 27.1 us  [body(): lax.psum(jnp.concatenate((own_half[:PAGE_TOK], slot_half)), 'seq', axis_i...]
    dot_general x8, matrix products: 35.9 us -> 50.4 us  [dot_plain(): return jnp.dot(first, second, preferred_element_type=jnp.float32)]
    dot_general x7, matrix products: 46 us -> 36.8 us  [dot_right(): lax.dot_general(first, second, (((1,), (1,)), ((), ())), preferred_elemen...]
    psum x1, waiting for transfers between devices: 1.98 us -> 9.25 us  [body(): mine = lax.psum(after(sent, x_all), 'seq', axis_index_groups=same_core)]
    dynamic_slice x0 -> x6, local copies, waits for them, and re-layouts: none -> 7.13 us  [blocks_of(): lax.dynamic_slice_in_dim(first, (2 * chip + which) * size, size, 1)]
  transfers between devices with their start and end apart: 15 -> 15, of which waited for: 4 -> 4; matrix products, arithmetic and copies ran while one was open for 13% -> 21% of each run, Pallas kernels for 38% -> 32%
where the time goes in v3:
time: 584 us; the launch traced here: 579 us
  Pallas kernels  299 us (51%)
  matrix products  122 us (21%)
  other arithmetic  50.9 us (9%)
  waiting for transfers between devices  50 us (9%)
  local copies, waits for them, and re-layouts  35.6 us (6%)
  between operations  16.8 us (3%)
    pallas_call x1, Pallas kernels, finish(): pl.pallas_call(functools.partial(finish_kernel, counts, ((len(over_chips)...  86.7 us
    pallas_call x1, Pallas kernels, self_backward(): pl.pallas_call(functools.partial(self_backward_kernel, counts, hosted), o...  64 us
    dot_general x8, matrix products, dot_plain(): return jnp.dot(first, second, preferred_element_type=jnp.float32)  50.4 us
    pallas_call x2, Pallas kernels, exchange(): pl.pallas_call(functools.partial(exchange_kernel, counts, len(arrays), pa...  45.8 us
    pallas_call x1, Pallas kernels, gather_rows(): pl.pallas_call(functools.partial(gather_kernel, count), out_shape=jax.Sha...  44.6 us
    dot_general x7, matrix products, dot_right(): lax.dot_general(first, second, (((1,), (1,)), ((), ())), preferred_elemen...  36.8 us
    dot_general x13, matrix products, dot_left(): lax.dot_general(first, second, (((0,), (0,)), ((), ())), preferred_elemen...  34.9 us
    psum x1, waiting for transfers between devices, body(): lax.psum(jnp.concatenate((own_half[:PAGE_TOK], slot_half)), 'seq', axis_i...  27.1 us
  transfers between devices with their start and end apart: 15, of which 4 were waited for; matrix products, arithmetic and copies ran while one was open for 21% of the time, Pallas kernels for 32%

profile of v3, /device:TPU:0, one launch (start us, length us, event | category | flops | bytes accessed | tf_op | source)
XLA Modules:
  0.0 578.9 jit_solution(2435805021033788901)
XLA Ops:
  14.0 44.6 %shard_map.416 = bf16[2048,1024]{1,0:T(8,128)(2,1)} custom-call(bf16[256,1024]{1,0:T(8,128)(2,1)} %bitcast.115), custom_call_target="tpu_custom_call" | custom-call | tf_op jit(solution)/shard_map/pallas_call | solution.py:169
  58.7 3.0 convert_reduce_fusion
  68.1 4.6 fusion.5
  75.2 5.9 %add_convert_fusion.6.qkv_ref.refs_0_ = bf16[2048,384]{1,0:T(8,128)(2,1)} fusion(bf16[2048,1024]{1,0:T(8,128)(2,1)} %fusion.5, f32[384]{0:T(512)S(1)} %maximum_convert_fusion, bf16[1024,128]{1,0:T(8,128)(2,1)} %get-tuple-element.153, bf16[1024,128]{1,0:T(8,128)(2,1)} %get-tuple-element.152, bf16[1024,128]{1,0:T(8,128)(2,1)} %get-tuple-element.151), kind=kOutput, calls=%fused_computation.35 | convolution fusion | flops 1614544896 | bytes 6555136 | tf_op jit(solution)/shard_map/dot_general | solution.py:42
  81.8 12.0 %shard_map.417 = (bf16[2048,128]{1,0:T(8,128)(2,1)}, f32[2,2048]{1,0:T(2,128)}) custom-call(bf16[2048,384]{1,0:T(8,128)(2,1)} %add_convert_fusion.6.qkv_ref.refs_0_, s32[8]{0:T(128)} %convert_reduce_fusion.9.start_ref.refs_3_), custom_call_target="tpu_custom_call" | custom-call | tf_op jit(solution)/shard_map/pallas_call | solution.py:602
  97.2 25.1 %shard_map.418 = (bf16[256,1024]{1,0:T(8,128)(2,1)}, bf16[128,1024]{1,0:T(8,128)(2,1)}) custom-call(bf16[2048,128]{1,0:T(8,128)(2,1)} %get-tuple-element.53.refs_0_.refs_1_, bf16[128,128]{1,0:T(8,128)(2,1)} %slice_select_fusion.6.refs_1_), custom_call_target="tpu_custom_call" | custom-call | tf_op jit(solution)/shard_map/pallas_call | solution.py:312
  124.5 9.2 %all-reduce.6.cloned.1.call-done = bf16[448,1024]{1,0:T(8,128)(2,1)} async-done(((bf16[448,1024]{1,0:T(8,128)(2,1)}), bf16[448,1024]{1,0:T(8,128)(2,1)}) %all-reduce.6.cloned.1.call-update) | async-done | bytes 917520 | tf_op jit(solution)/shard_map/psum | solution.py:932
  134.9 6.4 %add_convert_fusion.3.own_key_ref.own_value_ref = bf16[640,2048]{1,0:T(8,128)(2,1)} fusion(bf16[1024,2048]{1,0:T(8,128)(2,1)} %param.40, f32[2048]{0:T(1024)S(1)} %pad_convert_fusion, bf16[588,1024]{1,0:T(8,128)(2,1)S(1)} %bitcast.120), kind=kOutput, calls=%fused_computation.30 | convolution fusion | flops 2686976000 | bytes 8028160 | tf_op jit(solution)/shard_map/dot_general | solution.py:42
  146.7 4.7 add_convert_fusion.4.key_ref.value_ref
  153.6 15.2 %shard_map.419 = (bf16[384,1024]{1,0:T(8,128)(2,1)}, f32[8,2,384]{2,1,0:T(2,128)}) custom-call(bf16[384,1024]{1,0:T(8,128)(2,1)} %add_convert_fusion.12.query_ref, bf16[640,2048]{1,0:T(8,128)(2,1)} %add_convert_fusion.4.key_ref.value_ref, bf16[640,2048]{1,0:T(8,128)(2,1)} %add_convert_fusion.4.key_ref.value_ref, ...), custom_call_target="tpu_custom_call" | custom-call | tf_op jit(solution)/shard_map/pallas_call | solution.py:748
  172.6 20.5 %multiply_convert_fusion = (bf16[384,4096]{1,0:T(8,128)(2,1)S(1)}, f32[384,4096]{1,0:T(8,128)}, f32[384,4096]{1,0:T(8,128)}) fusion(f32[4096]{0:T(1024)S(1)} %convert_element_type.230, bf16[384,1024]{1,0:T(8,128)(2,1)S(1)} %add_convert_fusion.11, bf16[1024,4096]{1,0:T(8,128)(2,1)} %param.46), kind=kOutput, calls=%fused_computation.13 | convolution fusion | flops 3325034496 | bytes 24920064 | tf_op jit(solution)/shard_map/dot_general | solution.py:42
  197.7 6.8 %collective-permute-done.3 = bf16[2048,1024]{1,0:T(8,128)(2,1)S(1)} collective-permute-done((bf16[2048,1024]{1,0:T(8,128)(2,1)S(1)}, bf16[2048,1024]{1,0:T(8,128)(2,1)S(1)}, u32[]{:S(2)}, u32[]{:S(2)}) %collective-permute-start.3) | collective-permute-done | bytes 4194336 | tf_op jit(solution)/shard_map/ppermute | solution.py:886
  204.5 4.4 add_convert_fusion
  210.2 13.8 %convert_reduce_fusion.1 = (f32[4096]{0:T(1024)}, bf16[384,4096]{1,0:T(8,128)(2,1)S(1)}) fusion(f32[384,4096]{1,0:T(8,128)} %get-tuple-element.150, f32[384,4096]{1,0:T(8,128)} %get-tuple-element.234, bf16[4096,1024]{1,0:T(8,128)(2,1)} %param.48, bf16[128,1024]{1,0:T(8,128)(2,1)S(1)} %get-tuple-element.228, bf16[256,1024]{1,0:T(8,128)(2,1)S(1)} %bitcast.123, ...), kind=kOutput, calls=%fused_computation.12 | convolution fusion | flops 3248353280 | bytes 24920448 | tf_op jit(solution)/shard_map/dot_general | solution.py:52
  226.9 6.8 %collective-permute-done.2 = bf16[512,4096]{1,0:T(8,128)(2,1)S(1)} collective-permute-done((bf16[512,4096]{1,0:T(8,128)(2,1)S(1)}, bf16[512,4096]{1,0:T(8,128)(2,1)S(1)}, u32[]{:S(2)}, u32[]{:S(2)}) %collective-permute-start.2) | collective-permute-done | bytes 4194336 | tf_op jit(solution)/shard_map/ppermute | solution.py:886
  233.7 4.5 add_convert_fusion.1
  240.1 9.3 %multiply_reduce_fusion = (f32[1024]{0:T(1024)}, f32[384]{0:T(512)S(1)}, f32[1024]{0:T(1024)}, f32[384,1024]{1,0:T(8,128)S(1)}) fusion(f32[384,1024]{1,0:T(8,128)} %copy-done.4, f32[384]{0:T(512)S(1)} %fusion.134, f32[384]{0:T(512)S(1)} %broadcast_multiply_fusion.1, f32[1024]{0:T(1024)S(1)} %convert_element_type.227, bf16[384,4096]{1,0:T(8,128)(2,1)} %copy-done.24, ...), kind=kOutput, calls=%fused_computation.62 | convolution fusion | flops 3224368640 | bytes 14696960 | tf_op jit(solution)/shard_map/dot_general | solution.py:52
  255.4 7.8 %add_convert_fusion.10 = bf16[384,1024]{1,0:T(8,128)(2,1)} fusion(f32[384,1024]{1,0:T(8,128)S(1)} %copy-done.5, bf16[384,4096]{1,0:T(8,128)(2,1)S(1)} %copy-done.23, bf16[4096,1024]{1,0:T(8,128)(2,1)} %param.48, f32[1024]{0:T(1024)S(1)} %convert_element_type.241), kind=kOutput, calls=%fused_computation.70 | convolution fusion | flops 3222405120 | bytes 13897728 | tf_op jit(solution)/shard_map/dot_general | solution.py:42
  264.9 19.1 %shard_map.420 = (bf16[384,1024]{1,0:T(8,128)(2,1)}, bf16[640,1024]{1,0:T(8,128)(2,1)}, bf16[640,1024]{1,0:T(8,128)(2,1)}, bf16[640,1024]{1,0:T(8,128)(2,1)}, bf16[640,1024]{1,0:T(8,128)(2,1)}) custom-call(bf16[384,1024]{1,0:T(8,128)(2,1)} %add_convert_fusion.12.query_ref, bf16[640,2048]{1,0:T(8,128)(2,1)} %add_convert_fusion.4.key_ref.value_ref, ...), custom_call_target="tpu_custom_call" | custom-call | tf_op jit(solution)/shard_map/pallas_call | solution.py:815
  294.5 2.9 convolution_convert_fusion.3
  299.7 20.7 %shard_map.421 = (bf16[2048,128]{1,0:T(8,128)(2,1)}, bf16[8,128,128]{2,1,0:T(8,128)(2,1)}) custom-call(bf16[384,1024]{1,0:T(8,128)(2,1)} %convolution_convert_fusion.7.refs_0_), custom_call_target="tpu_custom_call" | custom-call | tf_op jit(solution)/shard_map/pallas_call | solution.py:312
  324.3 3.0 add_convert_fusion.8.refs_8_
  327.3 2.9 add_convert_fusion.7.refs_9_
  330.3 64.0 %shard_map.422 = (bf16[2048,384]{1,0:T(8,128)(2,1)}, bf16[4,512,256]{2,1,0:T(8,128)(2,1)}, bf16[4,128,1024]{2,1,0:T(8,128)(2,1)}, bf16[4,512,256]{2,1,0:T(8,128)...) custom-call(bf16[2048,384]{1,0:T(8,128)(2,1)} %add_convert_fusion.6.qkv_ref.refs_0_, ...), custom_call_target="tpu_custom_call" | custom-call | tf_op jit(solution)/shard_map/pallas_call | solution.py:698
  394.3 27.1 %all-reduce.8.cloned.1.call-done = bf16[716,1024]{1,0:T(8,128)(2,1)} async-done(((bf16[716,1024]{1,0:T(8,128)(2,1)}), bf16[716,1024]{1,0:T(8,128)(2,1)}) %all-reduce.8.cloned.1.call-update) | async-done | bytes 1466384 | tf_op jit(solution)/shard_map/psum | solution.py:1092
  436.8 3.3 convolution_convert_fusion.6
  440.1 2.7 convolution_bitcast_fusion
  442.8 3.9 copy.49
  449.3 3.1 add_convert_fusion.5.refs_7_
  452.5 86.7 %shard_map.423 = (bf16[256,3072]{1,0:T(8,128)(2,1)}, bf16[128,3072]{1,0:T(8,128)(2,1)}, bf16[512,1024]{1,0:T(8,128)(2,1)}, bf16[128,4096]{1,0:T(8,128)(2,1)}, bf...) custom-call(bf16[2048,384]{1,0:T(8,128)(2,1)} %get-tuple-element.66., ...), custom_call_target="tpu_custom_call" | custom-call | tf_op jit(solution)/shard_map/pallas_call | solution.py:472
  539.2 5.3 fusion.153
  546.9 12.0 %shard_map.424 = f32[4,8,384]{2,1,0:T(8,128)} custom-call(f32[8,8,384]{2,1,0:T(8,128)} %bitcast.127), custom_call_target="tpu_custom_call" | custom-call | tf_op jit(solution)/shard_map/pallas_call | solution.py:515
  (342 shorter events, 101.2 us)
Async XLA Ops:
  7.2 144.6 %copy-start = (bf16[1024,1024]{1,0:T(8,128)(2,1)S(1)}, bf16[1024,1024]{1,0:T(8,128)(2,1)}, u32[]{:S(2)}) copy-start(bf16[1024,1024]{1,0:T(8,128)(2,1)} %param.38) | copy-start | bytes 6291460
  7.2 126.5 %all-reduce.6.cloned.1.call-start = ((), (), s32[]{:S(2)}) async-start(), calls=%async_computation.2 | async-start | bytes 1835008 | tf_op jit(solution)/shard_map/psum | solution.py:932
  13.6 59.1 %collective-permute-start = (bf16[320,1024]{1,0:T(8,128)(2,1)}, bf16[320,1024]{1,0:T(8,128)(2,1)}, u32[]{:S(2)}, u32[]{:S(2)}) collective-permute-start(bf16[320,1024]{1,0:T(8,128)(2,1)} %dynamic-slice_bitcast_fusion), channel_id=1, source_target_pairs={{0,1},{1,0},{2,3},{3,2},{4,5},{5,4},{6,7},{7,6},{8,9},{9,8},{10,11... | collective-permute-start | bytes 1966088 | tf_op jit(solution)/shard_map/ppermute | solution.py:886
  14.0 44.6 %copy-start.72 = (bf16[1024]{0:T(1024)(128)(2,1)S(1)}, bf16[1024]{0:T(1024)(128)(2,1)}, u32[]{:S(2)}) copy-start(bf16[1024]{0:T(1024)(128)(2,1)} %param.31) | copy-start | bytes 6148
  14.0 44.6 %copy-start.73 = (bf16[1024]{0:T(1024)(128)(2,1)S(1)}, bf16[1024]{0:T(1024)(128)(2,1)}, u32[]{:S(2)}) copy-start(bf16[1024]{0:T(1024)(128)(2,1)} %param.30) | copy-start | bytes 6148
  74.9 255.4 %reduce-scatter.3.cloned.1.call-start = ((), (), s32[]{:S(2)}) async-start(), calls=%async_computation.4 | async-start | bytes 5242880 | tf_op jit(solution)/shard_map/reduce_scatter | solution.py:1010
  81.0 41.3 %copy-start.76 = (bf16[1024]{0:T(1024)(128)(2,1)S(1)}, bf16[1024]{0:T(1024)(128)(2,1)}, u32[]{:S(2)}) copy-start(bf16[1024]{0:T(1024)(128)(2,1)} %param.37) | copy-start | bytes 6148
  81.0 41.3 %copy-start.77 = (bf16[1024]{0:T(1024)(128)(2,1)S(1)}, bf16[1024]{0:T(1024)(128)(2,1)}, u32[]{:S(2)}) copy-start(bf16[1024]{0:T(1024)(128)(2,1)} %param.36) | copy-start | bytes 6148
  81.0 41.3 %copy-start.78 = (bf16[1024]{0:T(1024)(128)(2,1)S(1)}, bf16[1024]{0:T(1024)(128)(2,1)}, u32[]{:S(2)}) copy-start(bf16[1024]{0:T(1024)(128)(2,1)} %param.39) | copy-start | bytes 6148
  81.0 41.4 %copy-start.63 = (bf16[4096]{0:T(1024)(128)(2,1)S(1)}, bf16[4096]{0:T(1024)(128)(2,1)}, u32[]{:S(2)}) copy-start(bf16[4096]{0:T(1024)(128)(2,1)} %param.47) | copy-start | bytes 24580
  81.0 41.4 %copy-start.79 = (bf16[1024]{0:T(1024)(128)(2,1)S(1)}, bf16[1024]{0:T(1024)(128)(2,1)}, u32[]{:S(2)}) copy-start(bf16[1024]{0:T(1024)(128)(2,1)} %param.45) | copy-start | bytes 6148
  81.1 41.4 %copy-start.80 = (bf16[1024]{0:T(1024)(128)(2,1)S(1)}, bf16[1024]{0:T(1024)(128)(2,1)}, u32[]{:S(2)}) copy-start(bf16[1024]{0:T(1024)(128)(2,1)} %param.44) | copy-start | bytes 6148
  81.1 42.1 %copy-start.81 = (bf16[1024]{0:T(1024)(128)(2,1)S(1)}, bf16[1024]{0:T(1024)(128)(2,1)}, u32[]{:S(2)}) copy-start(bf16[1024]{0:T(1024)(128)(2,1)} %param.41) | copy-start | bytes 6148
  81.1 53.8 %copy-start.13 = (bf16[1,588,1024]{2,1,0:T(8,128)(2,1)S(1)}, bf16[1,588,1024]{2,1,0:T(8,128)(2,1)}, u32[]{:S(2)}) copy-start(bf16[1,588,1024]{2,1,0:T(8,128)(2,1)} %param.26) | copy-start | bytes 3612676
  95.7 45.9 %copy-start.64 = (pred[128]{0:T(512)(128)(4,1)}, pred[128]{0:T(512)(128)(4,1)S(1)}, u32[]{:S(2)}) copy-start(pred[128]{0:T(512)(128)(4,1)S(1)} %iota_compare_fusion.1) | copy-start | bytes 388
  133.7 7.6 %collective-permute-start.1 = (bf16[448,1024]{1,0:T(8,128)(2,1)}, bf16[448,1024]{1,0:T(8,128)(2,1)S(1)}, u32[]{:S(2)}, u32[]{:S(2)}) collective-permute-start(bf16[448,1024]{1,0:T(8,128)(2,1)} %all-reduce.6.cloned.1.call-done), channel_id=1, source_target_pairs={{0,1},{1,0},{2,3},{3,2},{4,5},{5,4},{6,7},{7,6},{8,9},{9,8},{10,11... | collective-permute-start | bytes 2752520 | tf_op jit(solution)/shard_map/ppermute | solution.py:886
  133.8 116.2 %copy-start.70 = (pred[384]{0:T(512)(128)(4,1)}, pred[384]{0:T(512)(128)(4,1)S(1)}, u32[]{:S(2)}) copy-start(pred[384]{0:T(512)(128)(4,1)S(1)} %pad_add_fusion) | copy-start | bytes 1156
  144.8 24.1 %copy-start.2 = (f32[384,1024]{1,0:T(8,128)}, f32[384,1024]{1,0:T(8,128)S(1)}, u32[]{:S(2)}) copy-start(f32[384,1024]{1,0:T(8,128)S(1)} %get-tuple-element.231) | copy-start | bytes 4718596
  197.2 7.3 %collective-permute-start.3 = (bf16[2048,1024]{1,0:T(8,128)(2,1)S(1)}, bf16[2048,1024]{1,0:T(8,128)(2,1)S(1)}, u32[]{:S(2)}, u32[]{:S(2)}) collective-permute-start(bf16[2048,1024]{1,0:T(8,128)(2,1)S(1)} %convolution_convert_fusion.1), channel_id=1, source_target_pairs={{0,1},{1,0},{2,3},{3,2},{4,5},{5,4},{6,7},{7,6},{8,9},{9,8},{10,11... | collective-permute-start | bytes 12582920 | tf_op jit(solution)/shard_map/ppermute | solution.py:886
  208.8 121.4 %reduce-scatter.5.cloned.1.call-start = ((), (), s32[]{:S(2)}) async-start(), calls=%async_computation.5 | async-start | bytes 5242880 | tf_op jit(solution)/shard_map/reduce_scatter | solution.py:1013
  226.4 7.3 %collective-permute-start.2 = (bf16[512,4096]{1,0:T(8,128)(2,1)S(1)}, bf16[512,4096]{1,0:T(8,128)(2,1)S(1)}, u32[]{:S(2)}, u32[]{:S(2)}) collective-permute-start(bf16[512,4096]{1,0:T(8,128)(2,1)S(1)} %convolution_convert_fusion), channel_id=1, source_target_pairs={{0,1},{1,0},{2,3},{3,2},{4,5},{5,4},{6,7},{7,6},{8,9},{9,8},{10,11... | collective-permute-start | bytes 12582920 | tf_op jit(solution)/shard_map/ppermute | solution.py:886
  238.2 183.2 %all-reduce.8.cloned.1.call-start = ((), (), s32[]{:S(2)}) async-start(), calls=%async_computation.3 | async-start | bytes 2949120 | tf_op jit(solution)/shard_map/psum | solution.py:1092
  251.1 12.0 %collective-permute-start.6 = (bf16[512,1024]{1,0:T(8,128)(2,1)S(1)}, bf16[512,1024]{1,0:T(8,128)(2,1)S(1)}, u32[]{:S(2)}, u32[]{:S(2)}) collective-permute-start(bf16[512,1024]{1,0:T(8,128)(2,1)S(1)} %convolution_convert_fusion.5), channel_id=1, source_target_pairs={{0,1},{1,0},{2,3},{3,2},{4,5},{5,4},{6,7},{7,6},{8,9},{9,8},{10,11... | collective-permute-start | bytes 3145736 | tf_op jit(solution)/shard_map/ppermute | solution.py:886
  285.6 7.2 %collective-permute-start.4 = (bf16[640,1024]{1,0:T(8,128)(2,1)S(1)}, bf16[640,1024]{1,0:T(8,128)(2,1)S(1)}, u32[]{:S(2)}, u32[]{:S(2)}) collective-permute-start(bf16[640,1024]{1,0:T(8,128)(2,1)S(1)} %broadcast_select_fusion.3), channel_id=1, source_target_pairs={{0,1},{1,0},{2,3},{3,2},{4,5},{5,4},{6,7},{7,6},{8,9},{9,8},{10,11... | collective-permute-start | bytes 3932168 | tf_op jit(solution)/shard_map/ppermute | solution.py:886
  290.4 2.3 collective-permute-start.5
  292.7 31.6 %collective-permute-start.7 = (bf16[512,1024]{1,0:T(8,128)(2,1)}, bf16[512,1024]{1,0:T(8,128)(2,1)}, u32[]{:S(2)}, u32[]{:S(2)}) collective-permute-start(bf16[512,1024]{1,0:T(8,128)(2,1)} %convolution_convert_fusion.4), channel_id=1, source_target_pairs={{0,1},{1,0},{2,3},{3,2},{4,5},{5,4},{6,7},{7,6},{8,9},{9,8},{10,11... | collective-permute-start | bytes 3145736 | tf_op jit(solution)/shard_map/ppermute | solution.py:886
  297.4 25.1 %copy-start.65 = (pred[128]{0:T(512)(128)(4,1)S(1)}, pred[128]{0:T(512)(128)(4,1)}, u32[]{:S(2)}) copy-start(pred[128]{0:T(512)(128)(4,1)} %copy-done.64) | copy-start | bytes 388
  297.4 29.9 %collective-permute-start.8 = (bf16[512,1024]{1,0:T(8,128)(2,1)}, bf16[512,1024]{1,0:T(8,128)(2,1)}, u32[]{:S(2)}, u32[]{:S(2)}) collective-permute-start(bf16[512,1024]{1,0:T(8,128)(2,1)} %convolution_convert_fusion.3), channel_id=1, source_target_pairs={{0,1},{1,0},{2,3},{3,2},{4,5},{5,4},{6,7},{7,6},{8,9},{9,8},{10,11... | collective-permute-start | bytes 3145736 | tf_op jit(solution)/shard_map/ppermute | solution.py:886
  394.3 30.1 %copy-start.62 = (f32[4096]{0:T(1024)S(1)}, f32[4096]{0:T(1024)}, u32[]{:S(2)}) copy-start(f32[4096]{0:T(1024)} %get-tuple-element.238) | copy-start | bytes 49156
  421.4 8.0 %collective-permute-start.9 = (bf16[716,1024]{1,0:T(8,128)(2,1)}, bf16[716,1024]{1,0:T(8,128)(2,1)}, u32[]{:S(2)}, u32[]{:S(2)}) collective-permute-start(bf16[716,1024]{1,0:T(8,128)(2,1)} %all-reduce.8.cloned.1.call-done), channel_id=1, source_target_pairs={{0,1},{1,0},{2,3},{3,2},{4,5},{5,4},{6,7},{7,6},{8,9},{9,8},{10,11... | collective-permute-start | bytes 4399112 | tf_op jit(solution)/shard_map/ppermute | solution.py:886
  436.3 13.0 %collective-permute-start.10 = (bf16[512,2048]{1,0:T(8,128)(2,1)S(1)}, bf16[512,2048]{1,0:T(8,128)(2,1)S(1)}, u32[]{:S(2)}, u32[]{:S(2)}) collective-permute-start(bf16[512,2048]{1,0:T(8,128)(2,1)S(1)} %convolution_convert_fusion.2), channel_id=1, source_target_pairs={{0,1},{1,0},{2,3},{3,2},{4,5},{5,4},{6,7},{7,6},{8,9},{9,8},{10,11... | collective-permute-start | bytes 6291464 | tf_op jit(solution)/shard_map/ppermute | solution.py:886
  452.4 86.7 %copy-start.60 = (f32[1024]{0:T(1024)S(1)}, f32[1024]{0:T(1024)}, u32[]{:S(2)}) copy-start(f32[1024]{0:T(1024)} %copy-done.59) | copy-start | bytes 12292
  (72 other events, 270.0 us)
Sparse Core Ops, SparseCore 0:
  75.0 58.6 all-reduce.5
  209.0 52.5 reduce-scatter.2
  264.8 52.6 reduce-scatter.4
  320.3 101.0 all-reduce.7

commit v4 on v3

--- a/solution.py
+++ b/solution.py
@@ -329,10 +329,19 @@
     return low(functools.reduce(jnp.add, [wide(ref[i]) for i in range(ref.shape[0])]))
 
 
-def finish_kernel(counts, sizes, lanes_ok, *refs):
-    ready, opened = sizes
-    over_chips, over_rows = ready
-    done = over_chips + over_rows
+def packed(sizes, lanes):
+    places, row, lane = [], 0, 0
+    for size in sizes:
+        if lane + size > lanes:
+            row, lane = row + 1, 0
+        places.append((row, lane))
+        lane += size
+    return places
+
+
+def finish_kernel(counts, sizes, places, lanes_ok, *refs):
+    over_chips, over_rows, opened = sizes
+    total_count = over_chips + over_rows + opened
     refs = list(refs)
 
     def take(number):
@@ -340,13 +349,16 @@
         del refs[:number]
         return found
 
-    dqkv_ref, own_ref = take(2)
-    done_in, open_in = take(done), take(opened)
-    tokens_ref, own_out = take(2)
-    outs = take(done + opened)
-    own_slots, own_sum, own_block = take(3)
+    dqkv_ref, normed_in, inputs_ref, gain_ref, weight_in, part_ref = take(6)
+    vectors_in = take(len(places) - 2)
+    chips_in, rows_in, open_in = take(over_chips), take(over_rows), take(opened)
+    grad_out, vectors_out, part_out, own_out = take(4)
+    outs = take(total_count)
+    tokens_ref, weight_ref, normed_ref, dqkv_here = take(4)
+    vectors_ref, vector_slots, vector_sum = take(3)
+    own_ref, own_slots, own_sum, own_block = take(4)
     row_slots, row_sum = take(over_rows + opened), take(over_rows + opened)
-    chip_slots, chip_sum = take(done + opened), take(done + opened)
+    chip_slots, chip_sum = take(total_count), take(total_count)
     load_sem, *sems = take(4)
     greet(("seq", "rows"), counts)
     number = 0
@@ -377,14 +389,13 @@
         move(ref, slots, "rows", columns_of(slots.shape[2]), lead)
         for ref, slots in zip(open_in, row_slots[over_rows:])
     ]
-    own_rows = move(own_ref, own_slots, "rows", second_dim, lead)
-    for item in home + open_rows + [own_rows]:
+    for item in open_rows:
         item.start()
+    sources = [*chips_in, *rows_in, dqkv_ref, normed_in, weight_in]
+    targets = [*chip_slots[:over_chips], *row_slots[:over_rows], dqkv_here, normed_ref, weight_ref]
     loads = [
-        pltpu.make_async_copy(ref, slots, load_sem.at[index])
-        for index, (ref, slots) in enumerate(
-            zip(done_in, chip_slots[:over_chips] + row_slots[:over_rows])
-        )
+        pltpu.make_async_copy(ref, there, load_sem.at[index])
+        for index, (ref, there) in enumerate(zip(sources, targets))
     ]
     for load in loads:
         load.start()
@@ -405,9 +416,22 @@
     for index in range(over_rows):
         loads[over_chips + index].wait()
         to_chips(index)
+    for item in home:
+        item.start()
     for index in range(over_chips):
         loads[index].wait()
         to_rows(index)
+    for load in loads[over_chips + over_rows :]:
+        load.wait()
+    own_grad = dot_left(dqkv_here[...], normed_ref[...]).T
+    own_ref[...] = low(own_grad).reshape(own_ref.shape)
+    own_rows = move(own_ref, own_slots, "rows", second_dim, lead)
+    own_rows.start()
+    for index, item in enumerate(open_rows):
+        item.arrived()
+        to_chips(over_rows + index)
+    last.append(move(part_ref, part_out, "chip", whole, lead))
+    last[-1].start()
     own_rows.arrived()
     own_sum[...] = add_slots(own_slots)
     if lanes_ok:
@@ -425,9 +449,43 @@
         own_chips = [move(own_sum, own_block, "seq", lead, lead)]
     for item in own_chips:
         item.start()
-    for index, item in enumerate(open_rows):
+    for item in home:
         item.arrived()
-        to_chips(over_rows + index)
+    if lanes_ok:
+        grad_tokens = tokens_ref[...]
+    else:
+        grad_tokens = jnp.concatenate(
+            [
+                tokens_ref[index, :, part * width : (part + 1) * width]
+                for part in range(3)
+                for index in range(count)
+            ],
+            axis=1,
+        )
+    normed_grad = dot_right(grad_tokens, weight_ref[...])
+    values = wide(inputs_ref[...])
+    center = values - jnp.mean(values, axis=-1, keepdims=True)
+    scale = lax.rsqrt(jnp.mean(center * center, axis=-1, keepdims=True) + EPSILON)
+    unit = center * scale
+    gain_grad = jnp.sum(normed_grad * unit, axis=0, keepdims=True)
+    shift_grad = jnp.sum(normed_grad, axis=0, keepdims=True)
+    normed_grad = normed_grad * gain_ref[...]
+    grad_out[...] = scale * (
+        normed_grad
+        - jnp.mean(normed_grad, axis=-1, keepdims=True)
+        - unit * jnp.mean(normed_grad * unit, axis=-1, keepdims=True)
+    )
+    vectors_ref[...] = jnp.zeros_like(vectors_ref)
+    for vector, (row, lane) in zip(
+        [gain_grad, shift_grad] + [ref[...] for ref in vectors_in], places
+    ):
+        size = vector.shape[1] // count
+        for index in range(count):
+            vectors_ref[index, row : row + 1, lane : lane + size] = vector[
+                :, index * size : (index + 1) * size
+            ]
+    vectors = move(vectors_ref, vector_slots, "seq", lead, lead)
+    vectors.start()
     for index, item in enumerate(chip_moves):
         item.arrived()
         to_rows(over_chips + index)
@@ -438,50 +496,89 @@
     else:
         last.append(move(own_block, own_out, "rows", whole, lead))
     last[-1].start()
-    for item in home + last:
+    vectors.arrived()
+    vector_sum[...] = functools.reduce(jnp.add, [vector_slots[i] for i in range(count)])
+    last.append(move(vector_sum, vectors_out, "rows", whole, lead))
+    last[-1].start()
+    for item in last:
         item.arrived()
-    for item in home + open_rows + [own_rows] + chip_moves + own_chips + last:
+    for item in home + open_rows + [own_rows, vectors] + chip_moves + own_chips + last:
         item.sent()
 
 
-def finish(dqkv, own_grad, over_chips, over_rows, rows_open, counts, collective_id):
+def finish(
+    dqkv,
+    normed,
+    inputs,
+    gain,
+    weight,
+    part,
+    vectors,
+    over_chips,
+    over_rows,
+    rows_open,
+    counts,
+    collective_id,
+):
     count, chips, rows = counts["seq"], counts["chip"], counts["rows"]
     length, all_width = dqkv.shape
+    features = inputs.shape[1]
     width = all_width // 3
     lanes_ok = width % 128 == 0
-    tokens, short = length // count, own_grad.shape[2]
-    bf = jnp.bfloat16
+    tokens, short = length // count, features // count // rows
+    bf, lanes = jnp.bfloat16, 512
     if lanes_ok:
         tokens_shape = (tokens, all_width * count)
         own_block, own_out = (short, all_width * count), (rows * short, all_width * count)
     else:
         tokens_shape = (count, tokens, all_width)
         own_block, own_out = (count, short, all_width), (rows, count, short, all_width)
+    pieces = [features // count] * 2 + [vector.shape[1] // count for vector in vectors]
+    places = packed(pieces, lanes)
+    vector = (8, lanes)
     shares = [term.shape[1:] for term in over_rows]
     shares += [(term.shape[0], term.shape[1] // rows) for term in rows_open]
     blocks = [term.shape[1:] for term in over_chips]
     blocks += [(shape[0] // chips, shape[1]) for shape in shares]
-    outs = [tokens_shape, own_out] + [(shape[0], shape[1] * rows) for shape in blocks]
-    own_share = own_grad.shape[:1] + own_grad.shape[2:]
-    scratch = [(rows,) + own_share, own_share, own_block]
+    outs = [own_out] + [(shape[0], shape[1] * rows) for shape in blocks]
+    own_share = (count, short, all_width)
+    scratch = [(count, rows, short, all_width), (rows,) + own_share, own_share, own_block]
     scratch += [(rows,) + shape for shape in shares] + shares
     scratch += [(chips,) + shape for shape in blocks] + blocks
-    moves = 3 + 3 + 2 + len(rows_open) + len(shares) + len(blocks)
+    moves = 3 + 3 + 2 + 3 + len(rows_open) + len(shares) + len(blocks)
     longest = max(count, rows)
-    arrays = [dqkv, own_grad, *over_chips, *over_rows, *rows_open]
-    return pl.pallas_call(
+    vmem, anywhere = pl.BlockSpec(memory_space=pltpu.VMEM), pl.BlockSpec(memory_space=pl.ANY)
+    rest = [*over_chips, *over_rows, *rows_open]
+    found = pl.pallas_call(
         functools.partial(
             finish_kernel,
             counts,
-            ((len(over_chips), len(over_rows)), len(rows_open)),
+            (len(over_chips), len(over_rows), len(rows_open)),
+            places,
             lanes_ok,
         ),
-        out_shape=[jax.ShapeDtypeStruct(shape, bf) for shape in outs],
-        in_specs=[pl.BlockSpec(memory_space=pl.ANY)] * len(arrays),
-        out_specs=[pl.BlockSpec(memory_space=pl.ANY)] * len(outs),
-        scratch_shapes=[pltpu.VMEM(shape, bf) for shape in scratch]
+        out_shape=[
+            jax.ShapeDtypeStruct(inputs.shape, jnp.float32),
+            jax.ShapeDtypeStruct((rows,) + vector, jnp.float32),
+            jax.ShapeDtypeStruct((chips,) + part.shape, bf),
+        ]
+        + [jax.ShapeDtypeStruct(shape, bf) for shape in outs],
+        in_specs=[anywhere, anywhere, vmem, vmem, anywhere, anywhere]
+        + [vmem] * len(vectors)
+        + [anywhere] * len(rest),
+        out_specs=[vmem] + [anywhere] * (2 + len(outs)),
+        scratch_shapes=[
+            pltpu.VMEM(tokens_shape, bf),
+            pltpu.VMEM(weight.shape, bf),
+            pltpu.VMEM(normed.shape, bf),
+            pltpu.VMEM(dqkv.shape, bf),
+            pltpu.VMEM((count,) + vector, jnp.float32),
+            pltpu.VMEM((count,) + vector, jnp.float32),
+            pltpu.VMEM(vector, jnp.float32),
+        ]
+        + [pltpu.VMEM(shape, bf) for shape in scratch]
         + [
-            pltpu.SemaphoreType.DMA((len(over_chips) + len(over_rows),)),
+            pltpu.SemaphoreType.DMA((len(over_chips) + len(over_rows) + 3,)),
             pltpu.SemaphoreType.DMA((moves,)),
             pltpu.SemaphoreType.DMA((moves, longest)),
             pltpu.SemaphoreType.DMA((moves, longest)),
@@ -489,43 +586,24 @@
         compiler_params=pltpu.CompilerParams(
             collective_id=collective_id, has_side_effects=True, vmem_limit_bytes=VMEM_LIMIT
         ),
+    )(dqkv, normed, inputs, gain, weight, part, *vectors, *rest)
+    return found[0], found[1], [(r, lane, size) for (r, lane), size in zip(places, pieces)], found[2:]
+
+
+def widen_kernel(*refs):
+    for given, out in zip(refs[: len(refs) // 2], refs[len(refs) // 2 :]):
+        out[...] = wide(given[...])
+
+
+def widen(arrays):
+    vmem = pl.BlockSpec(memory_space=pltpu.VMEM)
+    return pl.pallas_call(
+        widen_kernel,
+        out_shape=[jax.ShapeDtypeStruct(array.shape, jnp.float32) for array in arrays],
+        in_specs=[vmem] * len(arrays),
+        out_specs=[vmem] * len(arrays),
+        compiler_params=pltpu.CompilerParams(vmem_limit_bytes=VMEM_LIMIT),
     )(*arrays)
-
-
-def vectors_kernel(counts, given_ref, out_ref, slots, total, own_sem, send_sem, recv_sem):
-    greet(("seq", "rows"), counts)
-    over_seq = Transfers(
-        (given_ref, slots, "seq", lead, lead), counts, own_sem.at[0], send_sem.at[0], recv_sem.at[0]
-    )
-    over_seq.start()
-    over_seq.arrived()
-    total[...] = functools.reduce(jnp.add, [slots[i] for i in range(slots.shape[0])])
-    over_rows = Transfers(
-        (total, out_ref, "rows", whole, lead), counts, own_sem.at[1], send_sem.at[1], recv_sem.at[1]
-    )
-    over_rows.start()
-    over_rows.arrived()
-    over_seq.sent()
-    over_rows.sent()
-
-
-def sum_vectors(given, counts, collective_id):
-    longest = max(counts["seq"], counts["rows"])
-    block = given.shape[1:]
-    return pl.pallas_call(
-        functools.partial(vectors_kernel, counts),
-        out_shape=jax.ShapeDtypeStruct((counts["rows"],) + block, jnp.float32),
-        in_specs=[pl.BlockSpec(memory_space=pl.ANY)],
-        out_specs=pl.BlockSpec(memory_space=pl.ANY),
-        scratch_shapes=[
-            pltpu.VMEM((counts["seq"],) + block, jnp.float32),
-            pltpu.VMEM(block, jnp.float32),
-            pltpu.SemaphoreType.DMA((2,)),
-            pltpu.SemaphoreType.DMA((2, longest)),
-            pltpu.SemaphoreType.DMA((2, longest)),
-        ],
-        compiler_params=pltpu.CompilerParams(collective_id=collective_id, has_side_effects=True),
-    )(given)
 
 
 def head_lanes(width):
@@ -616,9 +694,9 @@
 
 def self_backward_kernel(counts, hosted, *refs):
     size = len(hosted)
-    qkv_ref, out_ref, grad_ref, start_ref, stat_ref = refs[:5]
-    sent, dqkv_ref, stacks = refs[5 : 5 + size], refs[5 + size], refs[6 + size : 6 + 2 * size]
-    dk_ref, dv_ref, own_sem, send_sem, recv_sem = refs[6 + 2 * size :]
+    qkv_ref, out_ref, blocks_ref, slots_ref, start_ref, stat_ref = refs[:6]
+    sent, dqkv_ref, stacks = refs[6 : 6 + size], refs[6 + size], refs[7 + size : 7 + 2 * size]
+    dk_ref, dv_ref, grad_ref, own_sem, send_sem, recv_sem = refs[7 + 2 * size :]
     length, width = out_ref.shape
     heads = width // DEPTH
     blocks = length // BLOCK
@@ -633,6 +711,12 @@
         moves[-1].start()
     dk_ref[...] = jnp.zeros_like(dk_ref)
     dv_ref[...] = jnp.zeros_like(dv_ref)
+    grad_ref[...] = blocks_ref[...]
+    slots = add_slots(slots_ref)
+    in_front = lax.broadcasted_iota(jnp.int32, slots.shape, 0) < start_ref[PAGES]
+    nothing = jnp.zeros_like(slots)
+    grad_ref[0:SLOTS, :] += jnp.where(in_front, slots, nothing)
+    grad_ref[length - SLOTS : length, :] += jnp.where(in_front, nothing, slots)
 
     def query_block(index, carry):
         rows = pl.ds(pl.multiple_of(index * BLOCK, BLOCK), BLOCK)
@@ -685,7 +769,9 @@
         item.sent()
 
 
-def self_backward(qkv, out, grad, starts, stats, sent, hosted, counts, collective_id):
+def self_backward(
+    qkv, out, grad, slots, starts, stats, sent, hosted, counts, collective_id
+):
     length, width = out.shape
     stacks = []
     for array, (axis, how) in zip(sent, hosted):
@@ -698,11 +784,13 @@
     return pl.pallas_call(
         functools.partial(self_backward_kernel, counts, hosted),
         out_shape=[jax.ShapeDtypeStruct((length, 3 * width), jnp.bfloat16), *stacks],
-        in_specs=[vmem, vmem, vmem, pl.BlockSpec(memory_space=pltpu.SMEM), vmem]
+        in_specs=[vmem] * 4
+        + [pl.BlockSpec(memory_space=pltpu.SMEM), vmem]
         + [anywhere] * len(sent),
         out_specs=[vmem] + [anywhere] * len(sent),
         scratch_shapes=[pltpu.VMEM((length, width), jnp.float32)] * 2
         + [
+            pltpu.VMEM((length, width), jnp.bfloat16),
             pltpu.SemaphoreType.DMA((len(sent),)),
             pltpu.SemaphoreType.DMA((len(sent), longest)),
             pltpu.SemaphoreType.DMA((len(sent), longest)),
@@ -710,7 +798,7 @@
         compiler_params=pltpu.CompilerParams(
             collective_id=collective_id, has_side_effects=True, vmem_limit_bytes=VMEM_LIMIT
         ),
-    )(qkv, out, grad, starts, stats, *sent)
+    )(qkv, out, grad, slots, starts, stats, *sent)
 
 
 def cross_forward_kernel(query_ref, key_ref, value_ref, own_key_ref, own_value_ref, out_ref, stat_ref):
@@ -759,6 +847,7 @@
 
 
 def cross_backward_kernel(
+    counts,
     query_ref,
     key_ref,
     value_ref,
@@ -767,12 +856,28 @@
     out_ref,
     grad_ref,
     stat_ref,
+    sent_ref,
     dq_ref,
     dk_ref,
     dv_ref,
     own_dk_ref,
     own_dv_ref,
+    stack_ref,
+    own_sem,
+    send_sem,
+    recv_sem,
 ):
+    step, steps = pl.program_id(0), pl.num_programs(0)
+
+    def move():
+        part = (sent_ref, stack_ref, "chip", rows_of(stack_ref.shape[1]), lead)
+        return Transfers(part, counts, own_sem, send_sem, recv_sem)
+
+    @pl.when(step == 0)
+    def _():
+        greet(("chip",), counts)
+        move().start()
+
     tokens = query_ref.shape[0] - SLOTS
     width = query_ref.shape[1]
     row = lax.broadcasted_iota(jnp.int32, (PAGE_PAD, 1), 0)
@@ -803,8 +908,14 @@
         dk_out[...] = low(dk_sum)
         dv_out[...] = low(dv_sum)
 
-
-def cross_backward(query, kv_big, kv_own, out, grad, stats):
+    @pl.when(step == steps - 1)
+    def _():
+        found = move()
+        found.arrived()
+        found.sent()
+
+
+def cross_backward(query, kv_big, kv_own, out, grad, stats, sent, counts, collective_id):
     rows, features = query.shape
     pair = 2 * DEPTH
     steps = features // pair
@@ -812,10 +923,22 @@
     keys = pl.BlockSpec((PAGE_PAD, pair), lambda i: (0, i))
     values = pl.BlockSpec((PAGE_PAD, pair), lambda i: (0, i + steps))
     page = jax.ShapeDtypeStruct((PAGE_PAD, features), jnp.bfloat16)
+    chips = counts["chip"]
+    stack = jax.ShapeDtypeStruct(
+        (chips, sent.shape[0] // chips, sent.shape[1]), jnp.bfloat16
+    )
+    anywhere = pl.BlockSpec(memory_space=pl.ANY)
     return pl.pallas_call(
-        cross_backward_kernel,
+        functools.partial(cross_backward_kernel, counts),
         grid=(steps,),
-        out_shape=(jax.ShapeDtypeStruct((rows, features), jnp.bfloat16), page, page, page, page),
+        out_shape=(
+            jax.ShapeDtypeStruct((rows, features), jnp.bfloat16),
+            page,
+            page,
+            page,
+            page,
+            stack,
+        ),
         in_specs=[
             tall,
             keys,
@@ -825,10 +948,18 @@
             tall,
             tall,
             pl.BlockSpec((1, 2, rows), lambda i: (i, 0, 0)),
+            anywhere,
         ],
-        out_specs=[tall, keys, keys, keys, keys],
-        compiler_params=pltpu.CompilerParams(vmem_limit_bytes=VMEM_LIMIT),
-    )(query, kv_big, kv_big, kv_own, kv_own, out, grad, stats)
+        out_specs=[tall, keys, keys, keys, keys, anywhere],
+        scratch_shapes=[
+            pltpu.SemaphoreType.DMA,
+            pltpu.SemaphoreType.DMA((chips,)),
+            pltpu.SemaphoreType.DMA((chips,)),
+        ],
+        compiler_params=pltpu.CompilerParams(
+            collective_id=collective_id, has_side_effects=True, vmem_limit_bytes=VMEM_LIMIT
+        ),
+    )(query, kv_big, kv_big, kv_own, kv_own, out, grad, stats, sent)
 
 
 def body(
@@ -867,20 +998,21 @@
     counts = {"seq": count, "chip": count // 2, "rows": rows_count}
     core = me % 2
 
-    def pair_sum(first, second):
+    def blocks_of(first, which):
         size = first.shape[1] // count
-
-        def blocks_of(which):
-            return jnp.concatenate(
-                [
-                    lax.dynamic_slice_in_dim(first, (2 * chip + which) * size, size, 1)
-                    for chip in range(count // 2)
-                ],
-                axis=1,
-            )
-
-        given = swap(low(dot_left(blocks_of(1 - core), second)))
-        return low(dot_left(blocks_of(core), second) + wide(given))
+        return jnp.concatenate(
+            [
+                lax.dynamic_slice_in_dim(first, (2 * chip + which) * size, size, 1)
+                for chip in range(count // 2)
+            ],
+            axis=1,
+        )
+
+    def pair_sum(first, second, behind=None):
+        given = swap(low(dot_left(blocks_of(first, 1 - core), second)))
+        if behind is not None:
+            given = after(given, behind)
+        return low(dot_left(blocks_of(first, core), second) + wide(given))
 
     def swap(value):
         return lax.ppermute(value, "seq", [(i, i ^ 1) for i in range(count)])
@@ -898,7 +1030,7 @@
 
     starts = jnp.sum(row_segs[None, :] < jnp.arange(PAGES)[:, None], axis=1, dtype=jnp.int32)
     big_page = row_segs[length // 2]
-    big_start = jnp.sum(row_segs < big_page)
+    big_start = jnp.sum(row_segs < big_page, dtype=jnp.int32)
     own_page = lax.dynamic_index_in_dim(row_pages, me // sharers, 0, keepdims=False)
     slot = jnp.arange(SLOTS)
     in_front = (slot < big_start)[:, None]
@@ -929,7 +1061,7 @@
     end_grad = jnp.where(core == 0, out_grad[0, :SLOTS], out_grad[0, tokens - SLOTS :])
     sent = jnp.concatenate((pair_page, jnp.where(at_end, end_grad, jnp.zeros_like(end_grad))))
     same_core = [[2 * chip + which for chip in range(count // 2)] for which in range(2)]
-    mine = lax.psum(after(sent, x_all), "seq", axis_index_groups=same_core)
+    mine = lax.psum(sent, "seq", axis_index_groups=same_core)
     theirs = swap(mine)
     zeroth, first = jnp.where(core == 0, mine, theirs), jnp.where(core == 0, theirs, mine)
     mem_big = jnp.concatenate((zeroth[:half], first[:half]))
@@ -1006,14 +1138,15 @@
     grad_act = dot_right(grad_out, fc2_weight)
     _, gelu_pull = jax.vjp(gelu_exact, pre_act)
     grad_pre = low(gelu_pull(grad_act)[0])
-    grad_fc2_w = pair_sum(hidden_act, grad_out)
+    grad_fc2_b = jnp.sum(wide(grad_out), axis=0)
+    grad_fc2_w = pair_sum(hidden_act, grad_out, grad_pre)
     fc2_share = lax.psum_scatter(grad_fc2_w, "rows", scatter_dimension=1, tiled=True)
-    grad_fc2_b = jnp.sum(wide(grad_out), axis=0)
-    grad_fc1_w = pair_sum(normed_three, grad_pre)
+    grad_normed_three = dot_right(grad_pre, fc1_weight)
+    grad_fc1_w = pair_sum(normed_three, grad_pre, grad_normed_three)
     fc1_share = lax.psum_scatter(grad_fc1_w, "rows", scatter_dimension=1, tiled=True)
     grad_fc1_b = jnp.sum(wide(grad_pre), axis=0)
     grad_two_norm, grad_gain_three, grad_shift_three = norm_backward(
-        resid_two, gain_three, shift_three, dot_right(grad_pre, fc1_weight)
+        resid_two, gain_three, shift_three, grad_normed_three
     )
     grad_resid_two = wide(grad_out) + grad_two_norm
     grad_branch_two = low(grad_resid_two)
@@ -1021,8 +1154,8 @@
     grad_co_b = jnp.sum(wide(grad_branch_two), axis=0)
     grad_cross_low = low(dot_right(grad_branch_two, cross_out_weight))
     grad_cross_low = after(grad_cross_low, (grad_fc1_w, grad_fc2_w))
-    grad_cross_q, big_dk, big_dv, own_dk, own_dv = cross_backward(
-        cross_queries, kv_big, kv_own, cross_low, grad_cross_low, cross_stats
+    grad_cross_q, big_dk, big_dv, own_dk, own_dv, fc2_stack = cross_backward(
+        cross_queries, kv_big, kv_own, cross_low, grad_cross_low, cross_stats, fc2_share, counts, 5
     )
     grad_cq_w = pair_sum(normed_two, grad_cross_q)
     grad_cq_b = jnp.sum(wide(grad_cross_q), axis=0)
@@ -1063,52 +1196,55 @@
         counts,
         2,
     )
-    slots_grad = low(jnp.sum(wide(slots_grad), axis=0))
-    no_slots = jnp.zeros_like(slots_grad)
-    grad_mixed = jnp.concatenate(
-        (
-            grad_mixed[:SLOTS] + jnp.where(in_front, slots_grad, no_slots),
-            grad_mixed[SLOTS : length - SLOTS],
-            grad_mixed[length - SLOTS :] + jnp.where(in_front, no_slots, slots_grad),
-        )
-    )
     dqkv, *stacks = self_backward(
         qkv,
         mixed,
         grad_mixed,
-        starts,
+        slots_grad,
+        jnp.concatenate((starts, big_start[None])),
         mixed_stats,
-        (fc2_share, fc1_share, grad_co_w, grad_cq_w, grad_o_w),
-        (("chip", "rows"), ("chip", "rows")) + (("rows", "columns"),) * 3,
+        (fc1_share, grad_co_w, grad_cq_w, grad_o_w),
+        (("chip", "rows"),) + (("rows", "columns"),) * 3,
         counts,
         3,
     )
 
     slot_final = jnp.where(active[tokens:], final[tokens:], jnp.zeros_like(final[tokens:]))
+    part_rows = PAGE_PAD // (count // 2)
     own_half = jnp.where(core == 0, big_dk, big_dv)
     own_half = own_half + swap(jnp.where(core == 0, big_dv, big_dk))
+    part = lax.psum_scatter(
+        after(own_half, (fc1_share, grad_mixed)), "seq", scatter_dimension=0, tiled=True, axis_index_groups=same_core
+    )
     slot_half = jnp.where(core == 0, slot_final, low(grad_resid_one[tokens:]))
     slot_half = slot_half + swap(jnp.where(core == 0, low(grad_resid_one[tokens:]), slot_final))
-    mine = lax.psum(
-        jnp.concatenate((own_half[:PAGE_TOK], slot_half)), "seq", axis_index_groups=same_core
-    )
-    mine = after(mine, dqkv)
-    theirs = swap(mine)
-    zeroth, first = jnp.where(core == 0, mine, theirs), jnp.where(core == 0, theirs, mine)
-    big_dk, big_dv = zeroth[:PAGE_TOK], first[:PAGE_TOK]
-    slot_final, slot_grad = zeroth[PAGE_TOK:], first[PAGE_TOK:]
-    grad_ckv = jnp.where(
-        gives_big,
-        jnp.concatenate((big_dk, big_dv), axis=1),
-        jnp.concatenate((own_dk[:PAGE_TOK], own_dv[:PAGE_TOK]), axis=1),
-    )
+    slot_half = lax.psum(after(slot_half, part), "seq", axis_index_groups=same_core)
+    grad_ckv = jnp.concatenate((own_dk[:PAGE_TOK], own_dv[:PAGE_TOK]), axis=1)
     if sharers > 1:
         grad_ckv = lax.psum_scatter(
             grad_ckv, "seq", scatter_dimension=0, tiled=True, axis_index_groups=groups
         )
-    grad_ckv_w = pair_sum(mem_own, grad_ckv)
-    grad_cv_b = jnp.sum(wide(grad_ckv[:, features:]), axis=0)
-    memory_grad = dot_right(grad_ckv, cross_kv_weight)[None]
+    part = after(part, dqkv)
+    nothing = jnp.zeros_like(part)
+    part_wide = jnp.concatenate(
+        (jnp.where(core == 0, part, nothing), jnp.where(core == 0, nothing, part)), axis=1
+    )
+    part_memory = lax.dynamic_slice_in_dim(mem_big, me // 2 * part_rows, part_rows, 0)
+
+    def ckv_terms(which):
+        return dot_left(blocks_of(mem_own, which), grad_ckv) + dot_left(
+            blocks_of(part_memory, which), part_wide
+        )
+
+    grad_ckv_w = low(ckv_terms(core) + wide(swap(low(ckv_terms(1 - core)))))
+    grad_cv_b = jnp.sum(wide(grad_ckv[:, features:]), axis=0) + jnp.sum(
+        wide(part_wide[:, features:]), axis=0
+    )
+    half_weight = lax.dynamic_slice_in_dim(cross_kv_weight, core * features, features, 1)
+    part_grad = dot_right(part, half_weight)
+    part_grad = part_grad.reshape(2, part_rows // 2, features)
+    part_grad = low(part_grad[core] + swap(part_grad[1 - core]))
+    memory_grad = dot_right(grad_ckv, cross_kv_weight)
 
     def at_home(own, returned):
         front = is_first & in_front
@@ -1117,11 +1253,7 @@
         tail = jnp.where(back, returned.astype(own.dtype), own[tokens - SLOTS :])
         return jnp.concatenate((head, own[SLOTS : tokens - SLOTS], tail))
 
-    layer_out = at_home(final[:tokens], slot_final)[None]
-    grad_home = at_home(grad_resid_one[:tokens], slot_grad)
-
-    grad_qkv_w = low(dot_left(normed_all, dqkv))
-    grad_qkv_w = grad_qkv_w.reshape(count, rows_count, -1, 3 * width)
+
     column_sums = jnp.sum(wide(dqkv), axis=0)
 
     def in_features(part):
@@ -1134,25 +1266,7 @@
 
     grad_qv_b = jnp.concatenate((in_features(0), in_features(2)))
 
-    grad_qkv, qkv_w, fc2_w, fc1_w, co_w, cq_w, o_w, ckv_w = finish(
-        dqkv, grad_qkv_w, stacks[:2], stacks[2:], (grad_ckv_w,), counts, 4
-    )
-    if not lanes_ok:
-        grad_qkv = grad_qkv.reshape(count, tokens, 3, width).transpose(1, 2, 0, 3)
-        grad_qkv = grad_qkv.reshape(tokens, 3 * features)
-        qkv_w = qkv_w.reshape(rows_count, count, -1, 3, width).transpose(0, 2, 3, 1, 4)
-        qkv_w = qkv_w.reshape(-1, 3 * features)
-    qkv_w, fc1_w, fc2_w, o_w, cq_w, co_w, ckv_w = [
-        wide(term) for term in (qkv_w, fc1_w, fc2_w, o_w, cq_w, co_w, ckv_w)
-    ]
-    grad_in_norm, grad_gain_one, grad_shift_one = norm_backward(
-        wide(x_own), gain_one, shift_one, dot_right(grad_qkv, qkv_weight)
-    )
-    input_grad = (grad_home + grad_in_norm)[None]
-
     vectors = (
-        grad_gain_one,
-        grad_shift_one,
         grad_qv_b,
         grad_o_b,
         grad_gain_two,
@@ -1165,14 +1279,43 @@
         grad_fc1_b,
         grad_fc2_b,
     )
-    joined = jnp.concatenate([vector.reshape(count, -1) for vector in vectors], axis=1)
-    joined = jnp.pad(joined, ((0, 0), (0, -joined.shape[1] % 1024))).reshape(count, 8, -1)
-    joined = jnp.sum(sum_vectors(joined, counts, 5), axis=0).reshape(-1)
-    pieces, offset = [], 0
-    for vector in vectors:
-        size = vector.shape[0] // count
-        pieces.append(joined[offset : offset + size])
-        offset += size
+    grad_in_norm, joined, places, sums = finish(
+        dqkv,
+        normed_all,
+        x_own,
+        gain_one[None, :],
+        qkv_weight,
+        part_grad,
+        [vector[None, :] for vector in vectors],
+        (fc2_stack, stacks[0]),
+        stacks[1:],
+        (grad_ckv_w,),
+        counts,
+        4,
+    )
+    big_grad, qkv_w, fc2_w, fc1_w, co_w, cq_w, o_w, ckv_w = sums
+    if not lanes_ok:
+        qkv_w = qkv_w.reshape(rows_count, count, -1, 3, width).transpose(0, 2, 3, 1, 4)
+        qkv_w = qkv_w.reshape(-1, 3 * features)
+    qkv_w, fc1_w, fc2_w, o_w, cq_w, co_w, ckv_w = widen(
+        (qkv_w, fc1_w, fc2_w, o_w, cq_w, co_w, ckv_w)
+    )
+    joined = jnp.sum(joined, axis=0)
+    slot_half = after(slot_half, joined)
+    theirs = swap(slot_half)
+    slot_final, slot_grad = (
+        jnp.where(core == 0, slot_half, theirs),
+        jnp.where(core == 0, theirs, slot_half),
+    )
+    layer_out = at_home(final[:tokens], slot_final)[None]
+    input_grad = (at_home(grad_resid_one[:tokens], slot_grad) + grad_in_norm)[None]
+    big_other = swap(big_grad)
+    big_grad = jnp.stack(
+        (jnp.where(core == 0, big_grad, big_other), jnp.where(core == 0, big_other, big_grad)), axis=1
+    ).reshape(PAGE_PAD, features)
+    big_grad = lax.dynamic_slice_in_dim(big_grad, me % sharers * mem_rows, mem_rows, 0)
+    memory_grad = jnp.where(own_page == big_page, memory_grad + wide(big_grad), memory_grad)[None]
+    pieces = [joined[row, lane : lane + size] for row, lane, size in places]
     g1, s1, qvb, ob, g2, s2, cqb, cvb, cob, g3, s3, f1b, f2b = pieces
     return (
         layer_out,

time: 584 us -> 574 us (0.983)
  waiting for transfers between devices: 50 us -> 19 us
  other arithmetic: 50.9 us -> 65.3 us
  Pallas kernels: 299 us -> 308 us
    psum x2, waiting for transfers between devices: 36.3 us -> 0.03 us  [the longest x1 0.02 us: body(): mine = lax.psum(sent, 'seq', axis_index_groups=same_core)]
    pallas_call x3, Pallas kernels: 118 us -> 139 us  [the longest x1 109 us: finish(): pl.pallas_call(functools.partial(finish_kernel, counts, (len(over_chips),...]
    pallas_call x1, Pallas kernels: 64 us -> 43.3 us  [self_backward(): pl.pallas_call(functools.partial(self_backward_kernel, counts, hosted), o...]
    reduce_scatter x1, waiting for transfers between devices: 0.01 us -> 18.5 us  [body(): lax.psum_scatter(grad_fc2_w, 'rows', scatter_dimension=1, tiled=True)]
    ppermute x11 -> x13, waiting for transfers between devices: 13.6 us -> 0.3 us  [swap(): return lax.ppermute(value, 'seq', [(i, i ^ 1) for i in range(count)])]
    select_n x2, other arithmetic: 2.74 us -> 11.9 us  [slots_of(): return jnp.where(in_front, front, back)]
    convert_element_type x19 -> x12, other arithmetic: 9.18 us -> 0.05 us  [wide(): return values.astype(jnp.float32)]
    pallas_call x2, Pallas kernels: 45.8 us -> 53.9 us  [exchange(): pl.pallas_call(functools.partial(exchange_kernel, counts, len(arrays), pa...]
  transfers between devices with their start and end apart: 15 -> 18, of which waited for: 4 -> 2; matrix products, arithmetic and copies ran while one was open for 21% -> 26% of each run, Pallas kernels for 32% -> 51%
where the time goes in v4:
time: 574 us; the launch traced here: 572 us
  Pallas kernels  308 us (54%)
  matrix products  126 us (22%)
  other arithmetic  65.3 us (11%)
  local copies, waits for them, and re-layouts  32.6 us (6%)
  waiting for transfers between devices  19 us (3%)
  between operations  16.7 us (3%)
    pallas_call x1, Pallas kernels, finish(): pl.pallas_call(functools.partial(finish_kernel, counts, (len(over_chips),...  109 us
    pallas_call x2, Pallas kernels, exchange(): pl.pallas_call(functools.partial(exchange_kernel, counts, len(arrays), pa...  53.9 us
    dot_general x8, matrix products, dot_plain(): return jnp.dot(first, second, preferred_element_type=jnp.float32)  50.8 us
    pallas_call x1, Pallas kernels, gather_rows(): pl.pallas_call(functools.partial(gather_kernel, count), out_shape=jax.Sha...  44.6 us
    pallas_call x1, Pallas kernels, self_backward(): pl.pallas_call(functools.partial(self_backward_kernel, counts, hosted), o...  43.3 us
    dot_general x14, matrix products, dot_left(): lax.dot_general(first, second, (((0,), (0,)), ((), ())), preferred_elemen...  42.4 us
    dot_general x7, matrix products, dot_right(): lax.dot_general(first, second, (((1,), (1,)), ((), ())), preferred_elemen...  32.3 us
    pallas_call x1, Pallas kernels, cross_backward(): pl.pallas_call(functools.partial(cross_backward_kernel, counts), grid=(st...  23.9 us
  transfers between devices with their start and end apart: 18, of which 2 were waited for; matrix products, arithmetic and copies ran while one was open for 26% of the time, Pallas kernels for 51%

profile of v4, /device:TPU:0, one launch (start us, length us, event | category | flops | bytes accessed | tf_op | source)
XLA Modules:
  0.0 572.1 jit_solution(4732649146030234016)
XLA Ops:
  14.1 44.6 %shard_map.416 = bf16[2048,1024]{1,0:T(8,128)(2,1)} custom-call(bf16[256,1024]{1,0:T(8,128)(2,1)} %bitcast.133), custom_call_target="tpu_custom_call" | custom-call | tf_op jit(solution)/shard_map/pallas_call | solution.py:169
  58.7 3.0 convert_reduce_fusion
  67.4 4.5 fusion.5.refs_1_
  74.7 5.9 %add_convert_fusion.7.qkv_ref.refs_0_ = bf16[2048,384]{1,0:T(8,128)(2,1)} fusion(bf16[2048,1024]{1,0:T(8,128)(2,1)} %fusion.5.refs_1_, f32[384]{0:T(512)S(1)} %maximum_convert_fusion, bf16[1024,128]{1,0:T(8,128)(2,1)} %get-tuple-element.199, bf16[1024,128]{1,0:T(8,128)(2,1)} %get-tuple-element.198, bf16[1024,128]{1,0:T(8,128)(2,1)} %get-tuple-element.197), kind=kOutput, calls=%fused_computation.37 | convolution fusion | flops 1614544896 | bytes 6555136 | tf_op jit(solution)/shard_map/dot_general | solution.py:42
  81.4 12.0 %shard_map.417 = (bf16[2048,128]{1,0:T(8,128)(2,1)}, f32[2,2048]{1,0:T(2,128)}) custom-call(bf16[2048,384]{1,0:T(8,128)(2,1)} %add_convert_fusion.7.qkv_ref.refs_0_, s32[8]{0:T(128)} %convert_reduce_fusion.9.start_ref), custom_call_target="tpu_custom_call" | custom-call | tf_op jit(solution)/shard_map/pallas_call | solution.py:680
  95.3 10.6 %slice_select_fusion.5.refs_1_ = bf16[128,128]{1,0:T(8,128)(2,1)} fusion(bf16[2048,128]{1,0:T(8,128)(2,1)} %get-tuple-element.66.refs_0_.refs_1_, pred[128]{0:T(512)(128)(4,1)S(1)} %iota_compare_fusion.1), kind=kLoop, calls=%fused_computation.253 | loop fusion | flops 16384 | bytes 98432 | tf_op jit(solution)/shard_map/jit(_where)/select_n | solution.py:1044
  105.9 29.6 %shard_map.418 = (bf16[256,1024]{1,0:T(8,128)(2,1)}, bf16[128,1024]{1,0:T(8,128)(2,1)}) custom-call(bf16[2048,128]{1,0:T(8,128)(2,1)} %get-tuple-element.66.refs_0_.refs_1_, bf16[128,128]{1,0:T(8,128)(2,1)} %slice_select_fusion.5.refs_1_), custom_call_target="tpu_custom_call" | custom-call | tf_op jit(solution)/shard_map/pallas_call | solution.py:312
  138.8 6.5 %add_convert_fusion.3.own_key_ref.own_value_ref = bf16[640,2048]{1,0:T(8,128)(2,1)} fusion(bf16[1024,2048]{1,0:T(8,128)(2,1)} %param.40, f32[2048]{0:T(1024)S(1)} %pad_convert_fusion, bf16[588,1024]{1,0:T(8,128)(2,1)S(1)} %bitcast.125), kind=kOutput, calls=%fused_computation.30 | convolution fusion | flops 2686976000 | bytes 8028160 | tf_op jit(solution)/shard_map/dot_general | solution.py:42
  150.8 4.7 add_convert_fusion.4.key_ref.value_ref
  157.7 15.2 %shard_map.419 = (bf16[384,1024]{1,0:T(8,128)(2,1)}, f32[8,2,384]{2,1,0:T(2,128)}) custom-call(bf16[384,1024]{1,0:T(8,128)(2,1)} %add_convert_fusion.13.query_ref, bf16[640,2048]{1,0:T(8,128)(2,1)} %add_convert_fusion.4.key_ref.value_ref, bf16[640,2048]{1,0:T(8,128)(2,1)} %add_convert_fusion.4.key_ref.value_ref, ...), custom_call_target="tpu_custom_call" | custom-call | tf_op jit(solution)/shard_map/pallas_call | solution.py:836
  176.7 20.4 %multiply_convert_fusion = (bf16[384,4096]{1,0:T(8,128)(2,1)S(1)}, f32[384,4096]{1,0:T(8,128)}, f32[384,4096]{1,0:T(8,128)}) fusion(f32[4096]{0:T(1024)S(1)} %convert_element_type.207, bf16[384,1024]{1,0:T(8,128)(2,1)S(1)} %add_convert_fusion.12, bf16[1024,4096]{1,0:T(8,128)(2,1)} %param.46), kind=kOutput, calls=%fused_computation.14 | convolution fusion | flops 3325034496 | bytes 24920064 | tf_op jit(solution)/shard_map/dot_general | solution.py:42
  198.8 4.4 convolution_convert_fusion.1
  203.6 12.5 %convert_reduce_fusion.1 = (f32[4096]{0:T(1024)}, bf16[384,4096]{1,0:T(8,128)(2,1)}) fusion(f32[384,4096]{1,0:T(8,128)} %get-tuple-element.196, f32[384,4096]{1,0:T(8,128)} %get-tuple-element.284, bf16[4096,1024]{1,0:T(8,128)(2,1)S(1)} %bitcast.154, bf16[128,1024]{1,0:T(8,128)(2,1)S(1)} %get-tuple-element.278, bf16[256,1024]{1,0:T(8,128)(2,1)S(1)} %bitcast.127, ...), kind=kOutput, calls=%fused_computation.12 | convolution fusion | flops 3248353280 | bytes 24920448 | tf_op jit(solution)/shard_map/dot_general | solution.py:52
  216.1 4.4 add_convert_fusion
  222.4 4.4 convolution_convert_fusion
  229.4 8.9 %multiply_reduce_fusion = (f32[1024]{0:T(1024)}, f32[384]{0:T(512)S(1)}, f32[1024]{0:T(1024)}, f32[384,1024]{1,0:T(8,128)}) fusion(f32[384,1024]{1,0:T(8,128)S(1)} %copy-done.3, f32[384]{0:T(512)S(1)} %fusion.146, f32[384]{0:T(512)S(1)} %broadcast_multiply_fusion.1, f32[1024]{0:T(1024)S(1)} %convert_element_type.204, bf16[384,4096]{1,0:T(8,128)(2,1)S(1)} %copy-done.9, ...), kind=kOutput, calls=%fused_computation.82 | convolution fusion | flops 3224368640 | bytes 14696960 | tf_op jit(solution)/shard_map/dot_general | solution.py:52
  238.2 5.7 add_convert_fusion.1
  255.6 18.5 %reduce-scatter.4.cloned.1.call-done.sent_ref = bf16[2048,256]{1,0:T(8,128)(2,1)} async-done(((bf16[2048,1024]{1,0:T(8,128)(2,1)}), bf16[2048,256]{1,0:T(8,128)(2,1)}) %reduce-scatter.4.cloned.1.call-update) | async-done | bytes 1048592 | tf_op jit(solution)/shard_map/reduce_scatter | solution.py:1143
  274.2 23.9 %shard_map.420 = (bf16[384,1024]{1,0:T(8,128)(2,1)}, bf16[640,1024]{1,0:T(8,128)(2,1)}, bf16[640,1024]{1,0:T(8,128)(2,1)}, bf16[640,1024]{1,0:T(8,128)(2,1)}, bf...) custom-call(bf16[384,1024]{1,0:T(8,128)(2,1)} %add_convert_fusion.13.query_ref, ...), custom_call_target="tpu_custom_call" | custom-call | tf_op jit(solution)/shard_map/pallas_call | solution.py:931
  298.0 2.9 broadcast_select_fusion
  309.5 24.3 %shard_map.421 = (bf16[2048,128]{1,0:T(8,128)(2,1)}, bf16[8,128,128]{2,1,0:T(8,128)(2,1)}) custom-call(bf16[384,1024]{1,0:T(8,128)(2,1)} %convolution_convert_fusion.5.refs_0_), custom_call_target="tpu_custom_call" | custom-call | tf_op jit(solution)/shard_map/pallas_call | solution.py:312
  333.9 3.0 select_add_fusion
  337.1 8.1 %add_convert_fusion.11 = bf16[384,1024]{1,0:T(8,128)(2,1)S(1)} fusion(f32[384,1024]{1,0:T(8,128)} %copy-done.2, bf16[384,4096]{1,0:T(8,128)(2,1)} %copy-done.20, bf16[4096,1024]{1,0:T(8,128)(2,1)} %param.48, f32[1024]{0:T(1024)S(1)} %convert_element_type.209), kind=kOutput, calls=%fused_computation.90 | convolution fusion | flops 3222405120 | bytes 13897728 | tf_op jit(solution)/shard_map/dot_general | solution.py:42
  351.0 3.0 add_convert_fusion.10.refs_7_
  356.8 3.8 fusion.39
  364.1 43.3 %shard_map.422 = (bf16[2048,384]{1,0:T(8,128)(2,1)}, bf16[4,128,1024]{2,1,0:T(8,128)(2,1)}, bf16[4,512,256]{2,1,0:T(8,128)(2,1)}, bf16[4,512,256]{2,1,0:T(8,128)(2,1)}, bf16[4,512,256]{2,1,0:T(8,128)(2,1)}) custom-call(bf16[2048,384]{1,0:T(8,128)(2,1)} %add_convert_fusion.7.qkv_ref.refs_0_, bf16[2048,128]{1,0:T(8,128)(2,1)} %get-tuple-element.66.refs_0_.refs_1_, ...), custom_call_target="tpu_custom_call" | custom-call | tf_op jit(solution)/shard_map/pallas_call | solution.py:784
  408.7 4.5 add_convert_fusion.6
  414.8 3.8 fusion.40
  429.1 5.0 add_convert_fusion.5.refs_22_
  434.1 109.4 %shard_map.423 = (f32[256,1024]{1,0:T(8,128)}, f32[4,8,512]{2,1,0:T(8,128)}, bf16[4,80,1024]{2,1,0:T(8,128)(2,1)}, bf16[128,3072]{1,0:T(8,128)(2,1)}, bf16[512,1...) custom-call(bf16[2048,384]{1,0:T(8,128)(2,1)} %get-tuple-element.82., ...), custom_call_target="tpu_custom_call" | custom-call | tf_op jit(solution)/shard_map/pallas_call | solution.py:552
  546.7 5.7 shard_map.424
  561.5 3.9 copy.52
  (332 shorter events, 94.9 us)
Async XLA Ops:
  7.2 148.7 %copy-start = (bf16[1024,1024]{1,0:T(8,128)(2,1)S(1)}, bf16[1024,1024]{1,0:T(8,128)(2,1)}, u32[]{:S(2)}) copy-start(bf16[1024,1024]{1,0:T(8,128)(2,1)} %param.38) | copy-start | bytes 6291460
  7.2 6.8 %copy-start.76 = (bf16[1024]{0:T(1024)(128)(2,1)S(1)}, bf16[1024]{0:T(1024)(128)(2,1)}, u32[]{:S(2)}) copy-start(bf16[1024]{0:T(1024)(128)(2,1)} %param.30) | copy-start | bytes 6148
  7.2 6.8 %copy-start.77 = (bf16[1024]{0:T(1024)(128)(2,1)S(1)}, bf16[1024]{0:T(1024)(128)(2,1)}, u32[]{:S(2)}) copy-start(bf16[1024]{0:T(1024)(128)(2,1)} %param.31) | copy-start | bytes 6148
  7.2 130.3 %all-reduce.5.cloned.1.call-start = ((), (), s32[]{:S(2)}) async-start(), calls=%async_computation.3 | async-start | bytes 1835008 | tf_op jit(solution)/shard_map/psum | solution.py:1064
  13.6 58.4 %collective-permute-start = (bf16[320,1024]{1,0:T(8,128)(2,1)}, bf16[320,1024]{1,0:T(8,128)(2,1)}, u32[]{:S(2)}, u32[]{:S(2)}) collective-permute-start(bf16[320,1024]{1,0:T(8,128)(2,1)} %dynamic-slice_bitcast_fusion), channel_id=1, source_target_pairs={{0,1},{1,0},{2,3},{3,2},{4,5},{5,4},{6,7},{7,6},{8,9},{9,8},{10,11... | collective-permute-start | bytes 1966088 | tf_op jit(solution)/shard_map/ppermute | solution.py:1018
  14.0 53.4 %copy-start.71 = (f32[1024]{0:T(1024)}, f32[1024]{0:T(1024)S(1)}, u32[]{:S(2)}) copy-start(f32[1024]{0:T(1024)S(1)} %convert_element_type.189) | copy-start | bytes 12292
  74.1 200.0 %reduce-scatter.4.cloned.1.call-start = ((), (), s32[]{:S(2)}) async-start(), calls=%async_computation.4 | async-start | bytes 5242880 | tf_op jit(solution)/shard_map/reduce_scatter | solution.py:1143
  80.6 55.6 %copy-start.85 = (bf16[1024]{0:T(1024)(128)(2,1)S(1)}, bf16[1024]{0:T(1024)(128)(2,1)}, u32[]{:S(2)}) copy-start(bf16[1024]{0:T(1024)(128)(2,1)} %param.41) | copy-start | bytes 6148
  80.6 58.2 %copy-start.10 = (bf16[1,588,1024]{2,1,0:T(8,128)(2,1)S(1)}, bf16[1,588,1024]{2,1,0:T(8,128)(2,1)}, u32[]{:S(2)}) copy-start(bf16[1,588,1024]{2,1,0:T(8,128)(2,1)} %param.26) | copy-start | bytes 3612676
  137.5 7.8 %copy-start.73 = (pred[128]{0:T(512)(128)(4,1)}, pred[128]{0:T(512)(128)(4,1)S(1)}, u32[]{:S(2)}) copy-start(pred[128]{0:T(512)(128)(4,1)S(1)} %compare_and_fusion) | copy-start | bytes 388
  137.5 7.8 %collective-permute-start.1 = (bf16[448,1024]{1,0:T(8,128)(2,1)}, bf16[448,1024]{1,0:T(8,128)(2,1)S(1)}, u32[]{:S(2)}, u32[]{:S(2)}) collective-permute-start(bf16[448,1024]{1,0:T(8,128)(2,1)} %all-reduce.5.cloned.1.call-done), channel_id=1, source_target_pairs={{0,1},{1,0},{2,3},{3,2},{4,5},{5,4},{6,7},{7,6},{8,9},{9,8},{10,11... | collective-permute-start | bytes 2752520 | tf_op jit(solution)/shard_map/ppermute | solution.py:1018
  147.7 68.5 %copy-start.27 = (bf16[128,1024]{1,0:T(8,128)(2,1)}, bf16[128,1024]{1,0:T(8,128)(2,1)S(1)}, u32[]{:S(2)}) copy-start(bf16[128,1024]{1,0:T(8,128)(2,1)S(1)} %get-tuple-element.278) | copy-start | bytes 786436
  148.8 24.2 %copy-start.5 = (f32[384,1024]{1,0:T(8,128)}, f32[384,1024]{1,0:T(8,128)S(1)}, u32[]{:S(2)}) copy-start(f32[384,1024]{1,0:T(8,128)S(1)} %get-tuple-element.281) | copy-start | bytes 4718596
  157.7 15.2 %copy-start.87 = (bf16[1024,1024]{1,0:T(8,128)(2,1)S(1)}, bf16[1024,1024]{1,0:T(8,128)(2,1)}, u32[]{:S(2)}) copy-start(bf16[1024,1024]{1,0:T(8,128)(2,1)} %param.42) | copy-start | bytes 6291460
  176.7 20.5 %copy-start.19 = (bf16[384,1024]{1,0:T(8,128)(2,1)}, bf16[384,1024]{1,0:T(8,128)(2,1)S(1)}, u32[]{:S(2)}) copy-start(bf16[384,1024]{1,0:T(8,128)(2,1)S(1)} %add_convert_fusion.12) | copy-start | bytes 2359300
  203.2 12.9 %collective-permute-start.3 = (bf16[2048,1024]{1,0:T(8,128)(2,1)}, bf16[2048,1024]{1,0:T(8,128)(2,1)S(1)}, u32[]{:S(2)}, u32[]{:S(2)}) collective-permute-start(bf16[2048,1024]{1,0:T(8,128)(2,1)} %convolution_convert_fusion.1), channel_id=1, source_target_pairs={{0,1},{1,0},{2,3},{3,2},{4,5},{5,4},{6,7},{7,6},{8,9},{9,8},{10,11... | collective-permute-start | bytes 12582920 | tf_op jit(solution)/shard_map/ppermute | solution.py:1018
  220.6 116.3 %reduce-scatter.6.cloned.1.call-start = ((), (), s32[]{:S(2)}) async-start(), calls=%async_computation.5 | async-start | bytes 5242880 | tf_op jit(solution)/shard_map/reduce_scatter | solution.py:1146
  226.8 11.4 %collective-permute-start.2 = (bf16[512,4096]{1,0:T(8,128)(2,1)S(1)}, bf16[512,4096]{1,0:T(8,128)(2,1)}, u32[]{:S(2)}, u32[]{:S(2)}) collective-permute-start(bf16[512,4096]{1,0:T(8,128)(2,1)S(1)} %convolution_convert_fusion), channel_id=1, source_target_pairs={{0,1},{1,0},{2,3},{3,2},{4,5},{5,4},{6,7},{7,6},{8,9},{9,8},{10,11... | collective-permute-start | bytes 12582920 | tf_op jit(solution)/shard_map/ppermute | solution.py:1018
  243.9 163.5 %reduce-scatter.8.cloned.1.call-start = ((), (), s32[]{:S(2)}) async-start(), calls=%async_computation.6 | async-start | bytes 1638400 | tf_op jit(solution)/shard_map/reduce_scatter | solution.py:1216
  253.1 97.8 %collective-permute-start.6 = (bf16[512,1024]{1,0:T(8,128)(2,1)}, bf16[512,1024]{1,0:T(8,128)(2,1)}, u32[]{:S(2)}, u32[]{:S(2)}) collective-permute-start(bf16[512,1024]{1,0:T(8,128)(2,1)} %convolution_convert_fusion.4), channel_id=1, source_target_pairs={{0,1},{1,0},{2,3},{3,2},{4,5},{5,4},{6,7},{7,6},{8,9},{9,8},{10,11... | collective-permute-start | bytes 3145736 | tf_op jit(solution)/shard_map/ppermute | solution.py:1018
  301.0 32.9 %collective-permute-start.5 = (bf16[640,1024]{1,0:T(8,128)(2,1)}, bf16[640,1024]{1,0:T(8,128)(2,1)}, u32[]{:S(2)}, u32[]{:S(2)}) collective-permute-start(bf16[640,1024]{1,0:T(8,128)(2,1)} %broadcast_select_fusion), channel_id=1, source_target_pairs={{0,1},{1,0},{2,3},{3,2},{4,5},{5,4},{6,7},{7,6},{8,9},{9,8},{10,11... | collective-permute-start | bytes 3932168 | tf_op jit(solution)/shard_map/ppermute | solution.py:1018
  336.9 207.5 %all-reduce.7.cloned.1.call-start = ((), (), s32[]{:S(2)}) async-start(), calls=%async_computation.7 | async-start | bytes 524288 | tf_op jit(solution)/shard_map/psum | solution.py:1221
  345.2 10.6 %copy-start.36 = (bf16[384,1024]{1,0:T(8,128)(2,1)}, bf16[384,1024]{1,0:T(8,128)(2,1)S(1)}, u32[]{:S(2)}) copy-start(bf16[384,1024]{1,0:T(8,128)(2,1)S(1)} %add_convert_fusion.11) | copy-start | bytes 2359300
  349.5 11.1 %collective-permute-start.7 = (bf16[512,1024]{1,0:T(8,128)(2,1)S(1)}, bf16[512,1024]{1,0:T(8,128)(2,1)S(1)}, u32[]{:S(2)}, u32[]{:S(2)}) collective-permute-start(bf16[512,1024]{1,0:T(8,128)(2,1)S(1)} %convolution_convert_fusion.3), channel_id=1, source_target_pairs={{0,1},{1,0},{2,3},{3,2},{4,5},{5,4},{6,7},{7,6},{8,9},{9,8},{10,11... | collective-permute-start | bytes 3145736 | tf_op jit(solution)/shard_map/ppermute | solution.py:1018
  350.8 11.5 %collective-permute-start.8 = (bf16[512,1024]{1,0:T(8,128)(2,1)S(1)}, bf16[512,1024]{1,0:T(8,128)(2,1)S(1)}, u32[]{:S(2)}, u32[]{:S(2)}) collective-permute-start(bf16[512,1024]{1,0:T(8,128)(2,1)S(1)} %convolution_convert_fusion.2), channel_id=1, source_target_pairs={{0,1},{1,0},{2,3},{3,2},{4,5},{5,4},{6,7},{7,6},{8,9},{9,8},{10,11... | collective-permute-start | bytes 3145736 | tf_op jit(solution)/shard_map/ppermute | solution.py:1018
  413.2 15.9 %collective-permute-start.10 = (bf16[512,2048]{1,0:T(8,128)(2,1)}, bf16[512,2048]{1,0:T(8,128)(2,1)}, u32[]{:S(2)}, u32[]{:S(2)}) collective-permute-start(bf16[512,2048]{1,0:T(8,128)(2,1)} %add_convert_fusion.6), channel_id=1, source_target_pairs={{0,1},{1,0},{2,3},{3,2},{4,5},{5,4},{6,7},{7,6},{8,9},{9,8},{10,11... | collective-permute-start | bytes 6291464 | tf_op jit(solution)/shard_map/ppermute | solution.py:1018
  413.4 5.2 collective-permute-start.4
  422.3 6.8 %copy-start.22 = (bf16[160,1024]{1,0:T(8,128)(2,1)S(1)}, bf16[160,1024]{1,0:T(8,128)(2,1)}, u32[]{:S(2)}) copy-start(bf16[160,1024]{1,0:T(8,128)(2,1)} %copy-done.21) | copy-start | bytes 983044
  422.3 6.8 %copy-start.24 = (bf16[160,1024]{1,0:T(8,128)(2,1)S(1)}, bf16[160,1024]{1,0:T(8,128)(2,1)}, u32[]{:S(2)}) copy-start(bf16[160,1024]{1,0:T(8,128)(2,1)} %copy-done.23) | copy-start | bytes 983044
  425.7 1.7 collective-permute-start.9
  544.4 8.6 %collective-permute-start.11 = (bf16[128,1024]{1,0:T(8,128)(2,1)}, bf16[128,1024]{1,0:T(8,128)(2,1)S(1)}, u32[]{:S(2)}, u32[]{:S(2)}) collective-permute-start(bf16[128,1024]{1,0:T(8,128)(2,1)} %all-reduce.7.cloned.1.call-done), channel_id=1, source_target_pairs={{0,1},{1,0},{2,3},{3,2},{4,5},{5,4},{6,7},{7,6},{8,9},{9,8},{10,11... | collective-permute-start | bytes 786440 | tf_op jit(solution)/shard_map/ppermute | solution.py:1018
  546.2 9.6 %collective-permute-start.12 = (bf16[4,80,1024]{2,1,0:T(8,128)(2,1)}, bf16[4,80,1024]{2,1,0:T(8,128)(2,1)S(1)}, u32[]{:S(2)}, u32[]{:S(2)}) collective-permute-start(bf16[4,80,1024]{2,1,0:T(8,128)(2,1)} %get-tuple-element.94), channel_id=1, source_target_pairs={{0,1},{1,0},{2,3},{3,2},{4,5},{5,4},{6,7},{7,6},{8,9},{9,8},{10,11... | collective-permute-start | bytes 1966088 | tf_op jit(solution)/shard_map/ppermute | solution.py:1018
  (79 other events, 269.2 us)
Sparse Core Ops, SparseCore 0:
  74.2 60.9 all-reduce.4
  220.7 53.4 reduce-scatter.3
  277.4 52.6 reduce-scatter.5
  337.0 31.0 reduce-scatter.7
  426.7 38.8 all-reduce.6

commit v5 on v4

--- a/solution.py
+++ b/solution.py
@@ -66,8 +66,32 @@
     return (lax.axis_index("rows"), index)
 
 
-def gather_kernel(count, block_ref, whole_ref, own_sem, send_sem, recv_sem):
-    rows = block_ref.shape[0]
+def gather_kernel(
+    count,
+    lanes_ok,
+    block_ref,
+    gain_ref,
+    shift_ref,
+    weight_in,
+    bias_ref,
+    page_in,
+    kv_in,
+    kv_shift_ref,
+    normed_ref,
+    qkv_ref,
+    ends_ref,
+    kv_ref,
+    whole_ref,
+    weight_ref,
+    page_ref,
+    kv_weight_ref,
+    load_sem,
+    own_sem,
+    send_sem,
+    recv_sem,
+):
+    rows, features = block_ref.shape
+    width = qkv_ref.shape[1] // 3
     me = lax.axis_index("seq")
     chip, core, chips = me // 2, me % 2, count // 2
     other = me + 1 - 2 * core
@@ -86,10 +110,32 @@
     def _():
         pl.semaphore_signal(barrier, inc=1, device_id=place(me + 2), device_id_type=MESH)
 
+    if lanes_ok:
+        loads = [
+            pltpu.make_async_copy(
+                weight_in.at[
+                    :, pl.ds(pl.multiple_of(part * features + me * width, width), width)
+                ],
+                weight_ref.at[:, part * width : (part + 1) * width],
+                load_sem.at[part],
+            )
+            for part in range(3)
+        ]
+        bias_query = bias_ref[:, pl.ds(pl.multiple_of(me * width, width), width)]
+        bias_value = bias_ref[:, pl.ds(pl.multiple_of(features + me * width, width), width)]
+    else:
+        loads = [pltpu.make_async_copy(weight_in, weight_ref, load_sem.at[0])]
+        bias_query = bias_ref[:, 0:width]
+        bias_value = bias_ref[:, width : 2 * width]
+    later_loads = [
+        pltpu.make_async_copy(page_in, page_ref, load_sem.at[3]),
+        pltpu.make_async_copy(kv_in, kv_weight_ref, load_sem.at[4]),
+    ]
+    own = pltpu.make_async_copy(block_ref, block(me), own_sem)
+    for load in [own] + loads + later_loads:
+        load.start()
     peers = 1 + jnp.where(chip > 0, 1, 0) + jnp.where(chip < chips - 1, 1, 0)
     pl.semaphore_wait(barrier, peers)
-    own = pltpu.make_async_copy(block_ref, block(me), own_sem)
-    own.start()
 
     def copy(lane, source, target, from_own=False):
         there = block(2 * source + core)
@@ -111,48 +157,85 @@
     def across(source, from_own=False):
         return copy(2, source, other, from_own)
 
-    @pl.when(chip < chips - 1)
-    def _():
-        right(chip, True).start()
-
-    @pl.when(chip > 0)
-    def _():
-        left(chip, True).start()
-
-    across(chip, True).start()
-    for step in range(1, chips):
-
-        @pl.when(chip - step >= 0)
-        def _():
-            right(chip - step).wait_recv()
-
-            @pl.when(chip < chips - 1)
-            def _():
-                right(chip - step).start()
-
-            across(chip - step).start()
-
-        @pl.when(chip + step < chips)
-        def _():
-            left(chip + step).wait_recv()
-
-            @pl.when(chip > 0)
-            def _():
-                left(chip + step).start()
-
-            across(chip + step).start()
-
-    own.wait()
-    for source in range(chips):
+    def from_across(source):
         there = block(2 * source + 1 - core)
-        pltpu.make_async_remote_copy(
+        return pltpu.make_async_remote_copy(
             src_ref=there,
             dst_ref=there,
             send_sem=send_sem.at[2, source],
             recv_sem=recv_sem.at[2, source],
             device_id=place(other),
             device_id_type=MESH,
-        ).wait_recv()
+        )
+
+    def process(index):
+        piece = rows // 2
+
+        def half(number, carry):
+            here = pl.ds(pl.multiple_of(index * rows + number * piece, piece), piece)
+            normed = low(norm_forward(wide(whole_ref[here, :]), gain_ref[...], shift_ref[...]))
+            normed_ref[here, :] = normed
+            product = dot_plain(normed, weight_ref[...])
+            qkv_ref[here, 0:width] = low(product[:, 0:width] + bias_query)
+            qkv_ref[here, width : 2 * width] = low(product[:, width : 2 * width])
+            qkv_ref[here, 2 * width : 3 * width] = low(product[:, 2 * width :] + bias_value)
+            return carry
+
+        lax.fori_loop(0, 2, half, 0)
+
+    @pl.when(chip < chips - 1)
+    def _():
+        right(chip, True).start()
+
+    @pl.when(chip > 0)
+    def _():
+        left(chip, True).start()
+
+    across(chip, True).start()
+    for load in [own] + loads:
+        load.wait()
+    process(me)
+    from_across(chip).wait_recv()
+    process(other)
+    for load in later_loads:
+        load.wait()
+    pages = page_ref.shape[0]
+    for first in range(0, pages, pages // 5):
+        here = slice(first, first + pages // 5)
+        kv_ref[here, :] = low(dot_plain(page_ref[here, :], kv_weight_ref[...]) + kv_shift_ref[...])
+    for step in range(1, chips):
+
+        @pl.when(chip - step >= 0)
+        def _():
+            right(chip - step).wait_recv()
+
+            @pl.when(chip < chips - 1)
+            def _():
+                right(chip - step).start()
+
+            across(chip - step).start()
+
+        @pl.when(chip + step < chips)
+        def _():
+            left(chip + step).wait_recv()
+
+            @pl.when(chip > 0)
+            def _():
+                left(chip + step).start()
+
+            across(chip + step).start()
+
+        for source, there in ((chip - step, chip - step >= 0), (chip + step, chip + step < chips)):
+
+            @pl.when(there)
+            def _():
+                process(2 * source + core)
+                from_across(source).wait_recv()
+                process(2 * source + 1 - core)
+
+    ends_ref[0:SLOTS, :] = whole_ref[0:SLOTS, :]
+    ends_ref[SLOTS : 2 * SLOTS, :] = whole_ref[count * rows - SLOTS : count * rows, :]
+    for source in range(chips):
         across(source).wait_send()
 
         @pl.when((source <= chip) & (chip < chips - 1))
@@ -164,22 +247,36 @@
             left(source).wait_send()
 
 
-def gather_rows(block_in, count, collective_id):
-    rows, width = block_in.shape
+def gather_rows(block_in, gain, shift, weight, bias, page, kv_weight, kv_shift, count, collective_id):
+    rows, features = block_in.shape
+    width = features // count
+    lanes_ok = width % 128 == 0
+    bf = jnp.bfloat16
+    vmem, anywhere = pl.BlockSpec(memory_space=pltpu.VMEM), pl.BlockSpec(memory_space=pl.ANY)
     return pl.pallas_call(
-        functools.partial(gather_kernel, count),
-        out_shape=jax.ShapeDtypeStruct((count * rows, width), block_in.dtype),
-        in_specs=[pl.BlockSpec(memory_space=pl.ANY)],
-        out_specs=pl.BlockSpec(memory_space=pl.ANY),
+        functools.partial(gather_kernel, count, lanes_ok),
+        out_shape=[
+            jax.ShapeDtypeStruct((count * rows, features), bf),
+            jax.ShapeDtypeStruct((count * rows, 3 * width), bf),
+            jax.ShapeDtypeStruct((2 * SLOTS, features), bf),
+            jax.ShapeDtypeStruct((page.shape[0], kv_weight.shape[1]), bf),
+        ],
+        in_specs=[anywhere, vmem, vmem, anywhere, vmem, anywhere, anywhere, vmem],
+        out_specs=[vmem] * 4,
         scratch_shapes=[
+            pltpu.VMEM((count * rows, features), bf),
+            pltpu.VMEM((features, 3 * width), bf),
+            pltpu.VMEM(page.shape, bf),
+            pltpu.VMEM(kv_weight.shape, bf),
+            pltpu.SemaphoreType.DMA((5,)),
             pltpu.SemaphoreType.DMA,
             pltpu.SemaphoreType.DMA((3, count // 2)),
             pltpu.SemaphoreType.DMA((3, count // 2)),
         ],
         compiler_params=pltpu.CompilerParams(
-            collective_id=collective_id, has_side_effects=True
+            collective_id=collective_id, has_side_effects=True, vmem_limit_bytes=VMEM_LIMIT
         ),
-    )(block_in)
+    )(block_in, gain, shift, weight, bias, page, kv_weight, kv_shift)
 
 
 AXES = {"seq": 1, "chip": 1, "rows": 0}
@@ -1052,7 +1149,6 @@
     gives_big = (own_page == big_page) & (me % sharers == 0)
 
     x_own = inputs[0]
-    x_all = gather_rows(x_own, count, 0)
 
     half = PAGE_PAD // 2
     masked_page = jnp.where(gives_big, mem_page, jnp.zeros_like(mem_page)).reshape(2, half, -1)
@@ -1061,31 +1157,38 @@
     end_grad = jnp.where(core == 0, out_grad[0, :SLOTS], out_grad[0, tokens - SLOTS :])
     sent = jnp.concatenate((pair_page, jnp.where(at_end, end_grad, jnp.zeros_like(end_grad))))
     same_core = [[2 * chip + which for chip in range(count // 2)] for which in range(2)]
-    mine = lax.psum(sent, "seq", axis_index_groups=same_core)
-    theirs = swap(mine)
-    zeroth, first = jnp.where(core == 0, mine, theirs), jnp.where(core == 0, theirs, mine)
-    mem_big = jnp.concatenate((zeroth[:half], first[:half]))
-    front_grad, back_grad = zeroth[half:], first[half:]
-
-    qkv_own_weight = jnp.concatenate(
-        [
-            lax.dynamic_slice_in_dim(qkv_weight, part * features + me * width, width, 1)
-            for part in range(3)
-        ],
-        axis=1,
-    )
-    qkv_own_bias = jnp.concatenate(
-        (
-            lax.dynamic_slice_in_dim(qv_bias, me * width, width, 0),
-            jnp.zeros((width,), jnp.bfloat16),
-            lax.dynamic_slice_in_dim(qv_bias, features + me * width, width, 0),
-        )
-    )
-    normed_all = low(norm_forward(wide(x_all), gain_one, shift_one))
-    qkv = low(dot_plain(normed_all, qkv_own_weight) + wide(qkv_own_bias))
-    mixed, mixed_stats = self_forward(qkv, starts)
     bf = jnp.bfloat16
     lanes_ok = width % 128 == 0
+    own_weight, own_bias = qkv_weight, wide(qv_bias)
+    if not lanes_ok:
+        own_weight = jnp.concatenate(
+            [
+                lax.dynamic_slice_in_dim(qkv_weight, part * features + me * width, width, 1)
+                for part in range(3)
+            ],
+            axis=1,
+        )
+        own_bias = jnp.concatenate(
+            [
+                lax.dynamic_slice_in_dim(own_bias, part * features + me * width, width, 0)
+                for part in range(2)
+            ]
+        )
+    kv_shift = jnp.concatenate((jnp.zeros((features,), jnp.float32), wide(cross_v_bias)))
+    normed_all, qkv, x_ends, kv_own = gather_rows(
+        x_own,
+        gain_one[None, :],
+        shift_one[None, :],
+        own_weight,
+        own_bias[None, :],
+        mem_page,
+        cross_kv_weight,
+        kv_shift[None, :],
+        count,
+        0,
+    )
+    mine = lax.psum(after(sent, x_ends), "seq", axis_index_groups=same_core)
+    mixed, mixed_stats = self_forward(qkv, starts)
     chosen = slots_of(mixed[:SLOTS], mixed[length - SLOTS :])
     if lanes_ok:
         blocks_mixed, slots_mixed = exchange(
@@ -1116,16 +1219,19 @@
             blocks.transpose(1, 0, 2).reshape(blocks.shape[1], -1)
             for blocks in (blocks_mixed, slots_mixed)
         )
+    mine = after(mine, slots_mixed)
+    theirs = swap(mine)
+    zeroth, first = jnp.where(core == 0, mine, theirs), jnp.where(core == 0, theirs, mine)
+    mem_big = jnp.concatenate((zeroth[:half], first[:half]))
+    front_grad, back_grad = zeroth[half:], first[half:]
     attended = jnp.concatenate((blocks_mixed, slots_mixed))
     resid = wide(
-        jnp.concatenate((x_own, slots_of(x_all[:SLOTS], x_all[length - SLOTS :])))
+        jnp.concatenate((x_own, slots_of(x_ends[:SLOTS], x_ends[SLOTS:])))
     )
     resid_one = resid + dot_plain(attended, self_out_weight) + wide(self_out_bias)
     normed_two = low(norm_forward(resid_one, gain_two, shift_two))
     cross_queries = low(dot_plain(normed_two, cross_q_weight) + wide(cross_q_bias))
-    kv_shift = jnp.concatenate((jnp.zeros((features,), jnp.float32), wide(cross_v_bias)))
     kv_big = low(dot_plain(mem_big, cross_kv_weight) + kv_shift)
-    kv_own = low(dot_plain(mem_page, cross_kv_weight) + kv_shift)
     cross_low, cross_stats = cross_forward(cross_queries, kv_big, kv_own)
     resid_two = resid_one + dot_plain(cross_low, cross_out_weight) + wide(cross_out_bias)
     normed_three = low(norm_forward(resid_two, gain_three, shift_three))
@@ -1153,7 +1259,7 @@
     grad_co_w = pair_sum(cross_low, grad_branch_two)
     grad_co_b = jnp.sum(wide(grad_branch_two), axis=0)
     grad_cross_low = low(dot_right(grad_branch_two, cross_out_weight))
-    grad_cross_low = after(grad_cross_low, (grad_fc1_w, grad_fc2_w))
+    grad_cross_low = after(grad_cross_low, (grad_fc1_w, grad_fc2_w, grad_co_w))
     grad_cross_q, big_dk, big_dv, own_dk, own_dv, fc2_stack = cross_backward(
         cross_queries, kv_big, kv_own, cross_low, grad_cross_low, cross_stats, fc2_share, counts, 5
     )

time: 574 us -> 563 us (0.981); the launches traced: 572 us -> 555 us
  other arithmetic: 65.3 us -> 49.8 us
    psum x1, waiting for transfers between devices: 0.02 us -> 14.4 us  [body(): mine = lax.psum(after(sent, x_ends), 'seq', axis_index_groups=same_core)]
    dot_general x8 -> x6, matrix products: 50.8 us -> 39.4 us  [dot_plain(): return jnp.dot(first, second, preferred_element_type=jnp.float32)]
    select_n x2, other arithmetic: 11.9 us -> 1.6 us  [slots_of(): return jnp.where(in_front, front, back)]
    reduce_scatter x1, waiting for transfers between devices: 18.5 us -> 8.84 us  [body(): lax.psum_scatter(grad_fc2_w, 'rows', scatter_dimension=1, tiled=True)]
    dot_general x14, matrix products: 42.4 us -> 48.9 us  [dot_left(): lax.dot_general(first, second, (((0,), (0,)), ((), ())), preferred_elemen...]
    pallas_call x2, Pallas kernels: 53.9 us -> 47.9 us  [exchange(): pl.pallas_call(functools.partial(exchange_kernel, counts, len(arrays), pa...]
    convert_element_type x5 -> x4, other arithmetic: 12.5 us -> 8.09 us  [low(): return values.astype(jnp.bfloat16)]
    unnamed x188 -> x206, local copies, waits for them, and re-layouts: 18.6 us -> 19 us
  transfers between devices with their start and end apart: 18 -> 18, of which waited for: 2 -> 3; matrix products, arithmetic and copies ran while one was open for 26% -> 22% of each run, Pallas kernels for 51% -> 52%
where the time goes in v5:
time: 563 us; the launch traced here: 555 us
  Pallas kernels  306 us (54%)
  matrix products  121 us (21%)
  other arithmetic  49.8 us (9%)
  local copies, waits for them, and re-layouts  33.9 us (6%)
  waiting for transfers between devices  23.6 us (4%)
  between operations  16.7 us (3%)
    pallas_call x1, Pallas kernels, finish(): pl.pallas_call(functools.partial(finish_kernel, counts, (len(over_chips),...  110 us
    dot_general x14, matrix products, dot_left(): lax.dot_general(first, second, (((0,), (0,)), ((), ())), preferred_elemen...  48.9 us
    pallas_call x1, Pallas kernels, gather_rows(): pl.pallas_call(functools.partial(gather_kernel, count, lanes_ok), out_sha...  48.3 us
    pallas_call x2, Pallas kernels, exchange(): pl.pallas_call(functools.partial(exchange_kernel, counts, len(arrays), pa...  47.9 us
    pallas_call x1, Pallas kernels, self_backward(): pl.pallas_call(functools.partial(self_backward_kernel, counts, hosted), o...  43.2 us
    dot_general x6, matrix products, dot_plain(): return jnp.dot(first, second, preferred_element_type=jnp.float32)  39.4 us
    dot_general x7, matrix products, dot_right(): lax.dot_general(first, second, (((1,), (1,)), ((), ())), preferred_elemen...  32.2 us
    pallas_call x1, Pallas kernels, cross_backward(): pl.pallas_call(functools.partial(cross_backward_kernel, counts), grid=(st...  24 us
  transfers between devices with their start and end apart: 18, of which 3 were waited for; matrix products, arithmetic and copies ran while one was open for 22% of the time, Pallas kernels for 52%

profile of v5, /device:TPU:0, one launch (start us, length us, event | category | flops | bytes accessed | tf_op | source)
XLA Modules:
  0.0 555.0 jit_solution(8175319150888792012)
XLA Ops:
  11.2 2.9 broadcast_select_fusion.1
  17.8 48.3 %shard_map.416 = (bf16[2048,1024]{1,0:T(8,128)(2,1)}, bf16[2048,384]{1,0:T(8,128)(2,1)}, bf16[256,1024]{1,0:T(8,128)(2,1)}, bf16[640,2048]{1,0:T(8,128)(2,1)}) custom-call(bf16[256,1024]{1,0:T(8,128)(2,1)} %bitcast.133, f32[1,1024]{1,0:T(1,128)} %bitcast.139, f32[1,1024]{1,0:T(1,128)} %bitcast.148, bf16[1024,3072]{1,0:T(8,128)(2,1)} %refs_4_.1, ...), custom_call_target="tpu_custom_call" | custom-call | tf_op jit(solution)/shard_map/pallas_call | solution.py:256
  69.2 12.0 %shard_map.417 = (bf16[2048,128]{1,0:T(8,128)(2,1)}, f32[2,2048]{1,0:T(2,128)}) custom-call(bf16[2048,384]{1,0:T(8,128)(2,1)} %get-tuple-element.73.qkv_ref.refs_0_, s32[8]{0:T(128)} %convert_reduce_fusion.8.start_ref), custom_call_target="tpu_custom_call" | custom-call | tf_op jit(solution)/shard_map/pallas_call | solution.py:777
  85.2 23.6 %shard_map.418 = (bf16[256,1024]{1,0:T(8,128)(2,1)}, bf16[128,1024]{1,0:T(8,128)(2,1)}) custom-call(bf16[2048,128]{1,0:T(8,128)(2,1)} %get-tuple-element.74.refs_0_.refs_1_, bf16[128,128]{1,0:T(8,128)(2,1)} %slice_select_fusion.5.refs_1_), custom_call_target="tpu_custom_call" | custom-call | tf_op jit(solution)/shard_map/pallas_call | solution.py:409
  108.8 14.4 %all-reduce.5.cloned.1.call-done = bf16[448,1024]{1,0:T(8,128)(2,1)} async-done(((bf16[448,1024]{1,0:T(8,128)(2,1)}), bf16[448,1024]{1,0:T(8,128)(2,1)}) %all-reduce.5.cloned.1.call-update) | async-done | bytes 917520 | tf_op jit(solution)/shard_map/psum | solution.py:1190
  132.2 5.0 add_convert_fusion.3.key_ref.value_ref
  139.4 15.1 %shard_map.419 = (bf16[384,1024]{1,0:T(8,128)(2,1)}, f32[8,2,384]{2,1,0:T(2,128)}) custom-call(bf16[384,1024]{1,0:T(8,128)(2,1)} %add_convert_fusion.11.query_ref, bf16[640,2048]{1,0:T(8,128)(2,1)} %add_convert_fusion.3.key_ref.value_ref, bf16[640,2048]{1,0:T(8,128)(2,1)} %add_convert_fusion.3.key_ref.value_ref, ...), custom_call_target="tpu_custom_call" | custom-call | tf_op jit(solution)/shard_map/pallas_call | solution.py:933
  154.5 2.9 fusion.159
  158.9 20.6 %multiply_convert_fusion = (bf16[384,4096]{1,0:T(8,128)(2,1)S(1)}, f32[384,4096]{1,0:T(8,128)}, f32[384,4096]{1,0:T(8,128)}) fusion(f32[4096]{0:T(1024)S(1)} %convert_element_type.178, bf16[384,1024]{1,0:T(8,128)(2,1)S(1)} %add_convert_fusion.10, bf16[1024,4096]{1,0:T(8,128)(2,1)} %param.46), kind=kOutput, calls=%fused_computation.6 | convolution fusion | flops 3325034496 | bytes 24920064 | tf_op jit(solution)/shard_map/dot_general | solution.py:42
  181.2 4.4 convolution_convert_fusion.1
  186.0 12.5 %convert_reduce_fusion = (f32[4096]{0:T(1024)}, bf16[384,4096]{1,0:T(8,128)(2,1)}) fusion(f32[384,4096]{1,0:T(8,128)} %get-tuple-element.208, f32[384,4096]{1,0:T(8,128)} %get-tuple-element.293, bf16[4096,1024]{1,0:T(8,128)(2,1)S(1)} %bitcast.158, bf16[128,1024]{1,0:T(8,128)(2,1)S(1)} %get-tuple-element.287, bf16[256,1024]{1,0:T(8,128)(2,1)S(1)} %bitcast.127, ...), kind=kOutput, calls=%fused_computation.4 | convolution fusion | flops 3248353280 | bytes 24920448 | tf_op jit(solution)/shard_map/dot_general | solution.py:52
  198.5 6.0 %add_convert_fusion = bf16[2048,1024]{1,0:T(8,128)(2,1)} fusion(bf16[2048,1024]{1,0:T(8,128)(2,1)} %collective-permute-done.3, bf16[384,512]{1,0:T(8,128)(2,1)S(1)} %get-tuple-element.214, bf16[384,512]{1,0:T(8,128)(2,1)S(1)} %get-tuple-element.215, bf16[384,512]{1,0:T(8,128)(2,1)S(1)} %get-tuple-element.216, bf16[384,512]{1,0:T(8,128)(2,1)S(1)} %get-tuple-element.209, ...), kind=kOutput, calls=%fused_computation.1 | convolution fusion | flops 1625161728 | bytes 10748288 | tf_op jit(solution)/shard_map/dot_general | solution.py:46
  206.1 4.4 convolution_convert_fusion
  213.1 8.8 %multiply_reduce_fusion = (f32[1024]{0:T(1024)}, f32[384]{0:T(512)S(1)}, f32[1024]{0:T(1024)}, f32[384,1024]{1,0:T(8,128)}) fusion(f32[384,1024]{1,0:T(8,128)S(1)} %copy-done.2, f32[384]{0:T(512)S(1)} %fusion.134, f32[384]{0:T(512)S(1)} %broadcast_multiply_fusion, f32[1024]{0:T(1024)S(1)} %convert_element_type.175, bf16[384,4096]{1,0:T(8,128)(2,1)S(1)} %copy-done.9, ...), kind=kOutput, calls=%fused_computation.72 | convolution fusion | flops 3224368640 | bytes 14696960 | tf_op jit(solution)/shard_map/dot_general | solution.py:52
  221.9 5.8 %add_convert_fusion.1 = bf16[512,4096]{1,0:T(8,128)(2,1)} fusion(f32[512,4096]{1,0:T(8,128)S(1)} %fusion.43, bf16[512,4096]{1,0:T(8,128)(2,1)} %collective-permute-done.2), kind=kLoop, calls=%fused_computation.2 | loop fusion | flops 6291456 | bytes 16777216 | tf_op jit(solution)/shard_map/convert_element_type | solution.py:58
  244.6 2.9 add_convert_fusion.8.refs_7_
  247.6 8.8 %reduce-scatter.4.cloned.1.call-done.sent_ref = bf16[2048,256]{1,0:T(8,128)(2,1)} async-done(((bf16[2048,1024]{1,0:T(8,128)(2,1)}), bf16[2048,256]{1,0:T(8,128)(2,1)}) %reduce-scatter.4.cloned.1.call-update) | async-done | bytes 1048592 | tf_op jit(solution)/shard_map/reduce_scatter | solution.py:1249
  256.4 24.0 %shard_map.420 = (bf16[384,1024]{1,0:T(8,128)(2,1)}, bf16[640,1024]{1,0:T(8,128)(2,1)}, bf16[640,1024]{1,0:T(8,128)(2,1)}, bf16[640,1024]{1,0:T(8,128)(2,1)}, bf...) custom-call(bf16[384,1024]{1,0:T(8,128)(2,1)} %add_convert_fusion.11.query_ref, ...), custom_call_target="tpu_custom_call" | custom-call | tf_op jit(solution)/shard_map/pallas_call | solution.py:1028
  280.5 3.1 convolution_convert_fusion.3
  294.3 24.3 %shard_map.421 = (bf16[2048,128]{1,0:T(8,128)(2,1)}, bf16[8,128,128]{2,1,0:T(8,128)(2,1)}) custom-call(bf16[384,1024]{1,0:T(8,128)(2,1)} %convolution_convert_fusion.5.refs_0_), custom_call_target="tpu_custom_call" | custom-call | tf_op jit(solution)/shard_map/pallas_call | solution.py:409
  318.6 3.0 select_add_fusion
  324.8 8.0 %add_convert_fusion.9 = bf16[384,1024]{1,0:T(8,128)(2,1)S(1)} fusion(f32[384,1024]{1,0:T(8,128)S(1)} %copy-done.4, bf16[384,4096]{1,0:T(8,128)(2,1)} %copy-done.25, bf16[4096,1024]{1,0:T(8,128)(2,1)} %param.48, f32[1024]{0:T(1024)S(1)} %convert_element_type.180), kind=kOutput, calls=%fused_computation.80 | convolution fusion | flops 3222405120 | bytes 13897728 | tf_op jit(solution)/shard_map/dot_general | solution.py:42
  338.3 3.8 fusion.27
  342.3 3.0 add_convert_fusion.7.refs_8_
  347.0 43.2 %shard_map.422 = (bf16[2048,384]{1,0:T(8,128)(2,1)}, bf16[4,128,1024]{2,1,0:T(8,128)(2,1)}, bf16[4,512,256]{2,1,0:T(8,128)(2,1)}, bf16[4,512,256]{2,1,0:T(8,128)(2,1)}, bf16[4,512,256]{2,1,0:T(8,128)(2,1)}) custom-call(bf16[2048,384]{1,0:T(8,128)(2,1)} %get-tuple-element.73.qkv_ref.refs_0_, bf16[2048,128]{1,0:T(8,128)(2,1)} %get-tuple-element.74.refs_0_.refs_1_, ...), custom_call_target="tpu_custom_call" | custom-call | tf_op jit(solution)/shard_map/pallas_call | solution.py:881
  391.4 4.5 add_convert_fusion.5
  397.5 3.8 fusion.28
  411.8 5.0 add_convert_fusion.4.refs_22_
  416.8 109.5 %shard_map.423 = (f32[256,1024]{1,0:T(8,128)}, f32[4,8,512]{2,1,0:T(8,128)}, bf16[4,80,1024]{2,1,0:T(8,128)(2,1)}, bf16[128,3072]{1,0:T(8,128)(2,1)}, bf16[512,1...) custom-call(bf16[2048,384]{1,0:T(8,128)(2,1)} %get-tuple-element.93., ...), custom_call_target="tpu_custom_call" | custom-call | tf_op jit(solution)/shard_map/pallas_call | solution.py:649
  529.6 5.7 %shard_map.424 = (f32[128,3072]{1,0:T(8,128)}, f32[128,4096]{1,0:T(8,128)}, f32[512,1024]{1,0:T(8,128)}, f32[128,1024]{1,0:T(8,128)}, f32[128,1024]{1,0:T(8,128)...) custom-call(bf16[128,3072]{1,0:T(8,128)(2,1)} %get-tuple-element.107.refs_0_, bf16[128,4096]{1,0:T(8,128)(2,1)} %get-tuple-element.108.refs_1_, ...), custom_call_target="tpu_custom_call" | custom-call | tf_op jit(solution)/shard_map/pallas_call | solution.py:697
  541.6 2.7 fusion.6
  544.3 3.9 copy.52
  (340 shorter events, 92.5 us)
Async XLA Ops:
  7.2 130.3 %copy-start = (bf16[1024,1024]{1,0:T(8,128)(2,1)S(1)}, bf16[1024,1024]{1,0:T(8,128)(2,1)}, u32[]{:S(2)}) copy-start(bf16[1024,1024]{1,0:T(8,128)(2,1)} %param.38) | copy-start | bytes 6291460
  7.2 116.0 %all-reduce.5.cloned.1.call-start = ((), (), s32[]{:S(2)}) async-start(), calls=%async_computation.3 | async-start | bytes 1835008 | tf_op jit(solution)/shard_map/psum | solution.py:1190
  14.9 51.2 %collective-permute-start = (bf16[320,1024]{1,0:T(8,128)(2,1)}, bf16[320,1024]{1,0:T(8,128)(2,1)}, u32[]{:S(2)}, u32[]{:S(2)}) collective-permute-start(bf16[320,1024]{1,0:T(8,128)(2,1)} %dynamic-slice_bitcast_fusion), channel_id=1, source_target_pairs={{0,1},{1,0},{2,3},{3,2},{4,5},{5,4},{6,7},{7,6},{8,9},{9,8},{10,11... | collective-permute-start | bytes 1966088 | tf_op jit(solution)/shard_map/ppermute | solution.py:1115
  17.8 48.3 %copy-start.15 = (bf16[1,256,1024]{2,1,0:T(8,128)(2,1)S(1)}, bf16[1,256,1024]{2,1,0:T(8,128)(2,1)}, u32[]{:S(2)}) copy-start(bf16[1,256,1024]{2,1,0:T(8,128)(2,1)} %param.27) | copy-start | bytes 1572868
  67.3 56.0 %copy-start.89 = (bf16[1024]{0:T(1024)(128)(2,1)S(1)}, bf16[1024]{0:T(1024)(128)(2,1)}, u32[]{:S(2)}) copy-start(bf16[1024]{0:T(1024)(128)(2,1)} %param.36) | copy-start | bytes 6148
  67.3 56.0 %copy-start.90 = (bf16[1024]{0:T(1024)(128)(2,1)S(1)}, bf16[1024]{0:T(1024)(128)(2,1)}, u32[]{:S(2)}) copy-start(bf16[1024]{0:T(1024)(128)(2,1)} %param.44) | copy-start | bytes 6148
  67.3 56.0 %copy-start.91 = (bf16[1024]{0:T(1024)(128)(2,1)S(1)}, bf16[1024]{0:T(1024)(128)(2,1)}, u32[]{:S(2)}) copy-start(bf16[1024]{0:T(1024)(128)(2,1)} %param.35) | copy-start | bytes 6148
  67.3 56.0 %copy-start.92 = (bf16[1024]{0:T(1024)(128)(2,1)S(1)}, bf16[1024]{0:T(1024)(128)(2,1)}, u32[]{:S(2)}) copy-start(bf16[1024]{0:T(1024)(128)(2,1)} %param.37) | copy-start | bytes 6148
  67.3 56.0 %copy-start.93 = (bf16[1024]{0:T(1024)(128)(2,1)S(1)}, bf16[1024]{0:T(1024)(128)(2,1)}, u32[]{:S(2)}) copy-start(bf16[1024]{0:T(1024)(128)(2,1)} %param.39) | copy-start | bytes 6148
  67.3 56.0 %copy-start.94 = (bf16[1024]{0:T(1024)(128)(2,1)S(1)}, bf16[1024]{0:T(1024)(128)(2,1)}, u32[]{:S(2)}) copy-start(bf16[1024]{0:T(1024)(128)(2,1)} %param.43) | copy-start | bytes 6148
  68.3 55.0 %copy-start.95 = (bf16[1024]{0:T(1024)(128)(2,1)S(1)}, bf16[1024]{0:T(1024)(128)(2,1)}, u32[]{:S(2)}) copy-start(bf16[1024]{0:T(1024)(128)(2,1)} %param.45) | copy-start | bytes 6148
  68.3 55.0 %copy-start.83 = (bf16[4096]{0:T(1024)(128)(2,1)S(1)}, bf16[4096]{0:T(1024)(128)(2,1)}, u32[]{:S(2)}) copy-start(bf16[4096]{0:T(1024)(128)(2,1)} %param.47) | copy-start | bytes 24580
  68.3 188.1 %reduce-scatter.4.cloned.1.call-start = ((), (), s32[]{:S(2)}) async-start(), calls=%async_computation.4 | async-start | bytes 5242880 | tf_op jit(solution)/shard_map/reduce_scatter | solution.py:1249
  123.2 3.0 collective-permute-start.1
  128.1 70.5 %copy-start.28 = (bf16[128,1024]{1,0:T(8,128)(2,1)}, bf16[128,1024]{1,0:T(8,128)(2,1)S(1)}, u32[]{:S(2)}) copy-start(bf16[128,1024]{1,0:T(8,128)(2,1)S(1)} %get-tuple-element.287) | copy-start | bytes 786436
  185.6 12.9 %collective-permute-start.3 = (bf16[2048,1024]{1,0:T(8,128)(2,1)}, bf16[2048,1024]{1,0:T(8,128)(2,1)}, u32[]{:S(2)}, u32[]{:S(2)}) collective-permute-start(bf16[2048,1024]{1,0:T(8,128)(2,1)} %convolution_convert_fusion.1), channel_id=1, source_target_pairs={{0,1},{1,0},{2,3},{3,2},{4,5},{5,4},{6,7},{7,6},{8,9},{9,8},{10,11... | collective-permute-start | bytes 12582920 | tf_op jit(solution)/shard_map/ppermute | solution.py:1115
  204.5 117.1 %reduce-scatter.6.cloned.1.call-start = ((), (), s32[]{:S(2)}) async-start(), calls=%async_computation.5 | async-start | bytes 5242880 | tf_op jit(solution)/shard_map/reduce_scatter | solution.py:1252
  210.5 11.4 %collective-permute-start.2 = (bf16[512,4096]{1,0:T(8,128)(2,1)S(1)}, bf16[512,4096]{1,0:T(8,128)(2,1)}, u32[]{:S(2)}, u32[]{:S(2)}) collective-permute-start(bf16[512,4096]{1,0:T(8,128)(2,1)S(1)} %convolution_convert_fusion), channel_id=1, source_target_pairs={{0,1},{1,0},{2,3},{3,2},{4,5},{5,4},{6,7},{7,6},{8,9},{9,8},{10,11... | collective-permute-start | bytes 12582920 | tf_op jit(solution)/shard_map/ppermute | solution.py:1115
  227.7 162.5 %reduce-scatter.8.cloned.1.call-start = ((), (), s32[]{:S(2)}) async-start(), calls=%async_computation.6 | async-start | bytes 1638400 | tf_op jit(solution)/shard_map/reduce_scatter | solution.py:1322
  236.0 8.6 %collective-permute-start.4 = (bf16[512,1024]{1,0:T(8,128)(2,1)}, bf16[512,1024]{1,0:T(8,128)(2,1)}, u32[]{:S(2)}, u32[]{:S(2)}) collective-permute-start(bf16[512,1024]{1,0:T(8,128)(2,1)} %convolution_convert_fusion.4), channel_id=1, source_target_pairs={{0,1},{1,0},{2,3},{3,2},{4,5},{5,4},{6,7},{7,6},{8,9},{9,8},{10,11... | collective-permute-start | bytes 3145736 | tf_op jit(solution)/shard_map/ppermute | solution.py:1115
  256.4 24.1 %copy-start.78 = (bf16[384,128]{1,0:T(8,128)(2,1)S(1)}, bf16[384,128]{1,0:T(8,128)(2,1)}, u32[]{:S(2)}) copy-start(bf16[384,128]{1,0:T(8,128)(2,1)} %get-tuple-element.254) | copy-start | bytes 294916
  256.4 24.1 %copy-start.79 = (bf16[384,128]{1,0:T(8,128)(2,1)S(1)}, bf16[384,128]{1,0:T(8,128)(2,1)}, u32[]{:S(2)}) copy-start(bf16[384,128]{1,0:T(8,128)(2,1)} %get-tuple-element.255) | copy-start | bytes 294916
  256.4 24.1 %copy-start.80 = (bf16[384,128]{1,0:T(8,128)(2,1)S(1)}, bf16[384,128]{1,0:T(8,128)(2,1)}, u32[]{:S(2)}) copy-start(bf16[384,128]{1,0:T(8,128)(2,1)} %get-tuple-element.256) | copy-start | bytes 294916
  283.6 58.5 %collective-permute-start.7 = (bf16[512,1024]{1,0:T(8,128)(2,1)}, bf16[512,1024]{1,0:T(8,128)(2,1)}, u32[]{:S(2)}, u32[]{:S(2)}) collective-permute-start(bf16[512,1024]{1,0:T(8,128)(2,1)} %convolution_convert_fusion.3), channel_id=1, source_target_pairs={{0,1},{1,0},{2,3},{3,2},{4,5},{5,4},{6,7},{7,6},{8,9},{9,8},{10,11... | collective-permute-start | bytes 3145736 | tf_op jit(solution)/shard_map/ppermute | solution.py:1115
  284.8 33.8 %collective-permute-start.6 = (bf16[640,1024]{1,0:T(8,128)(2,1)}, bf16[640,1024]{1,0:T(8,128)(2,1)}, u32[]{:S(2)}, u32[]{:S(2)}) collective-permute-start(bf16[640,1024]{1,0:T(8,128)(2,1)} %broadcast_select_fusion), channel_id=1, source_target_pairs={{0,1},{1,0},{2,3},{3,2},{4,5},{5,4},{6,7},{7,6},{8,9},{9,8},{10,11... | collective-permute-start | bytes 3932168 | tf_op jit(solution)/shard_map/ppermute | solution.py:1115
  321.6 205.6 %all-reduce.7.cloned.1.call-start = ((), (), s32[]{:S(2)}) async-start(), calls=%async_computation.7 | async-start | bytes 524288 | tf_op jit(solution)/shard_map/psum | solution.py:1327
  324.2 21.1 %collective-permute-start.8 = (bf16[512,1024]{1,0:T(8,128)(2,1)S(1)}, bf16[512,1024]{1,0:T(8,128)(2,1)S(1)}, u32[]{:S(2)}, u32[]{:S(2)}) collective-permute-start(bf16[512,1024]{1,0:T(8,128)(2,1)S(1)} %convolution_convert_fusion.2), channel_id=1, source_target_pairs={{0,1},{1,0},{2,3},{3,2},{4,5},{5,4},{6,7},{7,6},{8,9},{9,8},{10,11... | collective-permute-start | bytes 3145736 | tf_op jit(solution)/shard_map/ppermute | solution.py:1115
  395.9 15.9 %collective-permute-start.10 = (bf16[512,2048]{1,0:T(8,128)(2,1)}, bf16[512,2048]{1,0:T(8,128)(2,1)}, u32[]{:S(2)}, u32[]{:S(2)}) collective-permute-start(bf16[512,2048]{1,0:T(8,128)(2,1)} %add_convert_fusion.5), channel_id=1, source_target_pairs={{0,1},{1,0},{2,3},{3,2},{4,5},{5,4},{6,7},{7,6},{8,9},{9,8},{10,11... | collective-permute-start | bytes 6291464 | tf_op jit(solution)/shard_map/ppermute | solution.py:1115
  396.2 5.2 collective-permute-start.5
  408.4 1.7 collective-permute-start.9
  527.2 8.6 %collective-permute-start.11 = (bf16[128,1024]{1,0:T(8,128)(2,1)}, bf16[128,1024]{1,0:T(8,128)(2,1)S(1)}, u32[]{:S(2)}, u32[]{:S(2)}) collective-permute-start(bf16[128,1024]{1,0:T(8,128)(2,1)} %all-reduce.7.cloned.1.call-done), channel_id=1, source_target_pairs={{0,1},{1,0},{2,3},{3,2},{4,5},{5,4},{6,7},{7,6},{8,9},{9,8},{10,11... | collective-permute-start | bytes 786440 | tf_op jit(solution)/shard_map/ppermute | solution.py:1115
  529.1 9.6 %collective-permute-start.12 = (bf16[4,80,1024]{2,1,0:T(8,128)(2,1)}, bf16[4,80,1024]{2,1,0:T(8,128)(2,1)S(1)}, u32[]{:S(2)}, u32[]{:S(2)}) collective-permute-start(bf16[4,80,1024]{2,1,0:T(8,128)(2,1)} %get-tuple-element.106), channel_id=1, source_target_pairs={{0,1},{1,0},{2,3},{3,2},{4,5},{5,4},{6,7},{7,6},{8,9},{9,8},{10,11... | collective-permute-start | bytes 1966088 | tf_op jit(solution)/shard_map/ppermute | solution.py:1115
  (88 other events, 345.4 us)
Sparse Core Ops, SparseCore 0:
  68.5 54.6 all-reduce.4
  204.6 51.7 reduce-scatter.3
  259.7 52.6 reduce-scatter.5
  321.7 31.0 reduce-scatter.7
  409.4 38.7 all-reduce.6
